TPU v7x, 32 devices: a whole 2x2x4 slice. The times are simulated.
32 devices in a mesh: fsdp: 4 (over z), ctx: 4 (over x, core), tp: 2 (over y).
Axes of the slice: x: 2, y: 2, z: 4, core: 2. Of those that a mesh axis runs over, the one named last changes fastest.
Arguments:
- tokens: bfloat16 [8192, 1024], P(('fsdp', 'ctx'), 'tp'), may hold values from -6 to 6
- cotangent: bfloat16 [8192, 1024], P(('fsdp', 'ctx'), 'tp'), may hold values from -6 to 6
- slot_of: int32 [8192], replicated, may hold values from 0 to 8191, as said below
- lengths: int32 [4, 3], P('fsdp'), may hold values from 0 to 2048, as said below
- w_query: bfloat16 [1024, 1024], P(('fsdp', 'ctx'), 'tp'), may hold values from -0.1875 to 0.1875
- key_weight: bfloat16 [1024, 512], P(('fsdp', 'ctx'), 'tp'), may hold values from -0.1875 to 0.1875
- value_weight: bfloat16 [1024, 512], P(('fsdp', 'ctx'), 'tp'), may hold values from -0.1875 to 0.1875
- w_out: bfloat16 [1024, 1024], P('tp', ('fsdp', 'ctx')), may hold values from -3 to 3
- w_gate: bfloat16 [1024, 4608], P(('fsdp', 'ctx'), 'tp'), may hold values from -0.1875 to 0.1875
- w_up: bfloat16 [1024, 4608], P(('fsdp', 'ctx'), 'tp'), may hold values from -0.1875 to 0.1875
- w_down: bfloat16 [4608, 1024], P('tp', ('fsdp', 'ctx')), may hold values from -0.09375 to 0.09375
- gain_attn: float32 [1024], replicated, may hold values from 0.25 to 1.75
- gain_ffn: float32 [1024], replicated, may hold values from 0.25 to 1.75
- gain_query: float32 [64], replicated, may hold values from 0.25 to 1.75
- gain_key: float32 [64], replicated, may hold values from 0.25 to 1.75
Outputs:
- output: bfloat16 [8192, 1024], P(('fsdp', 'ctx'), 'tp')
- grad_tokens: bfloat16 [8192, 1024], P(('fsdp', 'ctx'), 'tp')
- grad_w_query: float32 [1024, 1024], P(('fsdp', 'ctx'), 'tp')
- grad_w_key: float32 [1024, 512], P(('fsdp', 'ctx'), 'tp')
- grad_w_value: float32 [1024, 512], P(('fsdp', 'ctx'), 'tp')
- grad_w_out: float32 [1024, 1024], P('tp', ('fsdp', 'ctx'))
- grad_w_gate: float32 [1024, 4608], P(('fsdp', 'ctx'), 'tp')
- grad_w_up: float32 [1024, 4608], P(('fsdp', 'ctx'), 'tp')
- grad_w_down: float32 [4608, 1024], P('tp', ('fsdp', 'ctx'))
- grad_gain_attn: float32 [1024], replicated
- grad_gain_ffn: float32 [1024], replicated
- grad_gain_query: float32 [64], replicated
- grad_gain_key: float32 [64], replicated
- rms_stats: float32 [3], replicated
Inputs may be any that keep to these rules, and one draw needn't show every extreme that they name: slot_of is a permutation of the 8192 slots; the tokens of each index of fsdp+ctx go in equal shares to the slots held by every index of fsdp+ctx (each index holds one piece of 2048 / 4 slots of its row). Each row's lengths sum to 2048; its nonzero lengths come first and are at least 512; a row holds one to three sequences, and the first row holds one.
All inputs are finite; a program needn't handle non-finite values.
Results may differ from a plain program's by a relative error of at most 0.024.
Values may be sent and summed in bfloat16 or wider, within the bound.
A program may use at most 256 MiB of HBM per device.

v0:
```python
import jax
import jax.numpy as jnp
from jax import lax
from jax.sharding import PartitionSpec as P

MODEL_WIDTH = 1024
QUERY_HEADS = 16
KEY_VALUE_HEADS = 8
HEAD_SIZE = 64
PACKED_ROW_SLOTS = 2048
QUERY_BLOCK_ROWS = 512


EPSILON = 1e-05
ROPE_THETA = 1000000.0
NEG_FILL = -1e30


def rms_scale(values, gain):
    return values * lax.rsqrt(jnp.mean(values * values, axis=-1, keepdims=True) + EPSILON) * gain


def rotate(values, cosines, sines):
    middle = values.shape[-1] // 2
    first_half = values[..., :middle]
    second_half = values[..., middle:]
    return jnp.concatenate(
        [first_half * cosines - second_half * sines, second_half * cosines + first_half * sines],
        axis=-1,
    )


def slot_tables(lengths, slot_ids):
    seg_ends = jnp.cumsum(lengths, dtype=jnp.int32)
    passed = (slot_ids[:, None] >= seg_ends[None, :]).astype(jnp.int32)
    segment = jnp.sum(passed, axis=1, dtype=jnp.int32)
    position = slot_ids - jnp.sum(passed * lengths[None, :], axis=1, dtype=jnp.int32)
    return (segment, position)


def angle_tables(position):
    frequency = ROPE_THETA ** (-jnp.arange(0, HEAD_SIZE, 2).astype(jnp.float32) / HEAD_SIZE)
    angles = position.astype(jnp.float32)[:, None] * frequency[None, :]
    return (jnp.cos(angles)[:, None, :], jnp.sin(angles)[:, None, :])


def product(left_arr, right_arr, pattern):
    return jnp.einsum(pattern, left_arr, right_arr, preferred_element_type=jnp.float32)


def swish_product(gate_act, up_proj):
    return jax.nn.silu(gate_act) * up_proj


def score_probs(q_block, key_rows, q_seg, q_slot, k_seg, k_slot, lse_block):
    raw_scores = product(q_block, key_rows, "qhgd,khd->hgqk") * 0.125
    allowed = (q_seg[:, None] == k_seg[None, :]) & (k_slot[None, :] <= q_slot[:, None])
    shifted = raw_scores - jnp.transpose(lse_block, (1, 2, 0))[..., None]
    return jnp.exp(jnp.where(allowed, shifted, NEG_FILL))


def attend_row(query_row, key_rows, value_rows, q_segment, q_slot, k_segment, k_slot):
    block_list = query_row.shape[0] // QUERY_BLOCK_ROWS

    def attend_one_block(packed):
        q_block, seg_block, slot_block = packed
        raw_scores = product(q_block, key_rows, "qhgd,khd->hgqk") * 0.125
        allowed = (seg_block[:, None] == k_segment[None, :]) & (
            k_slot[None, :] <= slot_block[:, None]
        )
        masked = jnp.where(allowed, raw_scores, NEG_FILL)
        row_peak = jnp.max(masked, axis=-1, keepdims=True)
        weights = jnp.exp(masked - row_peak)
        row_total = jnp.sum(weights, axis=-1, keepdims=True)
        probabilities = weights / row_total
        head_out = product(probabilities.astype(jnp.bfloat16), value_rows, "hgqk,khd->qhgd")
        log_total = jnp.transpose((row_peak + jnp.log(row_total))[..., 0], (2, 0, 1))
        return (head_out, log_total)

    shaped = query_row.reshape((block_list, QUERY_BLOCK_ROWS) + query_row.shape[1:])
    return lax.map(
        attend_one_block,
        (
            shaped,
            q_segment.reshape(block_list, QUERY_BLOCK_ROWS),
            q_slot.reshape(block_list, QUERY_BLOCK_ROWS),
        ),
    )


def query_back(
    query_row, key_rows, value_rows, q_segment, q_slot, k_segment, k_slot, log_total, grad_heads
):
    block_list = query_row.shape[0] // QUERY_BLOCK_ROWS

    def query_one_block(carried, packed):
        q_block, seg_block, slot_block, lse_block, grad_block = packed
        probabilities = score_probs(
            q_block, key_rows, seg_block, slot_block, k_segment, k_slot, lse_block
        )
        d_prob = product(grad_block, value_rows, "qhgd,khd->hgqk")
        delta = jnp.sum(probabilities * d_prob, axis=-1, keepdims=True)
        d_score = (probabilities * (d_prob - delta)).astype(jnp.bfloat16)
        q_grad = product(d_score, key_rows, "hgqk,khd->qhgd") * 0.125
        key_grad = carried[0] + product(d_score, q_block, "hgqk,qhgd->khd") * 0.125
        value_grad = carried[1] + product(
            probabilities.astype(jnp.bfloat16), grad_block, "hgqk,qhgd->khd"
        )
        carried = (key_grad, value_grad)
        return (carried, (q_grad, jnp.transpose(delta[..., 0], (2, 0, 1))))

    block_shape = (block_list, QUERY_BLOCK_ROWS) + query_row.shape[1:]
    initial = (jnp.zeros(key_rows.shape, jnp.float32), jnp.zeros(key_rows.shape, jnp.float32))
    packed = (
        query_row.reshape(block_shape),
        q_segment.reshape(block_list, QUERY_BLOCK_ROWS),
        q_slot.reshape(block_list, QUERY_BLOCK_ROWS),
        log_total,
        grad_heads.reshape(block_shape),
    )
    return lax.scan(query_one_block, initial, packed)


def ffn_pass(mid_rows, dy_rows, gate_w, up_w, down_w, gain_ffn):
    mid_float = mid_rows.astype(jnp.float32)
    normed_two, norm_pull = jax.vjp(rms_scale, mid_float, gain_ffn)
    normed_b = normed_two.astype(jnp.bfloat16)
    gate_act = product(normed_b, gate_w, "nd,df->nf")
    up_proj = product(normed_b, up_w, "nd,df->nf")
    hidden_f, swish_pull = jax.vjp(swish_product, gate_act, up_proj)
    hidden = hidden_f.astype(jnp.bfloat16)
    ffn_out = product(hidden, down_w, "nf,fd->nd")
    d_hidden = product(dy_rows, down_w, "nd,fd->nf")
    g_down = product(hidden, dy_rows, "nf,nd->fd")
    d_gate, d_up = swish_pull(d_hidden)
    d_gate = d_gate.astype(jnp.bfloat16)
    d_up = d_up.astype(jnp.bfloat16)
    g_gate = product(normed_b, d_gate, "nd,nf->df")
    g_up = product(normed_b, d_up, "nd,nf->df")
    d_normed = product(d_gate, gate_w, "nf,df->nd") + product(d_up, up_w, "nf,df->nd")
    d_mid, d_gain = norm_pull(d_normed)
    return (ffn_out, d_mid, g_gate, g_up, g_down, d_gain)


def local(
    tokens,
    cotangent,
    slot_of,
    lengths,
    w_query,
    key_weight,
    value_weight,
    w_out,
    w_gate,
    w_up,
    w_down,
    gain_attn,
    gain_ffn,
    gain_query,
    gain_key,
):
    stream_len = tokens.shape[0]
    feat_len = tokens.shape[1]
    tensor_split_count = lax.axis_size("tp")
    ctx_size = lax.axis_size("ctx")
    local_len = PACKED_ROW_SLOTS // ctx_size
    row_count = stream_len // local_len
    q_heads = QUERY_HEADS // tensor_split_count
    key_value_heads = KEY_VALUE_HEADS // tensor_split_count
    query_group_width = QUERY_HEADS // KEY_VALUE_HEADS
    kv_width = key_value_heads * HEAD_SIZE
    flat_len = row_count * local_len
    row_len = PACKED_ROW_SLOTS
    gathered = (
        lax.all_gather(w_query, ("fsdp", "ctx"), axis=0, tiled=True),
        lax.all_gather(key_weight, ("fsdp", "ctx"), axis=0, tiled=True),
        lax.all_gather(value_weight, ("fsdp", "ctx"), axis=0, tiled=True),
        lax.all_gather(w_out, ("fsdp", "ctx"), axis=1, tiled=True),
        lax.all_gather(w_gate, ("fsdp", "ctx"), axis=0, tiled=True),
        lax.all_gather(w_up, ("fsdp", "ctx"), axis=0, tiled=True),
        lax.all_gather(w_down, ("fsdp", "ctx"), axis=1, tiled=True),
    )
    query_w, key_w, value_w, out_w, gate_w, up_w, down_w = gathered
    fsdp_index = lax.axis_index("fsdp")
    ctx_index = lax.axis_index("ctx")
    stream_index = fsdp_index * ctx_size + ctx_index
    target = lax.dynamic_slice_in_dim(slot_of, stream_index * stream_len, stream_len, 0)
    target_dev = (
        target // PACKED_ROW_SLOTS // row_count * ctx_size + target % PACKED_ROW_SLOTS // local_len
    )
    send_order = jnp.argsort(target_dev, stable=True)
    arrived_tok, arrived_cot = (
        lax.all_to_all(
            tokens[send_order], ("fsdp", "ctx"), split_axis=0, concat_axis=0, tiled=True
        ),
        lax.all_to_all(
            cotangent[send_order], ("fsdp", "ctx"), split_axis=0, concat_axis=0, tiled=True
        ),
    )
    my_rows = fsdp_index * row_count + jnp.arange(row_count, dtype=jnp.int32)
    my_slot = (
        my_rows[:, None] * PACKED_ROW_SLOTS
        + ctx_index * local_len
        + jnp.arange(local_len, dtype=jnp.int32)[None, :]
    ).reshape(flat_len)
    source = jnp.argsort(slot_of)[my_slot]
    source_order = jnp.argsort(source)
    arrival_rank = jnp.argsort(source_order)
    packed_tok = arrived_tok[arrival_rank].reshape(row_count, local_len, feat_len)
    packed_cot = arrived_cot[arrival_rank].reshape(row_count, local_len, feat_len)
    own_slots = ctx_index * local_len + jnp.arange(local_len, dtype=jnp.int32)
    row_slots = jnp.arange(row_len, dtype=jnp.int32)

    def tables(row_lengths):
        q_segment, q_position = slot_tables(row_lengths, own_slots)
        k_segment = slot_tables(row_lengths, row_slots)[0]
        return (q_segment, q_position, k_segment)

    q_segment, q_position, k_segment = jax.vmap(tables)(lengths)
    cosines, sines = angle_tables(q_position.reshape(flat_len))
    x_full, dy_full = (
        lax.all_gather(packed_tok, "tp", axis=2, tiled=True),
        lax.all_gather(packed_cot, "tp", axis=2, tiled=True),
    )
    x_float = x_full.reshape(flat_len, MODEL_WIDTH).astype(jnp.float32)
    dy_full = dy_full.reshape(flat_len, MODEL_WIDTH)
    normed_f, attn_norm_pull = jax.vjp(rms_scale, x_float, gain_attn)
    first_normed = normed_f.astype(jnp.bfloat16)
    query_raw = product(first_normed, query_w, "nd,de->ne")
    key_raw = product(first_normed, key_w, "nd,de->ne")
    value_b = product(first_normed, value_w, "nd,de->ne").astype(jnp.bfloat16)

    def head_prep(query_in, key_in, gain_q, gain_k):
        query_out = rotate(
            rms_scale(query_in.reshape(flat_len, q_heads, HEAD_SIZE), gain_q), cosines, sines
        )
        key_out = rotate(
            rms_scale(key_in.reshape(flat_len, key_value_heads, HEAD_SIZE), gain_k), cosines, sines
        )
        return (query_out, key_out)

    (query_rot, key_rot), prep_pull = jax.vjp(head_prep, query_raw, key_raw, gain_query, gain_key)
    query_b = query_rot.astype(jnp.bfloat16)
    key_b = key_rot.astype(jnp.bfloat16).reshape(flat_len, kv_width)
    local_kv = jnp.concatenate([key_b, value_b], axis=1).reshape(row_count, local_len, 2 * kv_width)
    row_kv = lax.all_gather(local_kv, "ctx", axis=1, tiled=True)
    key_rows = row_kv[..., :kv_width].reshape(row_count, row_len, key_value_heads, HEAD_SIZE)
    value_rows = row_kv[..., kv_width:].reshape(row_count, row_len, key_value_heads, HEAD_SIZE)
    query_rows = query_b.reshape(
        row_count, local_len, key_value_heads, query_group_width, HEAD_SIZE
    )

    def row_forward(packed):
        q_row, k_row, v_row, qs_row, ks_row = packed
        return attend_row(q_row, k_row, v_row, qs_row, own_slots, ks_row, row_slots)

    head_out, log_total = lax.map(
        row_forward, (query_rows, key_rows, value_rows, q_segment, k_segment)
    )
    heads_b = head_out.reshape(flat_len, q_heads * HEAD_SIZE).astype(jnp.bfloat16)
    attn_part = product(heads_b, out_w, "nq,qd->nd")
    attn_full = lax.psum(attn_part.astype(jnp.bfloat16), "tp").astype(jnp.float32)
    middle_full = x_float + attn_full
    middle_b = middle_full.astype(jnp.bfloat16)
    tp_index = lax.axis_index("tp")
    attn_own = lax.dynamic_slice_in_dim(
        attn_full.reshape(row_count, local_len, MODEL_WIDTH), tp_index * feat_len, feat_len, 2
    )
    token_f = packed_tok.astype(jnp.float32)
    middle_own = token_f + attn_own
    ffn_part, d_mid_part, g_gate, g_up, g_down, d_gain_ffn = ffn_pass(
        middle_b, dy_full, gate_w, up_w, down_w, gain_ffn
    )
    ffn_out, d_back = (
        lax.psum_scatter(
            ffn_part.reshape(row_count, local_len, MODEL_WIDTH).astype(jnp.bfloat16),
            "tp",
            scatter_dimension=2,
            tiled=True,
        ).astype(jnp.float32),
        lax.psum_scatter(
            d_mid_part.reshape(row_count, local_len, MODEL_WIDTH).astype(jnp.bfloat16),
            "tp",
            scatter_dimension=2,
            tiled=True,
        ).astype(jnp.float32),
    )
    d_middle = packed_cot.astype(jnp.float32) + d_back
    d_attn = lax.all_gather(d_middle.astype(jnp.bfloat16), "tp", axis=2, tiled=True).reshape(
        flat_len, MODEL_WIDTH
    )
    g_out = product(heads_b, d_attn, "nq,nd->qd")
    d_heads = product(d_attn, out_w, "nd,qd->nq").astype(jnp.bfloat16)
    grad_rows = d_heads.reshape(row_count, local_len, key_value_heads, query_group_width, HEAD_SIZE)

    def row_query_keys(packed):
        q_row, k_row, v_row, qs_row, ks_row, lse_row, g_row = packed
        return query_back(q_row, k_row, v_row, qs_row, own_slots, ks_row, row_slots, lse_row, g_row)

    (key_grads, value_grads), (q_grads, unused) = lax.map(
        row_query_keys,
        (query_rows, key_rows, value_rows, q_segment, k_segment, log_total, grad_rows),
    )
    kv_grads = jnp.concatenate(
        [
            key_grads.reshape(row_count, row_len, kv_width),
            value_grads.reshape(row_count, row_len, kv_width),
        ],
        axis=2,
    )
    own_kv = lax.psum_scatter(
        kv_grads.astype(jnp.bfloat16), "ctx", scatter_dimension=1, tiled=True
    ).astype(jnp.float32)
    d_key_rot = own_kv[..., :kv_width].reshape(flat_len, key_value_heads, HEAD_SIZE)
    d_value = own_kv[..., kv_width:].reshape(flat_len, kv_width).astype(jnp.bfloat16)
    d_query_raw, d_key_raw, d_gain_q, d_gain_k = prep_pull(
        (q_grads.reshape(flat_len, q_heads, HEAD_SIZE), d_key_rot)
    )
    d_query = d_query_raw.astype(jnp.bfloat16)
    d_key = d_key_raw.astype(jnp.bfloat16)
    g_query = product(first_normed, d_query, "nd,ne->de")
    g_key = product(first_normed, d_key, "nd,ne->de")
    g_value = product(first_normed, d_value, "nd,ne->de")
    d_normed_one = (
        product(d_query, query_w, "ne,de->nd")
        + product(d_key, key_w, "ne,de->nd")
        + product(d_value, value_w, "ne,de->nd")
    )
    d_x_part, d_gain_attn = attn_norm_pull(d_normed_one)
    d_x = lax.psum_scatter(
        d_x_part.reshape(row_count, local_len, MODEL_WIDTH).astype(jnp.bfloat16),
        "tp",
        scatter_dimension=2,
        tiled=True,
    ).astype(jnp.float32)
    grad_packed = (d_middle + d_x).astype(jnp.bfloat16)
    output_packed = (middle_own + ffn_out).astype(jnp.bfloat16)
    weight_sums = (
        lax.psum_scatter(
            g_query.astype(jnp.bfloat16), ("fsdp", "ctx"), scatter_dimension=0, tiled=True
        ).astype(jnp.float32),
        lax.psum_scatter(
            g_key.astype(jnp.bfloat16), ("fsdp", "ctx"), scatter_dimension=0, tiled=True
        ).astype(jnp.float32),
        lax.psum_scatter(
            g_value.astype(jnp.bfloat16), ("fsdp", "ctx"), scatter_dimension=0, tiled=True
        ).astype(jnp.float32),
        lax.psum_scatter(
            g_out.astype(jnp.bfloat16), ("fsdp", "ctx"), scatter_dimension=1, tiled=True
        ).astype(jnp.float32),
        lax.psum_scatter(
            g_gate.astype(jnp.bfloat16), ("fsdp", "ctx"), scatter_dimension=0, tiled=True
        ).astype(jnp.float32),
        lax.psum_scatter(
            g_up.astype(jnp.bfloat16), ("fsdp", "ctx"), scatter_dimension=0, tiled=True
        ).astype(jnp.float32),
        lax.psum_scatter(
            g_down.astype(jnp.bfloat16), ("fsdp", "ctx"), scatter_dimension=1, tiled=True
        ).astype(jnp.float32),
    )
    squares = jnp.stack(
        [jnp.sum(token_f * token_f), jnp.sum(attn_own * attn_own), jnp.sum(ffn_out * ffn_out)]
    )
    gain_a, gain_f, gain_qs, gain_ks, square_sums = lax.psum(
        (d_gain_attn, d_gain_ffn, d_gain_q, d_gain_k, squares), ("fsdp", "ctx", "tp")
    )
    entry_count = flat_len * ctx_size * lax.axis_size("fsdp") * MODEL_WIDTH
    rms_stats = jnp.sqrt(square_sums / entry_count)
    out_send = output_packed.reshape(flat_len, feat_len)[source_order]
    grad_send = grad_packed.reshape(flat_len, feat_len)[source_order]
    out_back, grad_back = (
        lax.all_to_all(out_send, ("fsdp", "ctx"), split_axis=0, concat_axis=0, tiled=True),
        lax.all_to_all(grad_send, ("fsdp", "ctx"), split_axis=0, concat_axis=0, tiled=True),
    )
    stream_rank = jnp.argsort(send_order)
    output = out_back[stream_rank]
    grad_tokens = grad_back[stream_rank]
    return (
        output,
        grad_tokens,
        weight_sums[0],
        weight_sums[1],
        weight_sums[2],
        weight_sums[3],
        weight_sums[4],
        weight_sums[5],
        weight_sums[6],
        gain_a,
        gain_f,
        gain_qs,
        gain_ks,
        rms_stats,
    )


def solution(mesh):
    in_specs = (
        P(("fsdp", "ctx"), "tp"),
        P(("fsdp", "ctx"), "tp"),
        P(),
        P("fsdp", None),
        P(("fsdp", "ctx"), "tp"),
        P(("fsdp", "ctx"), "tp"),
        P(("fsdp", "ctx"), "tp"),
        P("tp", ("fsdp", "ctx")),
        P(("fsdp", "ctx"), "tp"),
        P(("fsdp", "ctx"), "tp"),
        P("tp", ("fsdp", "ctx")),
        P(),
        P(),
        P(),
        P(),
    )
    out_specs = (
        P(("fsdp", "ctx"), "tp"),
        P(("fsdp", "ctx"), "tp"),
        P(("fsdp", "ctx"), "tp"),
        P(("fsdp", "ctx"), "tp"),
        P(("fsdp", "ctx"), "tp"),
        P("tp", ("fsdp", "ctx")),
        P(("fsdp", "ctx"), "tp"),
        P(("fsdp", "ctx"), "tp"),
        P("tp", ("fsdp", "ctx")),
        P(),
        P(),
        P(),
        P(),
        P(),
    )
    return jax.shard_map(local, mesh=mesh, in_specs=in_specs, out_specs=out_specs, check_vma=False)
```

profile of v0, /device:TPU:0, one launch (start us, length us, event | category | flops | bytes accessed | tf_op | source)
XLA Modules:
  0.0 1114.3 jit_solution(14384650494723473514)
XLA Ops:
  43.3 23.3 %all_gather.34 = bf16[1024,256]{1,0:T(8,128)(2,1)S(1)} all-gather(bf16[64,256]{1,0:T(8,128)(2,1)S(1)} %copy-done.40), channel_id=1, replica_groups=mesh['fsdp'=4,'ctx'=4,'tp'=2] {'fsdp','ctx'}, dimensions={0}, use_global_device_ids=true | all-gather | bytes 557056 | tf_op jit(solution)/shard_map/all_gather | solution.py:176
  66.5 18.9 %all_gather.35 = bf16[1024,256]{1,0:T(8,128)(2,1)S(1)} all-gather(bf16[64,256]{1,0:T(8,128)(2,1)S(1)} %copy-done.41), channel_id=1, replica_groups=mesh['fsdp'=4,'ctx'=4,'tp'=2] {'fsdp','ctx'}, dimensions={0}, use_global_device_ids=true | all-gather | bytes 557056 | tf_op jit(solution)/shard_map/all_gather | solution.py:177
  111.0 17.8 %all-gather.27.cloned.1.call-done = bf16[2048,512]{0,1:T(8,128)(2,1)} async-done(((bf16[512,512]{0,1:T(8,128)(2,1)}), bf16[2048,512]{0,1:T(8,128)(2,1)}) %all-gather.27.cloned.1.call-update) | async-done | bytes 2097168 | tf_op jit(solution)/shard_map/all_gather | solution.py:246
  144.2 14.4 %fusion.6 = f32[4,2,512]{2,1,0:T(2,128)S(1)} fusion(f32[4,2048,512,2]{2,1,3,0:T(8,128)} %get-tuple-element.224, f32[4,2,512]{2,1,0:T(2,128)S(1)} %get-tuple-element.223, pred[512,2048]{0,1:T(8,128)(4,1)S(1)} %fusion.16), kind=kLoop, calls=%fused_computation.21 | loop fusion | flops 33550336 | bytes 34635776 | tf_op jit(solution)/shard_map/while/body/eval_jaxpr/while/body/eval_jaxpr/reduce_sum | solution.py:74
  158.6 14.4 %fusion.44 = bf16[4,64,2,512]{3,1,2,0:T(8,128)(2,1)S(1)} fusion(bf16[2048,4,64,1]{0,2,3,1:T(8,128)(2,1)S(1)} %bitcast.219, f32[4,2048,512,2]{2,1,3,0:T(8,128)} %get-tuple-element.224, f32[4,2,512]{2,1,0:T(2,128)S(1)} %fusion.6, f32[4,2,512]{2,1,0:T(2,128)S(1)} %get-tuple-element.223, pred[512,2048]{0,1:T(8,128)(4,1)S(1)} %fusion.16), kind=kOutput, calls=%fused_computation.91 | convolution fusion | flops 1115947008 | bytes 36208640 | tf_op jit(solution)/shard_map/while/body/eval_jaxpr/while/body/eval_jaxpr/hgqk,khd->qhgd/dot_general | solution.py:48
  179.7 19.1 %all_to_all.48 = bf16[16,32,512]{2,1,0:T(8,128)(2,1)S(1)} all-to-all(bf16[16,32,512]{2,1,0:T(8,128)(2,1)S(1)} %bitcast.226), channel_id=1, replica_groups=mesh['fsdp'=4,'ctx'=4,'tp'=2] {'fsdp','ctx'}, dimensions={0} | all-to-all | bytes 1048576 | tf_op jit(solution)/shard_map/all_to_all | solution.py:196
  202.5 14.0 %all-reduce.7.cloned.1.call-done = bf16[512,1024]{1,0:T(8,128)(2,1)} async-done(((bf16[512,1024]{1,0:T(8,128)(2,1)}), bf16[512,1024]{1,0:T(8,128)(2,1)}) %all-reduce.7.cloned.1.call-update) | async-done | bytes 1048592 | tf_op jit(solution)/shard_map/psum | solution.py:262
  219.1 53.1 %all-gather.19.cloned.1.call-done = bf16[1024,2304]{1,0:T(8,128)(2,1)} async-done(((bf16[64,2304]{1,0:T(8,128)(2,1)}), bf16[1024,2304]{1,0:T(8,128)(2,1)}) %all-gather.19.cloned.1.call-update) | async-done | bytes 4718608 | tf_op jit(solution)/shard_map/all_gather | solution.py:180
  279.7 46.9 %all-gather.17.cloned.1.call-done = bf16[1024,2304]{1,0:T(8,128)(2,1)} async-done(((bf16[64,2304]{1,0:T(8,128)(2,1)}), bf16[1024,2304]{1,0:T(8,128)(2,1)}) %all-gather.17.cloned.1.call-update) | async-done | bytes 4718608 | tf_op jit(solution)/shard_map/all_gather | solution.py:179
  334.1 14.5 %all-gather.29.cloned.1.call-done = bf16[512,1024]{1,0:T(8,128)(2,1)} async-done(((bf16[512,512]{1,0:T(8,128)(2,1)}), bf16[512,1024]{1,0:T(8,128)(2,1)}) %all-gather.29.cloned.1.call-update) | async-done | bytes 1048592 | tf_op jit(solution)/shard_map/all_gather | solution.py:223
  348.7 55.8 %all-gather.21.cloned.1.call-done = bf16[2304,1024]{0,1:T(8,128)(2,1)} async-done(((bf16[2304,64]{0,1:T(8,128)(2,1)}), bf16[2304,1024]{0,1:T(8,128)(2,1)}) %all-gather.21.cloned.1.call-update) | async-done | bytes 4718608 | tf_op jit(solution)/shard_map/all_gather | solution.py:181
  424.8 19.0 %reduce-scatter.14.cloned.1.call-done = bf16[1,512,512]{2,1,0:T(8,128)(2,1)} async-done(((bf16[1,512,1024]{2,1,0:T(8,128)(2,1)}), bf16[1,512,512]{2,1,0:T(8,128)(2,1)}) %reduce-scatter.14.cloned.1.call-update) | async-done | bytes 524304 | tf_op jit(solution)/shard_map/reduce_scatter | solution.py:281
  446.0 21.3 %all-gather.23.cloned.1.call-done = bf16[1,512,1024]{2,1,0:T(8,128)(2,1)} async-done(((bf16[1,512,512]{2,1,0:T(8,128)(2,1)}), bf16[1,512,1024]{2,1,0:T(8,128)(2,1)}) %all-gather.23.cloned.1.call-update) | async-done | bytes 1048592 | tf_op jit(solution)/shard_map/all_gather | solution.py:289
  469.6 15.9 %fusion.22 = bf16[4,64,2048]{2,1,0:T(8,128)(2,1)} fusion(bf16[512,4,2,64]{0,3,2,1:T(8,128)(2,1)S(1)} %bitcast.240, f32[4,2048,512,2]{2,1,3,0:T(8,128)} %get-tuple-element.224, f32[4,2,512]{2,1,0:T(2,128)S(1)} %bitcast.243, pred[512,2048]{0,1:T(8,128)(4,1)S(1)} %fusion.16), kind=kOutput, calls=%fused_computation.55 | convolution fusion | flops 1107820544 | bytes 36192256 | tf_op jit(solution)/shard_map/while/body/eval_jaxpr/while/body/eval_jaxpr/hgqk,qhgd->khd/dot_general | solution.py:48
  485.5 23.6 %fusion = (f32[4,2,512]{2,1,0:T(2,128)S(1)}, f32[4,2048,512,2]{2,1,3,0:T(8,128)}) fusion(f32[4,2048,512,2]{2,1,3,0:T(8,128)} %get-tuple-element.224, f32[4,2,512]{2,1,0:T(2,128)S(1)} %bitcast.244, pred[512,2048]{0,1:T(8,128)(4,1)S(1)} %fusion.16, bf16[2048,4,64,1]{0,2,3,1:T(8,128)(2,1)} %bitcast.220, bf16[512,4,2,64]{0,3,2,1:T(8,128)(2,1)S(1)} %bitcast.241), kind=kOutput, calls=%fused_computation.11 | convolution fusion | flops 1115680768 | bytes 69763072 | tf_op jit(solution)/shard_map/while/body/eval_jaxpr/while/body/eval_jaxpr/qhgd,khd->hgqk/dot_general | solution.py:48
  509.1 28.5 %fusion.2 = bf16[4,2,512,2048]{2,3,1,0:T(8,128)(2,1)} fusion(f32[4,2048,512,2]{2,1,3,0:T(8,128)} %get-tuple-element.227, f32[4,2048,512,2]{2,1,3,0:T(8,128)} %get-tuple-element.224, f32[4,2,512]{2,1,0:T(2,128)S(1)} %get-tuple-element.226, f32[4,2,512]{2,1,0:T(2,128)S(1)} %bitcast.245, pred[512,2048]{0,1:T(8,128)(4,1)S(1)} %fusion.16), kind=kLoop, calls=%fused_computation.13 | loop fusion | flops 50331648 | bytes 84967424 | tf_op jit(solution)/shard_map/while/body/eval_jaxpr/while/body/eval_jaxpr/convert_element_type | solution.py:103
  654.5 34.8 %reduce-scatter.26.cloned.1.call-done = bf16[512,64]{0,1:T(8,128)(2,1)} async-done(((bf16[512,1024]{0,1:T(8,128)(2,1)}), bf16[512,64]{0,1:T(8,128)(2,1)}) %reduce-scatter.26.cloned.1.call-update) | async-done | bytes 65552 | tf_op jit(solution)/shard_map/reduce_scatter | solution.py:348
  690.8 58.4 %reduce-scatter.20.cloned.1.call-done = bf16[64,512]{1,0:T(8,128)(2,1)} async-done(((bf16[1024,512]{1,0:T(8,128)(2,1)}), bf16[64,512]{1,0:T(8,128)(2,1)}) %reduce-scatter.20.cloned.1.call-update) | async-done | bytes 65552 | tf_op jit(solution)/shard_map/reduce_scatter | solution.py:339
  750.7 77.4 %reduce-scatter.30.cloned.1.call-done = bf16[64,2304]{1,0:T(8,128)(2,1)} async-done(((bf16[1024,2304]{1,0:T(8,128)(2,1)}), bf16[64,2304]{1,0:T(8,128)(2,1)}) %reduce-scatter.30.cloned.1.call-update) | async-done | bytes 294928 | tf_op jit(solution)/shard_map/reduce_scatter | solution.py:354
  829.8 76.5 %reduce-scatter.28.cloned.1.call-done = bf16[64,2304]{1,0:T(8,128)(2,1)} async-done(((bf16[1024,2304]{1,0:T(8,128)(2,1)}), bf16[64,2304]{1,0:T(8,128)(2,1)}) %reduce-scatter.28.cloned.1.call-update) | async-done | bytes 294928 | tf_op jit(solution)/shard_map/reduce_scatter | solution.py:351
  908.2 77.2 %reduce-scatter.32.cloned.1.call-done = bf16[2304,64]{0,1:T(8,128)(2,1)} async-done(((bf16[2304,1024]{0,1:T(8,128)(2,1)}), bf16[2304,64]{0,1:T(8,128)(2,1)}) %reduce-scatter.32.cloned.1.call-update) | async-done | bytes 294928 | tf_op jit(solution)/shard_map/reduce_scatter | solution.py:357
  987.2 39.6 %all-reduce.4 = (f32[1024]{0:T(1024)}, f32[1024]{0:T(1024)}, f32[64]{0:T(128)}, f32[64]{0:T(128)}, f32[3]{0:T(128)S(1)}) all-reduce(f32[1024]{0:T(1024)S(1)} %get-tuple-element.187, f32[1024]{0:T(1024)S(1)} %get-tuple-element.185, f32[64]{0:T(128)S(1)} %get-tuple-element.189, ...), channel_id=1, replica_groups=mesh['fsdp'=4,'ctx'=4,'tp'=2] {'fsdp','ctx','tp'}, use_global_device_ids=true, to_apply=%region_33.34 | all-reduce | flops 2179 | bytes 17432 | tf_op jit(solution)/shard_map/psum | solution.py:364
  1027.4 16.2 %reduce-scatter.24.cloned.1.call-done = bf16[64,256]{1,0:T(8,128)(2,1)} async-done(((bf16[1024,256]{1,0:T(8,128)(2,1)}), bf16[64,256]{1,0:T(8,128)(2,1)}) %reduce-scatter.24.cloned.1.call-update) | async-done | bytes 32784 | tf_op jit(solution)/shard_map/reduce_scatter | solution.py:345
  1045.0 58.0 %reduce-scatter.22.cloned.1.call-done = bf16[64,256]{1,0:T(8,128)(2,1)} async-done(((bf16[1024,256]{1,0:T(8,128)(2,1)}), bf16[64,256]{1,0:T(8,128)(2,1)}) %reduce-scatter.22.cloned.1.call-update) | async-done | bytes 32784 | tf_op jit(solution)/shard_map/reduce_scatter | solution.py:342
  (293 shorter events, 260.0 us)
Async XLA Ops:
  14.5 24.9 %all-to-all-start = ((bf16[16,32,512]{2,1,0:T(8,128)(2,1)}), bf16[16,32,512]{2,1,0:T(8,128)(2,1)S(1)}, u32[]{:S(2)}, u32[]{:S(2)}) async-start(bf16[16,32,512]{2,1,0:T(8,128)(2,1)} %bitcast), calls=%async_computation | async-start | bytes 1048576 | tf_op jit(solution)/shard_map/all_to_all | solution.py:193
  21.8 64.2 %all-gather.25.cloned.1.call-start = ((), (), s32[]{:S(2)}) async-start(), calls=%async_computation.33 | async-start | bytes 1572864 | tf_op jit(solution)/shard_map/all_gather | solution.py:222
  42.1 63.0 %all-gather.13.cloned.1.call-start = ((), (), s32[]{:S(2)}) async-start(), calls=%async_computation.15 | async-start | bytes 1114112 | tf_op jit(solution)/shard_map/all_gather | solution.py:175
  42.9 85.9 %all-gather.27.cloned.1.call-start = ((), (), s32[]{:S(2)}) async-start(), calls=%async_computation.34 | async-start | bytes 2621440 | tf_op jit(solution)/shard_map/all_gather | solution.py:246
  92.4 80.7 %all-gather.15.cloned.1.call-start = ((), (), s32[]{:S(2)}) async-start(), calls=%async_computation.16 | async-start | bytes 1114112 | tf_op jit(solution)/shard_map/all_gather | solution.py:178
  93.0 123.6 %all-reduce.7.cloned.1.call-start = ((), (), s32[]{:S(2)}) async-start(), calls=%async_computation.17 | async-start | bytes 2097152 | tf_op jit(solution)/shard_map/psum | solution.py:262
  176.3 95.9 %all-gather.19.cloned.1.call-start = ((), (), s32[]{:S(2)}) async-start(), calls=%async_computation.19 | async-start | bytes 5013504 | tf_op jit(solution)/shard_map/all_gather | solution.py:180
  176.9 149.7 %all-gather.17.cloned.1.call-start = ((), (), s32[]{:S(2)}) async-start(), calls=%async_computation.18 | async-start | bytes 5013504 | tf_op jit(solution)/shard_map/all_gather | solution.py:179
  177.6 171.0 %all-gather.29.cloned.1.call-start = ((), (), s32[]{:S(2)}) async-start(), calls=%async_computation.35 | async-start | bytes 1572864 | tf_op jit(solution)/shard_map/all_gather | solution.py:223
  201.3 203.1 %all-gather.21.cloned.1.call-start = ((), (), s32[]{:S(2)}) async-start(), calls=%async_computation.20 | async-start | bytes 5013504 | tf_op jit(solution)/shard_map/all_gather | solution.py:181
  202.1 241.7 %reduce-scatter.14.cloned.1.call-start = ((), (), s32[]{:S(2)}) async-start(), calls=%async_computation.22 | async-start | bytes 1572864 | tf_op jit(solution)/shard_map/reduce_scatter | solution.py:281
  424.8 42.5 %all-gather.23.cloned.1.call-start = ((), (), s32[]{:S(2)}) async-start(), calls=%async_computation.23 | async-start | bytes 1572864 | tf_op jit(solution)/shard_map/all_gather | solution.py:289
  445.8 137.0 %reduce-scatter.16.cloned.1.call-start = ((), (), s32[]{:S(2)}) async-start(), calls=%async_computation.24 | async-start | bytes 2621440 | tf_op jit(solution)/shard_map/reduce_scatter | solution.py:311
  551.2 65.5 %reduce-scatter.12.cloned.1.call-start = ((), (), s32[]{:S(2)}) async-start(), calls=%async_computation.21 | async-start | bytes 1572864 | tf_op jit(solution)/shard_map/reduce_scatter | solution.py:275
  558.3 73.8 %reduce-scatter.18.cloned.1.call-start = ((), (), s32[]{:S(2)}) async-start(), calls=%async_computation.25 | async-start | bytes 1572864 | tf_op jit(solution)/shard_map/reduce_scatter | solution.py:330
  588.6 100.7 %reduce-scatter.26.cloned.1.call-start = ((), (), s32[]{:S(2)}) async-start(), calls=%async_computation.29 | async-start | bytes 1114112 | tf_op jit(solution)/shard_map/reduce_scatter | solution.py:348
  591.5 157.6 %reduce-scatter.20.cloned.1.call-start = ((), (), s32[]{:S(2)}) async-start(), calls=%async_computation.26 | async-start | bytes 1114112 | tf_op jit(solution)/shard_map/reduce_scatter | solution.py:339
  593.5 234.5 %reduce-scatter.30.cloned.1.call-start = ((), (), s32[]{:S(2)}) async-start(), calls=%async_computation.31 | async-start | bytes 5013504 | tf_op jit(solution)/shard_map/reduce_scatter | solution.py:354
  599.7 306.6 %reduce-scatter.28.cloned.1.call-start = ((), (), s32[]{:S(2)}) async-start(), calls=%async_computation.30 | async-start | bytes 5013504 | tf_op jit(solution)/shard_map/reduce_scatter | solution.py:351
  606.0 379.4 %reduce-scatter.32.cloned.1.call-start = ((), (), s32[]{:S(2)}) async-start(), calls=%async_computation.32 | async-start | bytes 5013504 | tf_op jit(solution)/shard_map/reduce_scatter | solution.py:357
  621.6 19.6 %all-to-all-start.1 = ((bf16[16,32,512]{2,1,0:T(8,128)(2,1)}), bf16[16,32,512]{2,1,0:T(8,128)(2,1)S(1)}, u32[]{:S(2)}, u32[]{:S(2)}) async-start(bf16[16,32,512]{2,1,0:T(8,128)(2,1)} %bitcast.29), calls=%async_computation.2 | async-start | bytes 1048576 | tf_op jit(solution)/shard_map/all_to_all | solution.py:372
  626.8 416.9 %reduce-scatter.24.cloned.1.call-start = ((), (), s32[]{:S(2)}) async-start(), calls=%async_computation.28 | async-start | bytes 557056 | tf_op jit(solution)/shard_map/reduce_scatter | solution.py:345
  641.2 463.2 %all-to-all-start.3 = ((bf16[16,32,512]{2,1,0:T(8,128)(2,1)}), bf16[16,32,512]{2,1,0:T(8,128)(2,1)S(1)}, u32[]{:S(2)}, u32[]{:S(2)}) async-start(bf16[16,32,512]{2,1,0:T(8,128)(2,1)} %bitcast.59), calls=%async_computation.7 | async-start | bytes 1048576 | tf_op jit(solution)/shard_map/all_to_all | solution.py:373
  645.3 457.7 %reduce-scatter.22.cloned.1.call-start = ((), (), s32[]{:S(2)}) async-start(), calls=%async_computation.27 | async-start | bytes 557056 | tf_op jit(solution)/shard_map/reduce_scatter | solution.py:342
  (66 other events, 651.2 us)
Sparse Core Ops, SparseCore 0:
  42.3 22.6 all-gather.24
  67.1 37.9 all-gather.12
  107.3 21.4 all-gather.26
  130.8 37.9 all-gather.14
  176.4 40.1 all-reduce.6
  218.9 53.2 all-gather.18
  274.8 51.7 all-gather.16
  328.8 19.8 all-gather.28
  351.2 53.2 all-gather.20
  424.9 18.8 reduce-scatter.13
  445.9 21.3 all-gather.22
  551.4 31.4 reduce-scatter.15
  585.1 20.3 reduce-scatter.11
  607.6 20.3 reduce-scatter.17
  631.9 57.3 reduce-scatter.25
  692.7 56.3 reduce-scatter.19
  753.4 74.6 reduce-scatter.29
  831.7 74.5 reduce-scatter.27
  910.7 74.6 reduce-scatter.31
  988.8 54.7 reduce-scatter.23
  1048.2 54.7 reduce-scatter.21
where the time goes:
time: 1120 us; the launch traced here: 1110 us
  waiting for transfers between devices  670 us (60%)
  matrix products  168 us (15%)
  other arithmetic  105 us (9%)
  blocking collectives  101 us (9%)
  local copies, waits for them, and re-layouts  35.7 us (3%)
  starting transfers between devices  18.7 us (2%)
  between operations  15.8 us (1%)
    dot_general x27, matrix products, product(): jnp.einsum(pattern, left_arr, right_arr, preferred_element_type=jnp.float32)  168 us
    reduce_scatter x1, waiting for transfers between devices, local(): lax.psum_scatter(g_up.astype(jnp.bfloat16), ('fsdp', 'ctx'), scatter_dime...  77.4 us
    reduce_scatter x1, waiting for transfers between devices, local(): lax.psum_scatter(g_down.astype(jnp.bfloat16), ('fsdp', 'ctx'), scatter_di...  77.2 us
    reduce_scatter x1, waiting for transfers between devices, local(): lax.psum_scatter(g_gate.astype(jnp.bfloat16), ('fsdp', 'ctx'), scatter_di...  76.5 us
    reduce_scatter x1, waiting for transfers between devices, local(): lax.psum_scatter(g_query.astype(jnp.bfloat16), ('fsdp', 'ctx'), scatter_d...  58.4 us
    reduce_scatter x1, waiting for transfers between devices, local(): lax.psum_scatter(g_key.astype(jnp.bfloat16), ('fsdp', 'ctx'), scatter_dim...  58 us
    all_gather x1, waiting for transfers between devices, local(): lax.all_gather(w_down, ('fsdp', 'ctx'), axis=1, tiled=True)  55.8 us
    all_gather x1, waiting for transfers between devices, local(): lax.all_gather(w_up, ('fsdp', 'ctx'), axis=0, tiled=True)  53.1 us
  transfers between devices with their start and end apart: 24, of which 18 were waited for; matrix products, arithmetic and copies ran while one was open for 16% of the time, Pallas kernels for 0%

commit v1 on v0

v1 whole, which is shorter than its diff:
```python
import functools

import jax
import jax.numpy as jnp
from jax import lax
from jax.experimental import pallas as pl
from jax.experimental.pallas import tpu as pltpu
from jax.sharding import PartitionSpec as P

MODEL_WIDTH = 1024
QUERY_HEADS = 16
KEY_VALUE_HEADS = 8
HEAD_SIZE = 64
PACKED_ROW_SLOTS = 2048
QUERY_BLOCK_ROWS = 512

EPSILON = 1e-05
ROPE_THETA = 1000000.0
NEG_FILL = -1e30
BF = jnp.bfloat16
F32 = jnp.float32


def rms_scale(values, gain):
    return values * lax.rsqrt(jnp.mean(values * values, axis=-1, keepdims=True) + EPSILON) * gain


def rotate(values, cosines, sines):
    middle = values.shape[-1] // 2
    first_half = values[..., :middle]
    second_half = values[..., middle:]
    return jnp.concatenate(
        [first_half * cosines - second_half * sines, second_half * cosines + first_half * sines],
        axis=-1,
    )


def segment_ends(lengths):
    total, ends = lengths[0], []
    for i in range(lengths.shape[0]):
        ends.append(total)
        if i + 1 < lengths.shape[0]:
            total = total + lengths[i + 1]
    return ends


def slot_tables(lengths, slot_ids):
    segment = jnp.zeros_like(slot_ids)
    start = jnp.zeros_like(slot_ids)
    for i, end in enumerate(segment_ends(lengths)):
        passed = (slot_ids >= end).astype(jnp.int32)
        segment = segment + passed
        start = start + passed * lengths[i]
    return (segment, slot_ids - start)


def angle_tables(position):
    frequency = ROPE_THETA ** (-jnp.arange(0, HEAD_SIZE, 2).astype(F32) / HEAD_SIZE)
    angles = position.astype(F32)[:, None] * frequency[None, :]
    return (jnp.cos(angles)[:, None, :], jnp.sin(angles)[:, None, :])


def product(left_arr, right_arr, pattern):
    return jnp.einsum(pattern, left_arr, right_arr, preferred_element_type=F32)


def score_probs(q_block, key_rows, q_seg, q_slot, k_seg, k_slot, lse_block):
    raw_scores = product(q_block, key_rows, "qhgd,khd->hgqk") * 0.125
    allowed = (q_seg[:, None] == k_seg[None, :]) & (k_slot[None, :] <= q_slot[:, None])
    shifted = raw_scores - jnp.transpose(lse_block, (1, 2, 0))[..., None]
    return jnp.exp(jnp.where(allowed, shifted, NEG_FILL))


def attend_row(query_row, key_rows, value_rows, q_segment, q_slot, k_segment, k_slot):
    block_list = query_row.shape[0] // QUERY_BLOCK_ROWS

    def attend_one_block(packed):
        q_block, seg_block, slot_block = packed
        raw_scores = product(q_block, key_rows, "qhgd,khd->hgqk") * 0.125
        allowed = (seg_block[:, None] == k_segment[None, :]) & (
            k_slot[None, :] <= slot_block[:, None]
        )
        masked = jnp.where(allowed, raw_scores, NEG_FILL)
        row_peak = jnp.max(masked, axis=-1, keepdims=True)
        weights = jnp.exp(masked - row_peak)
        row_total = jnp.sum(weights, axis=-1, keepdims=True)
        probabilities = weights / row_total
        head_out = product(probabilities.astype(BF), value_rows, "hgqk,khd->qhgd")
        log_total = jnp.transpose((row_peak + jnp.log(row_total))[..., 0], (2, 0, 1))
        return (head_out, log_total)

    shaped = query_row.reshape((block_list, QUERY_BLOCK_ROWS) + query_row.shape[1:])
    return lax.map(
        attend_one_block,
        (
            shaped,
            q_segment.reshape(block_list, QUERY_BLOCK_ROWS),
            q_slot.reshape(block_list, QUERY_BLOCK_ROWS),
        ),
    )


def query_back(
    query_row, key_rows, value_rows, q_segment, q_slot, k_segment, k_slot, log_total, grad_heads
):
    block_list = query_row.shape[0] // QUERY_BLOCK_ROWS

    def query_one_block(carried, packed):
        q_block, seg_block, slot_block, lse_block, grad_block = packed
        probabilities = score_probs(
            q_block, key_rows, seg_block, slot_block, k_segment, k_slot, lse_block
        )
        d_prob = product(grad_block, value_rows, "qhgd,khd->hgqk")
        delta = jnp.sum(probabilities * d_prob, axis=-1, keepdims=True)
        d_score = (probabilities * (d_prob - delta)).astype(BF)
        q_grad = product(d_score, key_rows, "hgqk,khd->qhgd") * 0.125
        key_grad = carried[0] + product(d_score, q_block, "hgqk,qhgd->khd") * 0.125
        value_grad = carried[1] + product(probabilities.astype(BF), grad_block, "hgqk,qhgd->khd")
        carried = (key_grad, value_grad)
        return (carried, q_grad)

    block_shape = (block_list, QUERY_BLOCK_ROWS) + query_row.shape[1:]
    initial = (jnp.zeros(key_rows.shape, F32), jnp.zeros(key_rows.shape, F32))
    packed = (
        query_row.reshape(block_shape),
        q_segment.reshape(block_list, QUERY_BLOCK_ROWS),
        q_slot.reshape(block_list, QUERY_BLOCK_ROWS),
        log_total,
        grad_heads.reshape(block_shape),
    )
    return lax.scan(query_one_block, initial, packed)


class Grid:
    def __init__(self):
        self.n = lax.axis_size("fsdp")
        self.ctx = lax.axis_size("ctx")
        self.tp = lax.axis_size("tp")
        self.z = lax.axis_index("fsdp")
        self.c = lax.axis_index("ctx")
        self.t = lax.axis_index("tp")

    def ring(self, v):
        return lax.ppermute(v, "fsdp", [(i, (i + 1) % self.n) for i in range(self.n)])

    def flip(self, v, bit):
        return lax.ppermute(v, "ctx", [(i, i ^ bit) for i in range(self.ctx)])

    def order(self):
        return [
            lax.rem(self.z - k + self.n, self.n) * self.ctx + (self.c ^ d)
            for d in range(self.ctx)
            for k in range(self.n)
        ]

    def collect(self, shard):
        have = [shard]
        for _ in range(self.n - 1):
            have.append(self.ring(have[-1]))
        bits = []
        b = self.ctx // 2
        while b:
            bits.append(b)
            b //= 2
        got = {(0, k): v for k, v in enumerate(have)}
        for bit in bits:
            more = {(d | bit, k): self.flip(v, bit) for (d, k), v in got.items()}
            got.update(more)
        return [got[(d, k)] for d in range(self.ctx) for k in range(self.n)]

    def reduce_ctx(self, keep, send):
        total = (keep.astype(F32) + self.flip(send, 1).astype(F32)).astype(BF)
        bit = self.ctx // 2
        stride = keep.shape[0] // 2
        if bit >= 2:
            away = self.flip(total[stride:], bit)
            total = (total[:stride].astype(F32) + away.astype(F32)).astype(BF)
        return total

    def reduce_ring(self, total):
        run = total[1 % self.n]
        for k in range(2, self.n + 1):
            run = self.ring(run).astype(F32) + total[k % self.n].astype(F32)
            if k < self.n:
                run = run.astype(BF)
        return run

    def tp_pair(self, own, other, axis):
        first = jnp.where(self.t == 0, own, other)
        second = jnp.where(self.t == 0, other, own)
        return jnp.concatenate([first, second], axis=axis)

    def tp_gather(self, v):
        if self.tp == 2:
            other = lax.ppermute(v, "tp", [(0, 1), (1, 0)])
            return self.tp_pair(v, other, 1)
        return lax.all_gather(v, "tp", axis=1, tiled=True)

    def tp_sum(self, v):
        if self.tp == 2:
            other = lax.ppermute(v, "tp", [(0, 1), (1, 0)])
            return v.astype(F32) + other.astype(F32)
        return lax.psum(v, "tp").astype(F32)

    def tp_scatter(self, v):
        if self.tp == 2:
            half = v.shape[1] // 2
            own = lax.dynamic_slice_in_dim(v, self.t * half, half, 1)
            away = lax.dynamic_slice_in_dim(v, (1 - self.t) * half, half, 1)
            other = lax.ppermute(away, "tp", [(0, 1), (1, 0)])
            return own.astype(F32) + other.astype(F32)
        return lax.psum_scatter(v, "tp", scatter_dimension=1, tiled=True).astype(F32)


def dot(a, b, ca, cb):
    return lax.dot_general(a, b, (((ca,), (cb,)), ((), ())), preferred_element_type=F32)


def ffn_kernel(pieces, shard_rows, tile, group, offs, mid, dy, gain, *refs):
    wg_in = refs[:pieces]
    wu_in = refs[pieces : 2 * pieces]
    wd_in = refs[2 * pieces : 3 * pieces]
    ffn, dmid, dgain, gk, gs, uk, us, dk, ds = refs[3 * pieces : 3 * pieces + 9]
    (wg, wu, wd, nb, n_t, dy_t, turn, ffn_acc, dn_acc, sem) = refs[3 * pieces + 9 :]
    step = pl.program_id(0)
    steps = pl.num_programs(0)
    n_groups = wg.shape[1] // group
    per_group = group // tile
    half = mid.shape[1] // 2

    def copies(g):
        out = []
        cols = pl.ds(g * group, group)
        for m, (src, dst) in enumerate(((wg_in, wg), (wu_in, wu), (wd_in, wd))):
            for i in range(pieces):
                rows = pl.ds(pl.multiple_of(offs[i], shard_rows), shard_rows)
                out.append(
                    pltpu.make_async_copy(src[i].at[:, cols], dst.at[rows, cols], sem.at[g, m, i])
                )
        return out

    @pl.when(step == 0)
    def _():
        for g in range(n_groups):
            for c in copies(g):
                c.start()
        v = mid[...].astype(F32)
        scale = lax.rsqrt(jnp.mean(v * v, axis=1, keepdims=True) + EPSILON)
        normed = v * scale * gain[...]
        nb[...] = normed.astype(BF)
        ffn_acc[...] = jnp.zeros_like(ffn_acc)
        dn_acc[...] = jnp.zeros_like(dn_acc)
        for value, to in ((normed, n_t), (dy[...].astype(F32), dy_t)):
            turn[...] = value.T.astype(BF)
            for i in range(pieces):
                row = pl.multiple_of(offs[pieces + i], shard_rows)
                to[i * shard_rows : (i + 1) * shard_rows, :] = turn[pl.ds(row, shard_rows), :]

    for g in range(n_groups):

        @pl.when(step == g * per_group)
        def _(g=g):
            for c in copies(g):
                c.wait()

    cols = pl.ds(pl.multiple_of(step * tile, tile), tile)
    w_gate = wg[:, cols]
    w_up = wu[:, cols]
    w_down = wd[:, cols]
    normed = nb[...]
    dyb = dy[...]
    gate = dot(normed, w_gate, 1, 0)
    up = dot(normed, w_up, 1, 0)
    d_hidden = dot(dyb, w_down, 1, 0)
    sig = 1.0 / (1.0 + jnp.exp(-gate))
    silu = gate * sig
    hidden = (silu * up).astype(BF)
    d_gate = (d_hidden * up * (sig * (1.0 + gate * (1.0 - sig)))).astype(BF)
    d_up = (d_hidden * silu).astype(BF)
    ffn_acc[...] += dot(hidden, w_down, 1, 1)
    dn_acc[...] += dot(d_gate, w_gate, 1, 1) + dot(d_up, w_up, 1, 1)
    for left, right, keep, send in (
        (n_t, d_gate, gk, gs),
        (n_t, d_up, uk, us),
        (dy_t, hidden, dk, ds),
    ):
        keep[...] = dot(left[:half, :], right, 1, 0).astype(BF)
        send[...] = dot(left[half:, :], right, 1, 0).astype(BF)

    @pl.when(step == steps - 1)
    def _():
        v = mid[...].astype(F32)
        scale = lax.rsqrt(jnp.mean(v * v, axis=1, keepdims=True) + EPSILON)
        unit = v * scale
        dn = dn_acc[...]
        dgain[...] = jnp.sum(dn * unit, axis=0, keepdims=True)
        scaled = dn * gain[...]
        dmid[...] = (
            scale * (scaled - unit * jnp.mean(scaled * unit, axis=1, keepdims=True))
        ).astype(BF)
        ffn[...] = ffn_acc[...].astype(BF)


def ffn_pass(mid, dy, gain, gate_p, up_p, down_p, offsets):
    rows, width = mid.shape
    pieces = len(gate_p)
    shard_rows, ff = gate_p[0].shape
    tile = 256 if ff % 256 == 0 else 128
    group = 3 * tile if ff % (3 * tile) == 0 else tile
    half = width // 2
    whole = lambda shape: pl.BlockSpec(shape, lambda s, o: (0, 0))
    column = pl.BlockSpec((half, tile), lambda s, o: (0, s))
    grad = jax.ShapeDtypeStruct((half, ff), BF)
    return pl.pallas_call(
        functools.partial(ffn_kernel, pieces, shard_rows, tile, group),
        grid_spec=pltpu.PrefetchScalarGridSpec(
            num_scalar_prefetch=1,
            grid=(ff // tile,),
            in_specs=[whole((rows, width)), whole((rows, width)), whole((1, width))]
            + [pl.BlockSpec(memory_space=pl.ANY)] * (3 * pieces),
            out_specs=[whole((rows, width)), whole((rows, width)), whole((1, width))]
            + [column] * 6,
            scratch_shapes=[
                pltpu.VMEM((width, ff), BF),
                pltpu.VMEM((width, ff), BF),
                pltpu.VMEM((width, ff), BF),
                pltpu.VMEM((rows, width), BF),
                pltpu.VMEM((width, rows), BF),
                pltpu.VMEM((width, rows), BF),
                pltpu.VMEM((width, rows), BF),
                pltpu.VMEM((rows, width), F32),
                pltpu.VMEM((rows, width), F32),
                pltpu.SemaphoreType.DMA((ff // group, 3, pieces)),
            ],
        ),
        out_shape=[
            jax.ShapeDtypeStruct((rows, width), BF),
            jax.ShapeDtypeStruct((rows, width), BF),
            jax.ShapeDtypeStruct((1, width), F32),
        ]
        + [grad] * 6,
        compiler_params=pltpu.CompilerParams(vmem_limit_bytes=58 * 2**20),
        cost_estimate=pl.CostEstimate(
            flops=18 * rows * width * ff, bytes_accessed=12 * width * ff, transcendentals=rows * ff
        ),
    )(offsets, mid, dy, gain, *gate_p, *up_p, *down_p)


def pad_columns(v, to):
    return v if v.shape[1] == to else jnp.pad(v, ((0, 0), (0, to - v.shape[1])))


def pick_blocks(stack, order):
    return jnp.concatenate([lax.dynamic_slice_in_dim(stack, i, 1, 0) for i in order], axis=0)


def one_hot(rows, columns):
    return (rows == columns).astype(BF)


def local(
    tokens,
    cotangent,
    slot_of,
    lengths,
    w_query,
    key_weight,
    value_weight,
    w_out,
    w_gate,
    w_up,
    w_down,
    gain_attn,
    gain_ffn,
    gain_query,
    gain_key,
):
    grid = Grid()
    stream_len = tokens.shape[0]
    feat_len = tokens.shape[1]
    local_len = PACKED_ROW_SLOTS // grid.ctx
    row_count = stream_len // local_len
    groups = grid.n * grid.ctx
    share = stream_len // groups
    q_heads = QUERY_HEADS // grid.tp
    key_value_heads = KEY_VALUE_HEADS // grid.tp
    query_group_width = QUERY_HEADS // KEY_VALUE_HEADS
    q_width = q_heads * HEAD_SIZE
    kv_width = key_value_heads * HEAD_SIZE
    flat_len = row_count * local_len
    row_len = PACKED_ROW_SLOTS
    me = grid.z * grid.ctx + grid.c
    both = ("fsdp", "ctx")

    def home(slots):
        row, place = slots // row_len, slots % row_len
        return (
            row // row_count * grid.ctx + place // local_len,
            row % row_count * local_len + place % local_len,
        )

    my_slots = lax.dynamic_slice_in_dim(slot_of, me * stream_len, stream_len, 0)
    my_target = home(my_slots)[0]
    ahead = (my_target[:, None] == my_target[None, :]) & (my_slots[None, :] < my_slots[:, None])
    send_place = my_target * share + jnp.sum(ahead.astype(jnp.int32), axis=1)
    line = jnp.arange(stream_len, dtype=jnp.int32)
    send_pick = one_hot(line[:, None], send_place[None, :])
    all_dev, all_local = home(slot_of)
    low = 32
    high = flat_len // low
    sender = (jnp.arange(slot_of.shape[0], dtype=jnp.int32) // stream_len).astype(F32)
    mine = (all_dev == me)[None, :] & (
        (all_local // low)[None, :] == jnp.arange(high, dtype=jnp.int32)[:, None]
    )
    left = jnp.where(mine, sender[None, :], 0.0).astype(BF)
    right = one_hot((all_local % low)[:, None], jnp.arange(low, dtype=jnp.int32)[None, :])
    source = product(left, right, "ht,tl->hl").reshape(flat_len).astype(jnp.int32)
    slot_line = jnp.arange(flat_len, dtype=jnp.int32)
    before = (source[:, None] == source[None, :]) & (slot_line[None, :] < slot_line[:, None])
    arrival = source * share + jnp.sum(before.astype(jnp.int32), axis=1)
    take_pick = one_hot(arrival[:, None], line[None, :])

    def spread(v):
        sent = product(send_pick, v, "pt,tf->pf").astype(BF)
        got = lax.all_to_all(sent, both, split_axis=0, concat_axis=0, tiled=True)
        return product(take_pick, got, "ja,af->jf").astype(BF)

    def bring_back(v):
        sent = product(take_pick, v, "ja,jf->af").astype(BF)
        got = lax.all_to_all(sent, both, split_axis=0, concat_axis=0, tiled=True)
        return product(send_pick, got, "pt,pf->tf").astype(BF)

    ff = w_gate.shape[1]
    ff_pad = -(-ff // 128) * 128
    attn_shard = jnp.concatenate([w_query, key_weight, value_weight, w_out.T], axis=1)
    attn_pieces = grid.collect(attn_shard)
    gate_p, up_p, down_p = (
        grid.collect(pad_columns(v, ff_pad)) for v in (w_gate, w_up, w_down.T)
    )
    shard_rows = w_gate.shape[0]
    order = grid.order()
    grad_order = [d for d in range(0, grid.ctx, 2)] + [d for d in range(1, grid.ctx, 2)]
    grad_order = [order[d * grid.n + k] for d in grad_order for k in range(grid.n)]
    offsets = (jnp.stack(order + grad_order) * shard_rows).astype(jnp.int32)

    packed_tok = spread(tokens)
    packed_cot = spread(cotangent)
    own_slots = grid.c * local_len + jnp.arange(local_len, dtype=jnp.int32)
    row_slots = jnp.arange(row_len, dtype=jnp.int32)

    def tables(row_lengths):
        q_segment, q_position = slot_tables(row_lengths, own_slots)
        k_segment = slot_tables(row_lengths, row_slots)[0]
        return (q_segment, q_position, k_segment)

    q_segment, q_position, k_segment = jax.vmap(tables)(lengths)
    cosines, sines = angle_tables(q_position.reshape(flat_len))
    x_full = grid.tp_gather(packed_tok)
    dy_full = grid.tp_gather(packed_cot)
    x_float = x_full.astype(F32)
    normed_f, attn_norm_pull = jax.vjp(rms_scale, x_float, gain_attn)
    first_normed = normed_f.astype(BF)

    stack = jnp.stack(attn_pieces)
    inverse = [
        (i % grid.ctx ^ grid.c) * grid.n + lax.rem(grid.z - i // grid.ctx + grid.n, grid.n)
        for i in range(groups)
    ]
    attn_w = pick_blocks(stack, inverse).reshape(MODEL_WIDTH, attn_shard.shape[1])
    a, b, c = q_width, q_width + kv_width, q_width + 2 * kv_width
    query_w, key_w, value_w, out_t = attn_w[:, :a], attn_w[:, a:b], attn_w[:, b:c], attn_w[:, c:]

    query_raw = product(first_normed, query_w, "nd,de->ne")
    key_raw = product(first_normed, key_w, "nd,de->ne")
    value_b = product(first_normed, value_w, "nd,de->ne").astype(BF)

    def head_prep(query_in, key_in, gain_q, gain_k):
        query_out = rotate(
            rms_scale(query_in.reshape(flat_len, q_heads, HEAD_SIZE), gain_q), cosines, sines
        )
        key_out = rotate(
            rms_scale(key_in.reshape(flat_len, key_value_heads, HEAD_SIZE), gain_k), cosines, sines
        )
        return (query_out, key_out)

    (query_rot, key_rot), prep_pull = jax.vjp(head_prep, query_raw, key_raw, gain_query, gain_key)
    query_b = query_rot.astype(BF)
    key_b = key_rot.astype(BF).reshape(flat_len, kv_width)
    local_kv = jnp.concatenate([key_b, value_b], axis=1).reshape(row_count, local_len, 2 * kv_width)
    row_kv = lax.all_gather(local_kv, "ctx", axis=1, tiled=True)
    key_rows = row_kv[..., :kv_width].reshape(row_count, row_len, key_value_heads, HEAD_SIZE)
    value_rows = row_kv[..., kv_width:].reshape(row_count, row_len, key_value_heads, HEAD_SIZE)
    query_rows = query_b.reshape(
        row_count, local_len, key_value_heads, query_group_width, HEAD_SIZE
    )

    def row_forward(packed):
        q_row, k_row, v_row, qs_row, ks_row = packed
        return attend_row(q_row, k_row, v_row, qs_row, own_slots, ks_row, row_slots)

    head_out, log_total = lax.map(
        row_forward, (query_rows, key_rows, value_rows, q_segment, k_segment)
    )
    heads_b = head_out.reshape(flat_len, q_width).astype(BF)
    attn_part = product(heads_b, out_t, "nq,dq->nd")
    attn_full = grid.tp_sum(attn_part.astype(BF))
    middle_full = x_float + attn_full
    middle_b = middle_full.astype(BF)
    own_features = lambda v: lax.dynamic_slice_in_dim(v, grid.t * feat_len, feat_len, 1)
    attn_own = own_features(attn_full)
    token_f = packed_tok.astype(F32)
    middle_own = token_f + attn_own

    ffn_part, d_mid_part, d_gain_ffn, *grads = ffn_pass(
        middle_b, dy_full, gain_ffn[None, :], gate_p, up_p, down_p, offsets
    )
    ffn_out = grid.tp_scatter(ffn_part)
    d_back = grid.tp_sum(d_mid_part)
    d_middle_full = dy_full.astype(F32) + d_back
    d_middle = own_features(d_middle_full)
    d_attn = d_middle_full.astype(BF)

    def reduce_weight(keep, send):
        blocks = (keep.shape[0] // shard_rows, shard_rows, keep.shape[1])
        return grid.reduce_ring(grid.reduce_ctx(keep.reshape(blocks), send.reshape(blocks)))

    sum_gate = reduce_weight(grads[0], grads[1])[:, :ff]
    sum_up = reduce_weight(grads[2], grads[3])[:, :ff]
    sum_down = reduce_weight(grads[4], grads[5])[:, :ff].T

    g_out = product(d_attn, heads_b, "nd,nq->dq")
    d_heads = product(d_attn, out_t, "nd,dq->nq").astype(BF)
    grad_rows = d_heads.reshape(row_count, local_len, key_value_heads, query_group_width, HEAD_SIZE)

    def row_query_keys(packed):
        q_row, k_row, v_row, qs_row, ks_row, lse_row, g_row = packed
        return query_back(q_row, k_row, v_row, qs_row, own_slots, ks_row, row_slots, lse_row, g_row)

    (key_grads, value_grads), q_grads = lax.map(
        row_query_keys,
        (query_rows, key_rows, value_rows, q_segment, k_segment, log_total, grad_rows),
    )
    kv_grads = jnp.concatenate(
        [
            key_grads.reshape(row_count, row_len, kv_width),
            value_grads.reshape(row_count, row_len, kv_width),
        ],
        axis=2,
    )
    own_kv = lax.psum_scatter(
        kv_grads.astype(BF), "ctx", scatter_dimension=1, tiled=True
    ).astype(F32)
    d_key_rot = own_kv[..., :kv_width].reshape(flat_len, key_value_heads, HEAD_SIZE)
    d_value = own_kv[..., kv_width:].reshape(flat_len, kv_width).astype(BF)
    d_query_raw, d_key_raw, d_gain_q, d_gain_k = prep_pull(
        (q_grads.reshape(flat_len, q_heads, HEAD_SIZE), d_key_rot)
    )
    d_query = d_query_raw.astype(BF)
    d_key = d_key_raw.astype(BF)
    d_qkv = jnp.concatenate([d_query, d_key, d_value], axis=1)
    g_qkv = product(first_normed, d_qkv, "nd,ne->de")
    d_normed_one = product(d_qkv, attn_w[:, :c], "ne,de->nd")
    d_x_part, d_gain_attn = attn_norm_pull(d_normed_one)
    d_x = grid.tp_scatter(d_x_part.astype(BF))
    grad_packed = (d_middle + d_x).astype(BF)
    output_packed = (middle_own + ffn_out).astype(BF)

    g_attn = jnp.concatenate([g_qkv.astype(BF), g_out.astype(BF)], axis=1)
    g_blocks = pick_blocks(g_attn.reshape(groups, shard_rows, -1), grad_order)
    sum_attn = grid.reduce_ring(
        grid.reduce_ctx(g_blocks[: groups // 2], g_blocks[groups // 2 :])
    )
    squares = jnp.stack(
        [jnp.sum(token_f * token_f), jnp.sum(attn_own * attn_own), jnp.sum(ffn_out * ffn_out)]
    )
    small = jnp.concatenate([d_gain_attn, d_gain_ffn[0], d_gain_q, d_gain_k, squares])
    small = lax.psum(small, ("fsdp", "ctx", "tp"))
    w, h = MODEL_WIDTH, HEAD_SIZE
    gain_a, gain_f = small[:w], small[w : 2 * w]
    gain_qs, gain_ks = small[2 * w : 2 * w + h], small[2 * w + h : 2 * w + 2 * h]
    entry_count = flat_len * groups * MODEL_WIDTH
    rms_stats = jnp.sqrt(small[2 * w + 2 * h :] / entry_count)
    output = bring_back(output_packed)
    grad_tokens = bring_back(grad_packed)
    return (
        output,
        grad_tokens,
        sum_attn[:, :a],
        sum_attn[:, a:b],
        sum_attn[:, b:c],
        sum_attn[:, c:].T,
        sum_gate,
        sum_up,
        sum_down,
        gain_a,
        gain_f,
        gain_qs,
        gain_ks,
        rms_stats,
    )


def solution(mesh):
    row = P(("fsdp", "ctx"), "tp")
    column = P("tp", ("fsdp", "ctx"))
    in_specs = (row, row, P(), P("fsdp", None), row, row, row, column, row, row, column) + (P(),) * 4
    out_specs = (row, row, row, row, row, column, row, row, column) + (P(),) * 5
    return jax.shard_map(local, mesh=mesh, in_specs=in_specs, out_specs=out_specs, check_vma=False)
```

time: 1120 us -> 691 us (0.62)
  waiting for transfers between devices: 670 us -> 243 us
  starting transfers between devices: 18.7 us -> 81.4 us
  blocking collectives: 101 us -> 46.7 us
  matrix products: 168 us -> 115 us
  Pallas kernels: 0 us -> 35.7 us
  local copies, waits for them, and re-layouts: 35.7 us -> 50.1 us
  other arithmetic: 105 us -> 92 us
    reduce_scatter x11 -> x1, waiting for transfers between devices: 428 us -> 0.01 us  [local(): lax.psum_scatter(kv_grads.astype(BF), 'ctx', scatter_dimension=1, tiled=T...]
    ppermute x0 -> x86, waiting for transfers between devices: none -> 243 us  [the longest x56 115 us: flip(): return lax.ppermute(v, 'ctx', [(i, i ^ bit) for i in range(self.ctx)])]
    all_gather x8 -> x0, waiting for transfers between devices: 202 us -> none  [the longest x1 55.8 us: local(): lax.all_gather(w_down, ('fsdp', 'ctx'), axis=1, tiled=True)]
    ppermute x0 -> x86, starting transfers between devices: none -> 61.5 us  [the longest x56 28.6 us: flip(): return lax.ppermute(v, 'ctx', [(i, i ^ bit) for i in range(self.ctx)])]
    dot_general x27 -> x23, matrix products: 168 us -> 115 us  [product(): return jnp.einsum(pattern, left_arr, right_arr, preferred_element_type=F32)]
    all_gather x2 -> x0, blocking collectives: 42.1 us -> none  [the longest x1 23.3 us: local(): lax.all_gather(key_weight, ('fsdp', 'ctx'), axis=0, tiled=True)]
    pallas_call x0 -> x1, Pallas kernels: none -> 35.7 us  [ffn_pass(): pl.pallas_call(functools.partial(ffn_kernel, pieces, shard_rows, tile, gr...]
    unnamed x132 -> x232, local copies, waits for them, and re-layouts: 7.07 us -> 30.8 us
  transfers between devices with their start and end apart: 24 -> 92, of which waited for: 18 -> 27; matrix products, arithmetic and copies ran while one was open for 16% -> 35% of each run, Pallas kernels for 0% -> 0%
where the time goes in v1:
time: 691 us; the launch traced here: 682 us
  waiting for transfers between devices  243 us (35%)
  matrix products  115 us (17%)
  other arithmetic  92 us (13%)
  starting transfers between devices  81.4 us (12%)
  local copies, waits for them, and re-layouts  50.1 us (7%)
  blocking collectives  46.7 us (7%)
  Pallas kernels  35.7 us (5%)
  between operations  18.4 us (3%)
    ppermute x56, waiting for transfers between devices, flip(): return lax.ppermute(v, 'ctx', [(i, i ^ bit) for i in range(self.ctx)])  115 us
    dot_general x23, matrix products, product(): return jnp.einsum(pattern, left_arr, right_arr, preferred_element_type=F32)  115 us
    ppermute x24, waiting for transfers between devices, ring(): lax.ppermute(v, 'fsdp', [(i, (i + 1) % self.n) for i in range(self.n)])  73.7 us
    psum x1, blocking collectives, local(): small = lax.psum(small, ('fsdp', 'ctx', 'tp'))  46.7 us
    pallas_call x1, Pallas kernels, ffn_pass(): pl.pallas_call(functools.partial(ffn_kernel, pieces, shard_rows, tile, gr...  35.7 us
    unnamed x232, local copies, waits for them, and re-layouts  30.8 us
    ppermute x2, waiting for transfers between devices, tp_scatter(): other = lax.ppermute(away, 'tp', [(0, 1), (1, 0)])  30 us
    ppermute x56, starting transfers between devices, flip(): return lax.ppermute(v, 'ctx', [(i, i ^ bit) for i in range(self.ctx)])  28.6 us
  transfers between devices with their start and end apart: 92, of which 27 were waited for; matrix products, arithmetic and copies ran while one was open for 35% of the time, Pallas kernels for 0%

profile of v1, /device:TPU:0, one launch (start us, length us, event | category | flops | bytes accessed | tf_op | source)
XLA Modules:
  0.0 681.7 jit_solution(6318716611059549788)
XLA Ops:
  31.1 11.2 %collective-permute-done.2 = bf16[64,1536]{1,0:T(8,128)(2,1)S(1)} collective-permute-done((bf16[64,1536]{1,0:T(8,128)(2,1)S(1)}, bf16[64,1536]{1,0:T(8,128)(2,1)S(1)}, u32[]{:S(2)}, u32[]{:S(2)}) %collective-permute-start.2) | collective-permute-done | bytes 196640 | tf_op jit(solution)/shard_map/ppermute | solution.py:144
  43.4 7.1 %collective-permute-done.3 = bf16[64,1536]{1,0:T(8,128)(2,1)S(1)} collective-permute-done((bf16[64,1536]{1,0:T(8,128)(2,1)S(1)}, bf16[64,1536]{1,0:T(8,128)(2,1)S(1)}, u32[]{:S(2)}, u32[]{:S(2)}) %collective-permute-start.3) | collective-permute-done | bytes 196640 | tf_op jit(solution)/shard_map/ppermute | solution.py:144
  105.8 11.2 %collective-permute-done.25.refs_8_ = bf16[64,2304]{1,0:T(8,128)(2,1)S(1)} collective-permute-done((bf16[64,2304]{1,0:T(8,128)(2,1)}, bf16[64,2304]{1,0:T(8,128)(2,1)S(1)}, u32[]{:S(2)}, u32[]{:S(2)}) %collective-permute-start.25) | collective-permute-done | bytes 294944 | tf_op jit(solution)/shard_map/ppermute | solution.py:147
  136.6 13.6 %fusion.5 = (f32[4,2,512]{2,1,0:T(2,128)S(1)}, f32[4,2048,512,2]{2,1,3,0:T(8,128)}) fusion(pred[512,2048]{0,1:T(8,128)(4,1)S(1)} %fusion.15, bf16[2048,4,64,1]{0,2,3,1:T(8,128)(2,1)S(1)} %bitcast.276, bf16[512,4,2,32]{0,3,2,1:T(8,128)(2,1)S(1)} %bitcast.290, bf16[512,4,2,32]{0,3,2,1:T(8,128)(2,1)S(1)} %bitcast.287), kind=kOutput, calls=%fused_computation.11 | convolution fusion | flops 1099952128 | bytes 36192256 | tf_op jit(solution)/shard_map/while/body/eval_jaxpr/while/body/eval_jaxpr/qhgd,khd->hgqk/dot_general | solution.py:64
  152.6 14.3 %fusion.6 = f32[4,2,512]{2,1,0:T(2,128)S(1)} fusion(f32[4,2048,512,2]{2,1,3,0:T(8,128)} %get-tuple-element.255, f32[4,2,512]{2,1,0:T(2,128)S(1)} %get-tuple-element.254, pred[512,2048]{0,1:T(8,128)(4,1)S(1)} %fusion.15), kind=kLoop, calls=%fused_computation.12 | loop fusion | flops 33550336 | bytes 34635776 | tf_op jit(solution)/shard_map/while/body/eval_jaxpr/while/body/eval_jaxpr/reduce_sum | solution.py:86
  171.5 14.4 %fusion.34 = bf16[4,64,2,512]{3,1,2,0:T(8,128)(2,1)S(1)} fusion(bf16[2048,4,64,1]{0,2,3,1:T(8,128)(2,1)S(1)} %bitcast.273, f32[4,2048,512,2]{2,1,3,0:T(8,128)} %get-tuple-element.255, f32[4,2,512]{2,1,0:T(2,128)S(1)} %fusion.6, f32[4,2,512]{2,1,0:T(2,128)S(1)} %get-tuple-element.254, pred[512,2048]{0,1:T(8,128)(4,1)S(1)} %fusion.15), kind=kOutput, calls=%fused_computation.71 | convolution fusion | flops 1115947008 | bytes 36208640 | tf_op jit(solution)/shard_map/while/body/eval_jaxpr/while/body/eval_jaxpr/hgqk,khd->qhgd/dot_general | solution.py:64
  209.8 20.3 %collective-permute-done.17 = bf16[512,512]{1,0:T(8,128)(2,1)S(1)} collective-permute-done((bf16[512,512]{1,0:T(8,128)(2,1)S(1)}, bf16[512,512]{1,0:T(8,128)(2,1)S(1)}, u32[]{:S(2)}, u32[]{:S(2)}) %collective-permute-start.17) | collective-permute-done | bytes 524320 | tf_op jit(solution)/shard_map/ppermute | solution.py:195
  244.9 35.7 %shard_map.254 = (bf16[512,1024]{1,0:T(8,128)(2,1)}, bf16[512,1024]{1,0:T(8,128)(2,1)}, f32[1,1024]{1,0:T(1,128)}, bf16[512,2304]{1,0:T(8,128)(2,1)}, bf16[512,2...) custom-call(s32[32]{0:T(128)} %broadcast_multiply_fusion.offs, ...), custom_call_target="tpu_custom_call" | custom-call | flops 21743271936 | bytes 28311552 | tf_op jit(solution)/shard_map/pallas_call | solution.py:314
  287.3 30.0 %collective-permute-done.63 = bf16[512,512]{1,0:T(8,128)(2,1)} collective-permute-done((bf16[512,512]{1,0:T(8,128)(2,1)}, bf16[512,512]{1,0:T(8,128)(2,1)}, u32[]{:S(2)}, u32[]{:S(2)}) %collective-permute-start.63) | collective-permute-done | bytes 524320 | tf_op jit(solution)/shard_map/ppermute | solution.py:210
  333.1 15.8 %fusion.21 = bf16[4,64,2048]{2,1,0:T(8,128)(2,1)} fusion(bf16[512,4,2,64]{0,3,2,1:T(8,128)(2,1)} %bitcast.282, f32[4,2048,512,2]{2,1,3,0:T(8,128)} %get-tuple-element.255, f32[4,2,512]{2,1,0:T(2,128)S(1)} %bitcast.310, pred[512,2048]{0,1:T(8,128)(4,1)S(1)} %fusion.15), kind=kOutput, calls=%fused_computation.37 | convolution fusion | flops 1107820544 | bytes 36192256 | tf_op jit(solution)/shard_map/while/body/eval_jaxpr/while/body/eval_jaxpr/hgqk,qhgd->khd/dot_general | solution.py:64
  348.9 23.5 %fusion = (f32[4,2,512]{2,1,0:T(2,128)S(1)}, f32[4,2048,512,2]{2,1,3,0:T(8,128)}) fusion(f32[4,2048,512,2]{2,1,3,0:T(8,128)} %get-tuple-element.255, f32[4,2,512]{2,1,0:T(2,128)S(1)} %bitcast.311, pred[512,2048]{0,1:T(8,128)(4,1)S(1)} %fusion.15, bf16[2048,4,64,1]{0,2,3,1:T(8,128)(2,1)S(1)} %bitcast.274, bf16[512,4,2,64]{0,3,2,1:T(8,128)(2,1)} %bitcast.283), kind=kOutput, calls=%fused_computation.2 | convolution fusion | flops 1115680768 | bytes 69763072 | tf_op jit(solution)/shard_map/while/body/eval_jaxpr/while/body/eval_jaxpr/qhgd,khd->hgqk/dot_general | solution.py:64
  372.4 28.3 %fusion.2 = bf16[4,2,512,2048]{2,3,1,0:T(8,128)(2,1)} fusion(f32[4,2048,512,2]{2,1,3,0:T(8,128)} %get-tuple-element.257, f32[4,2048,512,2]{2,1,3,0:T(8,128)} %get-tuple-element.255, f32[4,2,512]{2,1,0:T(2,128)S(1)} %get-tuple-element.256, f32[4,2,512]{2,1,0:T(2,128)S(1)} %bitcast.312, pred[512,2048]{0,1:T(8,128)(4,1)S(1)} %fusion.15), kind=kLoop, calls=%fused_computation.4 | loop fusion | flops 50331648 | bytes 84967424 | tf_op jit(solution)/shard_map/while/body/eval_jaxpr/while/body/eval_jaxpr/convert_element_type | solution.py:115
  400.7 11.0 %fusion.20 = bf16[4,64,2048]{2,1,0:T(8,128)(2,1)S(1)} fusion(bf16[4,2,512,2048]{2,3,1,0:T(8,128)(2,1)} %fusion.2, bf16[512,4,2,32]{0,3,2,1:T(8,128)(2,1)} %bitcast.289, bf16[512,4,2,32]{0,3,2,1:T(8,128)(2,1)S(1)} %bitcast.288), kind=kOutput, calls=%fused_computation.36 | convolution fusion | flops 1075838976 | bytes 18350080 | tf_op jit(solution)/shard_map/while/body/eval_jaxpr/while/body/eval_jaxpr/hgqk,qhgd->khd/dot_general | solution.py:64
  414.7 8.7 %convolution_multiply_fusion = f32[4,64,2,512]{3,1,2,0:T(8,128)S(1)} fusion(bf16[2048,4,64,1]{0,2,3,1:T(8,128)(2,1)S(1)} %bitcast.277, bf16[4,2,512,2048]{2,3,1,0:T(8,128)(2,1)} %fusion.2), kind=kOutput, calls=%fused_computation.61 | convolution fusion | flops 1074003968 | bytes 18874368 | tf_op jit(solution)/shard_map/while/body/eval_jaxpr/while/body/eval_jaxpr/hgqk,khd->qhgd/dot_general | solution.py:64
  443.5 28.4 %collective-permute-done.72 = bf16[4,64,2304]{2,1,0:T(8,128)(2,1)S(1)} collective-permute-done((bf16[4,64,2304]{2,1,0:T(8,128)(2,1)S(1)}, bf16[4,64,2304]{2,1,0:T(8,128)(2,1)S(1)}, u32[]{:S(2)}, u32[]{:S(2)}) %collective-permute-start.72) | collective-permute-done | bytes 1179680 | tf_op jit(solution)/shard_map/ppermute | solution.py:147
  473.7 23.5 %collective-permute-done.77 = bf16[4,64,2304]{2,1,0:T(8,128)(2,1)S(1)} collective-permute-done((bf16[4,64,2304]{2,1,0:T(8,128)(2,1)S(1)}, bf16[4,64,2304]{2,1,0:T(8,128)(2,1)S(1)}, u32[]{:S(2)}, u32[]{:S(2)}) %collective-permute-start.77) | collective-permute-done | bytes 1179680 | tf_op jit(solution)/shard_map/ppermute | solution.py:147
  499.0 23.2 %collective-permute-done.82 = bf16[4,64,2304]{2,1,0:T(8,128)(2,1)S(1)} collective-permute-done((bf16[4,64,2304]{2,1,0:T(8,128)(2,1)S(1)}, bf16[4,64,2304]{2,1,0:T(8,128)(2,1)S(1)}, u32[]{:S(2)}, u32[]{:S(2)}) %collective-permute-start.82) | collective-permute-done | bytes 1179680 | tf_op jit(solution)/shard_map/ppermute | solution.py:147
  527.3 7.0 %collective-permute-done.83 = bf16[64,2304]{1,0:T(8,128)(2,1)S(1)} collective-permute-done((bf16[64,2304]{1,0:T(8,128)(2,1)S(1)}, bf16[64,2304]{1,0:T(8,128)(2,1)S(1)}, u32[]{:S(2)}, u32[]{:S(2)}) %collective-permute-start.83) | collective-permute-done | bytes 294944 | tf_op jit(solution)/shard_map/ppermute | solution.py:144
  534.4 6.2 collective-permute-done.74
  540.7 6.2 collective-permute-done.79
  588.4 46.7 %psum.7 = f32[2179]{0:T(1024)S(1)} all-reduce(f32[2179]{0:T(1024)S(1)} %concatenate.76), channel_id=1, replica_groups=mesh['fsdp'=4,'ctx'=4,'tp'=2] {'fsdp','ctx','tp'}, use_global_device_ids=true, to_apply=%region_18.19 | all-reduce | flops 2179 | bytes 17432 | tf_op jit(solution)/shard_map/psum | solution.py:577
  640.4 6.4 all-to-all-start.3
  650.4 14.2 %collective-permute-done.69 = bf16[64,1536]{1,0:T(8,128)(2,1)S(1)} collective-permute-done((bf16[64,1536]{1,0:T(8,128)(2,1)S(1)}, bf16[64,1536]{1,0:T(8,128)(2,1)S(1)}, u32[]{:S(2)}, u32[]{:S(2)}) %collective-permute-start.69) | collective-permute-done | bytes 196640 | tf_op jit(solution)/shard_map/ppermute | solution.py:144
  666.5 6.5 collective-permute-done.70
  (512 shorter events, 250.0 us)
Async XLA Ops:
  8.2 44.4 %collective-permute-start.4 = (bf16[64,1536]{1,0:T(8,128)(2,1)S(1)}, bf16[64,1536]{1,0:T(8,128)(2,1)S(1)}, u32[]{:S(2)}, u32[]{:S(2)}) collective-permute-start(bf16[64,1536]{1,0:T(8,128)(2,1)S(1)} %pad_maximum_fusion.12), channel_id=1, source_target_pairs={{0,2},{2,0},{4,6},{6,4},{1,3},{3,1},{5,7},{7,5},{8,10},{10,8},{12,... | collective-permute-start | bytes 589832 | tf_op jit(solution)/shard_map/ppermute | solution.py:147
  20.5 45.8 %all-to-all-start = ((bf16[16,32,512]{2,1,0:T(8,128)(2,1)}), bf16[16,32,512]{2,1,0:T(8,128)(2,1)S(1)}, u32[]{:S(2)}, u32[]{:S(2)}) async-start(bf16[16,32,512]{2,1,0:T(8,128)(2,1)} %bitcast), calls=%async_computation | async-start | bytes 1048576 | tf_op jit(solution)/shard_map/all_to_all | solution.py:425
  24.5 101.3 %all-gather.3.cloned.1.call-start = ((), (), s32[]{:S(2)}) async-start(), calls=%async_computation.6 | async-start | bytes 2621440 | tf_op jit(solution)/shard_map/all_gather | solution.py:490
  26.7 26.0 %collective-permute-start.9 = (bf16[64,1536]{1,0:T(8,128)(2,1)S(1)}, bf16[64,1536]{1,0:T(8,128)(2,1)S(1)}, u32[]{:S(2)}, u32[]{:S(2)}) collective-permute-start(bf16[64,1536]{1,0:T(8,128)(2,1)S(1)} %collective-permute-done.1), channel_id=1, source_target_pairs={{0,4},{2,6},{4,0},{6,2},{1,5},{3,7},{5,1},{7,3},{8,12},{10,14},{12... | collective-permute-start | bytes 589832 | tf_op jit(solution)/shard_map/ppermute | solution.py:147
  30.1 34.1 %collective-permute-start.12 = (bf16[64,1536]{1,0:T(8,128)(2,1)S(1)}, bf16[64,1536]{1,0:T(8,128)(2,1)S(1)}, u32[]{:S(2)}, u32[]{:S(2)}) collective-permute-start(bf16[64,1536]{1,0:T(8,128)(2,1)S(1)} %collective-permute-done.8), channel_id=1, source_target_pairs={{0,2},{2,0},{4,6},{6,4},{1,3},{3,1},{5,7},{7,5},{8,10},{10,8},{12,... | collective-permute-start | bytes 589832 | tf_op jit(solution)/shard_map/ppermute | solution.py:147
  89.3 105.7 %all-to-all-start.1 = ((bf16[16,32,512]{2,1,0:T(8,128)(2,1)}), bf16[16,32,512]{2,1,0:T(8,128)(2,1)}, u32[]{:S(2)}, u32[]{:S(2)}) async-start(bf16[16,32,512]{2,1,0:T(8,128)(2,1)} %bitcast.56), calls=%async_computation.1 | async-start | bytes 1048576 | tf_op jit(solution)/shard_map/all_to_all | solution.py:425
  193.5 45.9 %collective-permute-start.16 = (bf16[512,1024]{1,0:T(8,128)(2,1)}, bf16[512,1024]{1,0:T(8,128)(2,1)}, u32[]{:S(2)}, u32[]{:S(2)}) collective-permute-start(bf16[512,1024]{1,0:T(8,128)(2,1)} %convolution_convert_fusion.2), channel_id=1, source_target_pairs={{0,1},{1,0},{2,3},{3,2},{4,5},{5,4},{6,7},{7,6},{8,9},{9,8},{10,11... | collective-permute-start | bytes 3145736 | tf_op jit(solution)/shard_map/ppermute | solution.py:201
  196.6 33.6 %collective-permute-start.17 = (bf16[512,512]{1,0:T(8,128)(2,1)S(1)}, bf16[512,512]{1,0:T(8,128)(2,1)S(1)}, u32[]{:S(2)}, u32[]{:S(2)}) collective-permute-start(bf16[512,512]{1,0:T(8,128)(2,1)S(1)} %convolution_convert_fusion.7), channel_id=1, source_target_pairs={{0,1},{1,0},{2,3},{3,2},{4,5},{5,4},{6,7},{7,6},{8,9},{9,8},{10,11... | collective-permute-start | bytes 1572872 | tf_op jit(solution)/shard_map/ppermute | solution.py:195
  202.8 31.5 %collective-permute-start.28 = (bf16[64,2304]{1,0:T(8,128)(2,1)}, bf16[64,2304]{1,0:T(8,128)(2,1)S(1)}, u32[]{:S(2)}, u32[]{:S(2)}) collective-permute-start(bf16[64,2304]{1,0:T(8,128)(2,1)} %copy-done.87), channel_id=1, source_target_pairs={{0,4},{2,6},{4,0},{6,2},{1,5},{3,7},{5,1},{7,3},{8,12},{10,14},{12... | collective-permute-start | bytes 884744 | tf_op jit(solution)/shard_map/ppermute | solution.py:147
  280.5 46.4 %collective-permute-start.64 = (bf16[512,1024]{1,0:T(8,128)(2,1)}, bf16[512,1024]{1,0:T(8,128)(2,1)}, u32[]{:S(2)}, u32[]{:S(2)}) collective-permute-start(bf16[512,1024]{1,0:T(8,128)(2,1)} %get-tuple-element.185), channel_id=1, source_target_pairs={{0,1},{1,0},{2,3},{3,2},{4,5},{5,4},{6,7},{7,6},{8,9},{9,8},{10,11... | collective-permute-start | bytes 3145736 | tf_op jit(solution)/shard_map/ppermute | solution.py:201
  284.0 33.3 %collective-permute-start.63 = (bf16[512,512]{1,0:T(8,128)(2,1)}, bf16[512,512]{1,0:T(8,128)(2,1)}, u32[]{:S(2)}, u32[]{:S(2)}) collective-permute-start(bf16[512,512]{1,0:T(8,128)(2,1)} %constant_dynamic-slice_fusion.1), channel_id=1, source_target_pairs={{0,1},{1,0},{2,3},{3,2},{4,5},{5,4},{6,7},{7,6},{8,9},{9,8},{10,11... | collective-permute-start | bytes 1572872 | tf_op jit(solution)/shard_map/ppermute | solution.py:210
  284.5 146.4 %collective-permute-start.71 = (bf16[8,64,2304]{2,1,0:T(8,128)(2,1)}, bf16[8,64,2304]{2,1,0:T(8,128)(2,1)}, u32[]{:S(2)}, u32[]{:S(2)}) collective-permute-start(bf16[8,64,2304]{2,1,0:T(8,128)(2,1)} %bitcast.318), channel_id=1, source_target_pairs={{0,2},{2,0},{4,6},{6,4},{1,3},{3,1},{5,7},{7,5},{8,10},{10,8},{12,... | collective-permute-start | bytes 7077896 | tf_op jit(solution)/shard_map/ppermute | solution.py:147
  284.6 151.2 %collective-permute-start.76 = (bf16[8,64,2304]{2,1,0:T(8,128)(2,1)}, bf16[8,64,2304]{2,1,0:T(8,128)(2,1)}, u32[]{:S(2)}, u32[]{:S(2)}) collective-permute-start(bf16[8,64,2304]{2,1,0:T(8,128)(2,1)} %bitcast.317), channel_id=1, source_target_pairs={{0,2},{2,0},{4,6},{6,4},{1,3},{3,1},{5,7},{7,5},{8,10},{10,8},{12,... | collective-permute-start | bytes 7077896 | tf_op jit(solution)/shard_map/ppermute | solution.py:147
  285.1 154.6 %collective-permute-start.81 = (bf16[8,64,2304]{2,1,0:T(8,128)(2,1)}, bf16[8,64,2304]{2,1,0:T(8,128)(2,1)}, u32[]{:S(2)}, u32[]{:S(2)}) collective-permute-start(bf16[8,64,2304]{2,1,0:T(8,128)(2,1)} %bitcast.316), channel_id=1, source_target_pairs={{0,2},{2,0},{4,6},{6,4},{1,3},{3,1},{5,7},{7,5},{8,10},{10,8},{12,... | collective-permute-start | bytes 7077896 | tf_op jit(solution)/shard_map/ppermute | solution.py:147
  320.4 108.2 %all-to-all-start.2 = ((bf16[16,32,512]{2,1,0:T(8,128)(2,1)}), bf16[16,32,512]{2,1,0:T(8,128)(2,1)}, u32[]{:S(2)}, u32[]{:S(2)}) async-start(bf16[16,32,512]{2,1,0:T(8,128)(2,1)} %bitcast.286), calls=%async_computation.2 | async-start | bytes 1048576 | tf_op jit(solution)/shard_map/all_to_all | solution.py:430
  324.6 235.8 %reduce-scatter.2.cloned.1.call-start = ((), (), s32[]{:S(2)}) async-start(), calls=%async_computation.5 | async-start | bytes 2621440 | tf_op jit(solution)/shard_map/reduce_scatter | solution.py:550
  434.0 37.9 %collective-permute-start.72 = (bf16[4,64,2304]{2,1,0:T(8,128)(2,1)S(1)}, bf16[4,64,2304]{2,1,0:T(8,128)(2,1)S(1)}, u32[]{:S(2)}, u32[]{:S(2)}) collective-permute-start(bf16[4,64,2304]{2,1,0:T(8,128)(2,1)S(1)} %slice.232), channel_id=1, source_target_pairs={{0,4},{2,6},{4,0},{6,2},{1,5},{3,7},{5,1},{7,3},{8,12},{10,14},{12... | collective-permute-start | bytes 3538952 | tf_op jit(solution)/shard_map/ppermute | solution.py:147
  438.1 59.1 %collective-permute-start.77 = (bf16[4,64,2304]{2,1,0:T(8,128)(2,1)S(1)}, bf16[4,64,2304]{2,1,0:T(8,128)(2,1)S(1)}, u32[]{:S(2)}, u32[]{:S(2)}) collective-permute-start(bf16[4,64,2304]{2,1,0:T(8,128)(2,1)S(1)} %slice.238), channel_id=1, source_target_pairs={{0,4},{2,6},{4,0},{6,2},{1,5},{3,7},{5,1},{7,3},{8,12},{10,14},{12... | collective-permute-start | bytes 3538952 | tf_op jit(solution)/shard_map/ppermute | solution.py:147
  442.0 80.2 %collective-permute-start.82 = (bf16[4,64,2304]{2,1,0:T(8,128)(2,1)S(1)}, bf16[4,64,2304]{2,1,0:T(8,128)(2,1)S(1)}, u32[]{:S(2)}, u32[]{:S(2)}) collective-permute-start(bf16[4,64,2304]{2,1,0:T(8,128)(2,1)S(1)} %slice.244), channel_id=1, source_target_pairs={{0,4},{2,6},{4,0},{6,2},{1,5},{3,7},{5,1},{7,3},{8,12},{10,14},{12... | collective-permute-start | bytes 3538952 | tf_op jit(solution)/shard_map/ppermute | solution.py:147
  472.2 51.8 %collective-permute-start.73 = (bf16[64,2304]{1,0:T(8,128)(2,1)S(1)}, bf16[64,2304]{1,0:T(8,128)(2,1)S(1)}, u32[]{:S(2)}, u32[]{:S(2)}) collective-permute-start(bf16[64,2304]{1,0:T(8,128)(2,1)S(1)} %slice_bitcast_fusion.11), channel_id=1, source_target_pairs={{0,8},{8,16},{16,24},{24,0},{1,9},{9,17},{17,25},{25,1},{2,10},{10... | collective-permute-start | bytes 884744 | tf_op jit(solution)/shard_map/ppermute | solution.py:144
  497.5 28.1 %collective-permute-start.78 = (bf16[64,2304]{1,0:T(8,128)(2,1)S(1)}, bf16[64,2304]{1,0:T(8,128)(2,1)S(1)}, u32[]{:S(2)}, u32[]{:S(2)}) collective-permute-start(bf16[64,2304]{1,0:T(8,128)(2,1)S(1)} %slice_bitcast_fusion.7), channel_id=1, source_target_pairs={{0,8},{8,16},{16,24},{24,0},{1,9},{9,17},{17,25},{25,1},{2,10},{10... | collective-permute-start | bytes 884744 | tf_op jit(solution)/shard_map/ppermute | solution.py:144
  547.7 27.8 %collective-permute-start.80 = (bf16[64,2304]{1,0:T(8,128)(2,1)}, bf16[64,2304]{1,0:T(8,128)(2,1)}, u32[]{:S(2)}, u32[]{:S(2)}) collective-permute-start(bf16[64,2304]{1,0:T(8,128)(2,1)} %fusion.47), channel_id=1, source_target_pairs={{0,8},{8,16},{16,24},{24,0},{1,9},{9,17},{17,25},{25,1},{2,10},{10... | collective-permute-start | bytes 884744 | tf_op jit(solution)/shard_map/ppermute | solution.py:144
  582.7 53.6 %collective-permute-start.67 = (bf16[4,64,1536]{2,1,0:T(8,128)(2,1)}, bf16[4,64,1536]{2,1,0:T(8,128)(2,1)}, u32[]{:S(2)}, u32[]{:S(2)}) collective-permute-start(bf16[4,64,1536]{2,1,0:T(8,128)(2,1)} %slice.222), channel_id=1, source_target_pairs={{0,4},{2,6},{4,0},{6,2},{1,5},{3,7},{5,1},{7,3},{8,12},{10,14},{12... | collective-permute-start | bytes 2359304 | tf_op jit(solution)/shard_map/ppermute | solution.py:147
  584.7 54.4 %collective-permute-start.65 = (bf16[512,512]{1,0:T(8,128)(2,1)}, bf16[512,512]{1,0:T(8,128)(2,1)S(1)}, u32[]{:S(2)}, u32[]{:S(2)}) collective-permute-start(bf16[512,512]{1,0:T(8,128)(2,1)} %constant_dynamic-slice_fusion), channel_id=1, source_target_pairs={{0,1},{1,0},{2,3},{3,2},{4,5},{5,4},{6,7},{7,6},{8,9},{9,8},{10,11... | collective-permute-start | bytes 1572872 | tf_op jit(solution)/shard_map/ppermute | solution.py:210
  (166 other events, 1991.2 us)
Sparse Core Ops, SparseCore 0:
  85.6 31.1 all-gather.2
  414.7 42.2 reduce-scatter.1

commit v2 on v1

v2 whole, which is shorter than its diff:
```python
import functools

import jax
import jax.numpy as jnp
from jax import lax
from jax.experimental import pallas as pl
from jax.experimental.pallas import tpu as pltpu
from jax.sharding import PartitionSpec as P

MODEL_WIDTH = 1024
QUERY_HEADS = 16
KEY_VALUE_HEADS = 8
HEAD_SIZE = 64
PACKED_ROW_SLOTS = 2048
QUERY_BLOCK_ROWS = 512

EPSILON = 1e-05
ROPE_THETA = 1000000.0
NEG_FILL = -1e30
BF = jnp.bfloat16
F32 = jnp.float32


def segment_ends(lengths):
    total, ends = lengths[0], []
    for i in range(lengths.shape[0]):
        ends.append(total)
        if i + 1 < lengths.shape[0]:
            total = total + lengths[i + 1]
    return ends


def slot_tables(lengths, slot_ids):
    segment = jnp.zeros_like(slot_ids)
    start = jnp.zeros_like(slot_ids)
    for i, end in enumerate(segment_ends(lengths)):
        passed = (slot_ids >= end).astype(jnp.int32)
        segment = segment + passed
        start = start + passed * lengths[i]
    return (segment, slot_ids - start)


def product(left_arr, right_arr, pattern):
    return jnp.einsum(pattern, left_arr, right_arr, preferred_element_type=F32)


class Grid:
    def __init__(self):
        self.n = lax.axis_size("fsdp")
        self.ctx = lax.axis_size("ctx")
        self.tp = lax.axis_size("tp")
        self.z = lax.axis_index("fsdp")
        self.c = lax.axis_index("ctx")
        self.t = lax.axis_index("tp")

    def ring(self, v):
        return lax.ppermute(v, "fsdp", [(i, (i + 1) % self.n) for i in range(self.n)])

    def flip(self, v, bit):
        return lax.ppermute(v, "ctx", [(i, i ^ bit) for i in range(self.ctx)])

    def order(self):
        return [
            lax.rem(self.z - k + self.n, self.n) * self.ctx + (self.c ^ d)
            for d in range(self.ctx)
            for k in range(self.n)
        ]

    def collect(self, shard):
        have = [shard]
        for _ in range(self.n - 1):
            have.append(self.ring(have[-1]))
        bits = []
        b = self.ctx // 2
        while b:
            bits.append(b)
            b //= 2
        got = {(0, k): v for k, v in enumerate(have)}
        for bit in bits:
            more = {(d | bit, k): self.flip(v, bit) for (d, k), v in got.items()}
            got.update(more)
        return [got[(d, k)] for d in range(self.ctx) for k in range(self.n)]

    def reduce_ctx(self, keep, send):
        total = (keep.astype(F32) + self.flip(send, 1).astype(F32)).astype(BF)
        bit = self.ctx // 2
        stride = keep.shape[0] // 2
        if bit >= 2:
            away = self.flip(total[stride:], bit)
            total = (total[:stride].astype(F32) + away.astype(F32)).astype(BF)
        return total

    def reduce_ring(self, total):
        run = total[1 % self.n]
        for k in range(2, self.n + 1):
            run = self.ring(run).astype(F32) + total[k % self.n].astype(F32)
            if k < self.n:
                run = run.astype(BF)
        return run

    def tp_pair(self, own, other, axis):
        first = jnp.where(self.t == 0, own, other)
        second = jnp.where(self.t == 0, other, own)
        return jnp.concatenate([first, second], axis=axis)

    def tp_gather(self, v):
        if self.tp == 2:
            other = lax.ppermute(v, "tp", [(0, 1), (1, 0)])
            return self.tp_pair(v, other, 1)
        return lax.all_gather(v, "tp", axis=1, tiled=True)

    def tp_sum(self, v):
        if self.tp == 2:
            other = lax.ppermute(v, "tp", [(0, 1), (1, 0)])
            return v.astype(F32) + other.astype(F32)
        return lax.psum(v, "tp").astype(F32)

    def tp_scatter(self, v):
        if self.tp == 2:
            half = v.shape[1] // 2
            own = lax.dynamic_slice_in_dim(v, self.t * half, half, 1)
            away = lax.dynamic_slice_in_dim(v, (1 - self.t) * half, half, 1)
            other = lax.ppermute(away, "tp", [(0, 1), (1, 0)])
            return own.astype(F32) + other.astype(F32)
        return lax.psum_scatter(v, "tp", scatter_dimension=1, tiled=True).astype(F32)

    def tp_parts(self, v):
        if self.tp == 2:
            return v, lax.ppermute(v, "tp", [(0, 1), (1, 0)])
        return lax.psum(v, "tp"), jnp.zeros_like(v)

    def sum_all(self, v):
        for axis, size in (("ctx", self.ctx), ("tp", self.tp), ("fsdp", self.n)):
            bit = 1
            while bit < size:
                v = v + lax.ppermute(v, axis, [(i, i ^ bit) for i in range(size)])
                bit *= 2
        return v


def dot(a, b, ca, cb, precision=None):
    return lax.dot_general(
        a, b, (((ca,), (cb,)), ((), ())), preferred_element_type=F32, precision=precision
    )


def lanes(shape):
    return lax.broadcasted_iota(jnp.int32, shape, 1)


def half_mean(v):
    low = lanes(v.shape) < HEAD_SIZE
    first = jnp.sum(jnp.where(low, v, 0.0), axis=1, keepdims=True)
    second = jnp.sum(jnp.where(low, 0.0, v), axis=1, keepdims=True)
    return jnp.where(low, first, second) * (1.0 / HEAD_SIZE)


def half_swap(v):
    quarter = HEAD_SIZE // 2
    left = pltpu.roll(v, 128 - quarter, 1)
    right = pltpu.roll(v, quarter, 1)
    return jnp.where(lanes(v.shape) % HEAD_SIZE < quarter, left, right)


def row_scale(v):
    return lax.rsqrt(jnp.mean(v * v, axis=1, keepdims=True) + EPSILON)


def norm_back(dn, v, gain):
    scale = row_scale(v)
    unit = v * scale
    scaled = dn * gain
    grad = scale * (scaled - unit * jnp.mean(scaled * unit, axis=1, keepdims=True))
    return grad, jnp.sum(dn * unit, axis=0, keepdims=True)


def qk_forward(raw, gain, cosines, sines, is_value):
    normed = raw * lax.rsqrt(half_mean(raw * raw) + EPSILON) * gain
    turned = normed * cosines + half_swap(normed) * sines
    return jnp.where(is_value, raw, turned)


def qk_backward(grad, raw, gain, cosines, sines, is_value):
    straight = grad * cosines - half_swap(grad) * sines
    scale = lax.rsqrt(half_mean(raw * raw) + EPSILON)
    unit = raw * scale
    scaled = straight * gain
    back = scale * (scaled - unit * half_mean(scaled * unit))
    gain_grad = jnp.sum(straight * unit, axis=0, keepdims=True)
    return jnp.where(is_value, grad, back), gain_grad


def two_heads(v):
    low = lanes(v.shape) < HEAD_SIZE
    zero = jnp.zeros_like(v)
    return jnp.concatenate([jnp.where(low, v, zero), jnp.where(low, zero, v)], axis=0)


def one_row(v):
    rows = v.shape[0] // 2
    return jnp.where(lanes((rows, v.shape[1])) < HEAD_SIZE, v[:rows], v[rows:])


def doubled(ref, rows, column):
    v = ref[rows, column : column + HEAD_SIZE]
    return jnp.concatenate([v, v], axis=1)


def qkv_kernel(q_width, kv_width, pieces, shard_rows, offs, x, gain, head_gain, cosines, sines, *refs):
    sources = refs[:pieces]
    qb, kv, raw, w, sem = refs[pieces:]
    copies = [
        pltpu.make_async_copy(
            sources[i], w.at[pl.ds(pl.multiple_of(offs[i], shard_rows), shard_rows), :], sem.at[i]
        )
        for i in range(pieces)
    ]
    for c in copies:
        c.start()
    v = x[...].astype(F32)
    normed = (v * row_scale(v) * gain[...]).astype(BF)
    for c in copies:
        c.wait()
    total = q_width + 2 * kv_width
    values_from = q_width + kv_width
    for b in range(0, total, 128):
        block = dot(normed, w[:, b : b + 128], 1, 0)
        is_value = lanes(block.shape) + b >= values_from
        done = qk_forward(block, head_gain[:, b : b + 128], cosines[...], sines[...], is_value)
        raw[:, b : b + 128] = block
        if b < q_width:
            qb[:, b : b + 128] = done.astype(BF)
        else:
            kv[:, b - q_width : b - q_width + 128] = done.astype(BF)


def attend_kernel(q_width, kv_width, piece, where, qb, kv, start_col, w, heads, sums, part, acc, total, bias):
    ctx = where[0]
    rows = qb.shape[0]
    q_slot = ctx * piece + lax.broadcasted_iota(jnp.int32, (rows, piece), 0)
    n_pairs = q_width // 128

    def one_piece(p, carry):
        k_slot = p * piece + lanes((rows, piece))
        open_ = (k_slot >= start_col[...]) & (k_slot <= q_slot)
        bias[...] = jnp.where(open_, 0.0, NEG_FILL)
        at = pl.ds(pl.multiple_of(p * piece, piece), piece)
        for g in range(n_pairs):
            q2 = two_heads(qb[:, 128 * g : 128 * g + 128])
            k2 = doubled(kv, at, HEAD_SIZE * g)
            v2 = doubled(kv, at, kv_width + HEAD_SIZE * g)
            s = dot(q2, k2, 1, 1)
            for h in range(2):
                e = jnp.exp(s[h * rows : (h + 1) * rows] * 0.125 + bias[...])
                part_sum = e[:, :128]
                for b in range(128, piece, 128):
                    part_sum = part_sum + e[:, b : b + 128]
                o = dot(e.astype(BF), v2, 1, 0)
                acc[g, h * rows : (h + 1) * rows, :] += o
                total[g, h * rows : (h + 1) * rows, :] += part_sum
        return carry

    acc[...] = jnp.zeros_like(acc)
    total[...] = jnp.zeros_like(total)
    lax.fori_loop(0, ctx + 1, one_piece, 0)
    ones = jnp.ones((8, 128), F32)
    for g in range(n_pairs):
        row_total = jnp.sum(total[g], axis=1, keepdims=True)
        heads[:, 128 * g : 128 * g + 128] = one_row(acc[g] / row_total)
        sums[g] = 1.0 / dot(ones, total[g], 1, 1, lax.Precision.HIGHEST)
    out_from = q_width + 2 * kv_width
    part[...] = dot(heads[...].astype(BF), w[:, out_from:], 1, 1).astype(BF)


def attend_back_kernel(
    q_width, kv_width, piece, where, qb, kv, heads, sums, start_row, w, d_attn,
    dq, dkv, g_out, dob, bias, dq_t, *more
):
    ctx = where[0]
    rows = qb.shape[0]
    n_pairs = q_width // 128
    out_from = q_width + 2 * kv_width
    d = d_attn[...]
    dob[...] = dot(d, w[:, out_from:], 1, 0).astype(BF)
    d_turned = d.astype(F32).T.astype(BF)
    g_out[...] = dot(d_turned, heads[...].astype(BF), 1, 0).astype(BF)
    q_slot = ctx * piece + lanes((piece, rows))
    dkv[...] = jnp.zeros_like(dkv)
    dq_t[...] = jnp.zeros_like(dq_t)
    ones = jnp.ones((8, 128), F32)

    def one_piece(p, carry):
        k_slot = p * piece + lax.broadcasted_iota(jnp.int32, (piece, rows), 0)
        open_ = (k_slot >= start_row[...]) & (k_slot <= q_slot)
        bias[...] = jnp.where(open_, 0.0, NEG_FILL)
        at = pl.ds(pl.multiple_of(p * piece, piece), piece)
        for g in range(n_pairs):
            block = slice(128 * g, 128 * g + 128)
            q2 = two_heads(qb[:, block])
            do = dob[:, block]
            do2 = two_heads(do)
            delta = dot(
                ones, two_heads(do.astype(F32) * heads[:, block]), 1, 1, lax.Precision.HIGHEST
            )
            k2 = doubled(kv, at, HEAD_SIZE * g)
            v2 = doubled(kv, at, kv_width + HEAD_SIZE * g)
            k_t = k2.astype(F32).T.astype(BF)
            s = dot(k2, q2, 1, 1)
            dp = dot(v2, do2, 1, 1)
            dk = jnp.zeros((piece, 128), F32)
            dv = jnp.zeros((piece, 128), F32)
            for h in range(2):
                part = slice(h * rows, (h + 1) * rows)
                pe = jnp.exp(s[:, part] * 0.125 + bias[...]) * sums[g, 0:1, part]
                ds = (pe * (dp[:, part] - delta[0:1, part])).astype(BF)
                dv = dv + dot(pe.astype(BF), do2[part], 1, 0)
                dk = dk + dot(ds, q2[part], 1, 0)
                dq_t[g, :, part] += dot(k_t, ds, 1, 0)
            dk = dk[:, :HEAD_SIZE] + dk[:, HEAD_SIZE:]
            dv = dv[:, :HEAD_SIZE] + dv[:, HEAD_SIZE:]
            c = HEAD_SIZE * g
            dkv[at, c : c + HEAD_SIZE] = (dk * 0.125).astype(BF)
            dkv[at, kv_width + c : kv_width + c + HEAD_SIZE] = dv.astype(BF)
        return carry

    lax.fori_loop(0, ctx + 1, one_piece, 0)
    for g in range(n_pairs):
        dq[:, 128 * g : 128 * g + 128] = one_row(dq_t[g].T) * 0.125


def qkv_back_kernel(
    q_width, kv_width, pieces, shard_rows, offs, x, gain, head_gain, cosines, sines, raw, w, dq, dkv,
    g_out, dx, d_gain, d_head_gain, keep, send, d_all, turned, g
):
    total = q_width + 2 * kv_width
    values_from = q_width + kv_width
    for b in range(0, total, 128):
        grad = dq[:, b : b + 128] if b < q_width else dkv[:, b - q_width : b - q_width + 128]
        is_value = lanes(grad.shape) + b >= values_from
        back, gain_grad = qk_backward(
            grad, raw[:, b : b + 128], head_gain[:, b : b + 128], cosines[...], sines[...], is_value
        )
        d_all[:, b : b + 128] = back.astype(BF)
        d_head_gain[:, b : b + 128] = gain_grad
    v = x[...].astype(F32)
    turned[...] = (v * row_scale(v) * gain[...]).T.astype(BF)
    g[:, :total] = dot(turned[...], d_all[...], 1, 0).astype(BF)
    g[:, total:] = g_out[...]
    half = pieces // 2
    for i in range(pieces):
        at = pl.ds(pl.multiple_of(offs[pieces + i], shard_rows), shard_rows)
        to = keep if i < half else send
        row = (i % half) * shard_rows
        to[row : row + shard_rows, :] = g[at, :]
    dn = dot(d_all[...], w[:, :total], 1, 1)
    grad, gain_sum = norm_back(dn, v, gain[...])
    dx[...] = grad.astype(BF)
    d_gain[...] = gain_sum


def ffn_kernel(pieces, shard_rows, tile, group, offs, x, att_a, att_b, dy, gain, *refs):
    wg_in = refs[:pieces]
    wu_in = refs[pieces : 2 * pieces]
    wd_in = refs[2 * pieces : 3 * pieces]
    ffn, dmid, dgain, squares, nb, hid, dgt, dup = refs[3 * pieces : 3 * pieces + 8]
    (wg, wu, wd, mid, ffn_acc, dn_acc, sem) = refs[3 * pieces + 8 :]
    step = pl.program_id(0)
    steps = pl.num_programs(0)
    n_groups = wg.shape[1] // group
    per_group = group // tile

    def copies(g):
        out = []
        cols = pl.ds(g * group, group)
        for m, (src, dst) in enumerate(((wg_in, wg), (wu_in, wu), (wd_in, wd))):
            for i in range(pieces):
                rows = pl.ds(pl.multiple_of(offs[i], shard_rows), shard_rows)
                out.append(
                    pltpu.make_async_copy(src[i].at[:, cols], dst.at[rows, cols], sem.at[g, m, i])
                )
        return out

    @pl.when(step == 0)
    def _():
        for g in range(n_groups):
            for c in copies(g):
                c.start()
        v = x[...].astype(F32)
        att = att_a[...].astype(F32) + att_b[...].astype(F32)
        squares[0:1, :] = jnp.sum(v * v, axis=0, keepdims=True)
        squares[1:2, :] = jnp.sum(att * att, axis=0, keepdims=True)
        mid[...] = (v + att).astype(BF)
        v = mid[...].astype(F32)
        nb[...] = (v * row_scale(v) * gain[...]).astype(BF)
        ffn_acc[...] = jnp.zeros_like(ffn_acc)
        dn_acc[...] = jnp.zeros_like(dn_acc)

    for g in range(n_groups):

        @pl.when(step == g * per_group)
        def _(g=g):
            for c in copies(g):
                c.wait()

    cols = pl.ds(pl.multiple_of(step * tile, tile), tile)
    w_gate = wg[:, cols]
    w_up = wu[:, cols]
    w_down = wd[:, cols]
    normed = nb[...]
    dyb = dy[...]
    gate = dot(normed, w_gate, 1, 0)
    up = dot(normed, w_up, 1, 0)
    d_hidden = dot(dyb, w_down, 1, 0)
    sig = 1.0 / (1.0 + jnp.exp(-gate))
    silu = gate * sig
    hidden = (silu * up).astype(BF)
    d_gate = (d_hidden * up * (sig * (1.0 + gate * (1.0 - sig)))).astype(BF)
    d_up = (d_hidden * silu).astype(BF)
    hid[...] = hidden
    dgt[...] = d_gate
    dup[...] = d_up
    ffn_acc[...] += dot(hidden, w_down, 1, 1)
    dn_acc[...] += dot(d_gate, w_gate, 1, 1) + dot(d_up, w_up, 1, 1)

    @pl.when(step == steps - 1)
    def _():
        grad, gain_sum = norm_back(dn_acc[...], mid[...].astype(F32), gain[...])
        dgain[...] = gain_sum
        dmid[...] = grad.astype(BF)
        ffn[...] = ffn_acc[...].astype(BF)


def weight_grad_kernel(pieces, shard_rows, offs, left, right, keep, send, turn, ordered):
    @pl.when(pl.program_id(0) == 0)
    def _():
        turn[...] = left[...].astype(F32).T.astype(BF)
        for i in range(pieces):
            at = pl.ds(pl.multiple_of(offs[pieces + i], shard_rows), shard_rows)
            ordered[i * shard_rows : (i + 1) * shard_rows, :] = turn[at, :]

    half = ordered.shape[0] // 2
    keep[...] = dot(ordered[:half, :], right[...], 1, 0).astype(BF)
    send[...] = dot(ordered[half:, :], right[...], 1, 0).astype(BF)


def shape(s, t):
    return jax.ShapeDtypeStruct(s, t)


VMEM_LIMIT = pltpu.CompilerParams(vmem_limit_bytes=58 * 2**20)
ANYWHERE = pl.BlockSpec(memory_space=pl.ANY)


def once(body, scalars, n_in, n_any, outs, scratch, flops):
    vm = pl.BlockSpec(memory_space=pltpu.VMEM)

    def call(scalar, *operands):
        return pl.pallas_call(
            body,
            grid_spec=pltpu.PrefetchScalarGridSpec(
                num_scalar_prefetch=scalars,
                grid=(1,),
                in_specs=[vm] * n_in + [ANYWHERE] * n_any,
                out_specs=[vm] * len(outs),
                scratch_shapes=scratch,
            ),
            out_shape=outs,
            compiler_params=VMEM_LIMIT,
            cost_estimate=pl.CostEstimate(flops=flops, bytes_accessed=8 * 2**20, transcendentals=0),
        )(scalar, *operands)

    return call


def ffn_pass(x, att_a, att_b, dy, gain, gate_p, up_p, down_p, offsets):
    rows, width = x.shape
    pieces = len(gate_p)
    shard_rows, ff = gate_p[0].shape
    tile = 256 if ff % 256 == 0 else 128
    group = 3 * tile if ff % (3 * tile) == 0 else tile
    whole = lambda shape: pl.BlockSpec(shape, lambda s, o: (0, 0))
    column = pl.BlockSpec((rows, tile), lambda s, o: (0, s))
    return pl.pallas_call(
        functools.partial(ffn_kernel, pieces, shard_rows, tile, group),
        grid_spec=pltpu.PrefetchScalarGridSpec(
            num_scalar_prefetch=1,
            grid=(ff // tile,),
            in_specs=[whole((rows, width))] * 4 + [whole((1, width))] + [ANYWHERE] * (3 * pieces),
            out_specs=[whole((rows, width))] * 2
            + [whole((1, width)), whole((2, width)), whole((rows, width))]
            + [column] * 3,
            scratch_shapes=[
                pltpu.VMEM((width, ff), BF),
                pltpu.VMEM((width, ff), BF),
                pltpu.VMEM((width, ff), BF),
                pltpu.VMEM((rows, width), BF),
                pltpu.VMEM((rows, width), F32),
                pltpu.VMEM((rows, width), F32),
                pltpu.SemaphoreType.DMA((ff // group, 3, pieces)),
            ],
        ),
        out_shape=[shape((rows, width), BF)] * 2
        + [shape((1, width), F32), shape((2, width), F32), shape((rows, width), BF)]
        + [shape((rows, ff), BF)] * 3,
        compiler_params=VMEM_LIMIT,
        cost_estimate=pl.CostEstimate(
            flops=12 * rows * width * ff, bytes_accessed=6 * width * ff, transcendentals=rows * ff
        ),
    )(offsets, x, att_a, att_b, dy, gain, *gate_p, *up_p, *down_p)


def weight_grad(left, right, offsets, pieces):
    rows, width = left.shape
    ff = right.shape[1]
    tile = 256 if ff % 256 == 0 else 128
    half = width // 2
    column = pl.BlockSpec((half, tile), lambda s, o: (0, s))
    return pl.pallas_call(
        functools.partial(weight_grad_kernel, pieces, width // pieces),
        grid_spec=pltpu.PrefetchScalarGridSpec(
            num_scalar_prefetch=1,
            grid=(ff // tile,),
            in_specs=[
                pl.BlockSpec((rows, width), lambda s, o: (0, 0)),
                pl.BlockSpec((rows, tile), lambda s, o: (0, s)),
            ],
            out_specs=[column, column],
            scratch_shapes=[pltpu.VMEM((width, rows), BF), pltpu.VMEM((width, rows), BF)],
        ),
        out_shape=[shape((half, ff), BF)] * 2,
        compiler_params=VMEM_LIMIT,
        cost_estimate=pl.CostEstimate(
            flops=2 * rows * width * ff, bytes_accessed=2 * width * ff, transcendentals=0
        ),
    )(offsets, left, right)


def pad_columns(v, to):
    return v if v.shape[1] == to else jnp.pad(v, ((0, 0), (0, to - v.shape[1])))


def one_hot(rows, columns):
    return (rows == columns).astype(BF)


def local(
    tokens,
    cotangent,
    slot_of,
    lengths,
    w_query,
    key_weight,
    value_weight,
    w_out,
    w_gate,
    w_up,
    w_down,
    gain_attn,
    gain_ffn,
    gain_query,
    gain_key,
):
    grid = Grid()
    stream_len = tokens.shape[0]
    feat_len = tokens.shape[1]
    local_len = PACKED_ROW_SLOTS // grid.ctx
    row_count = stream_len // local_len
    groups = grid.n * grid.ctx
    share = stream_len // groups
    q_heads = QUERY_HEADS // grid.tp
    key_value_heads = KEY_VALUE_HEADS // grid.tp
    query_group_width = QUERY_HEADS // KEY_VALUE_HEADS
    q_width = q_heads * HEAD_SIZE
    kv_width = key_value_heads * HEAD_SIZE
    flat_len = row_count * local_len
    row_len = PACKED_ROW_SLOTS
    me = grid.z * grid.ctx + grid.c
    both = ("fsdp", "ctx")

    def home(slots):
        row, place = slots // row_len, slots % row_len
        return (
            row // row_count * grid.ctx + place // local_len,
            row % row_count * local_len + place % local_len,
        )

    my_slots = lax.dynamic_slice_in_dim(slot_of, me * stream_len, stream_len, 0)
    my_target = home(my_slots)[0]
    ahead = (my_target[:, None] == my_target[None, :]) & (my_slots[None, :] < my_slots[:, None])
    send_place = my_target * share + jnp.sum(ahead.astype(jnp.int32), axis=1)
    line = jnp.arange(stream_len, dtype=jnp.int32)
    send_pick = one_hot(line[:, None], send_place[None, :])
    all_dev, all_local = home(slot_of)
    low = 32
    high = flat_len // low
    sender = (jnp.arange(slot_of.shape[0], dtype=jnp.int32) // stream_len).astype(F32)
    mine = (all_dev == me)[None, :] & (
        (all_local // low)[None, :] == jnp.arange(high, dtype=jnp.int32)[:, None]
    )
    left = jnp.where(mine, sender[None, :], 0.0).astype(BF)
    right = one_hot((all_local % low)[:, None], jnp.arange(low, dtype=jnp.int32)[None, :])
    source = product(left, right, "ht,tl->hl").reshape(flat_len).astype(jnp.int32)
    slot_line = jnp.arange(flat_len, dtype=jnp.int32)
    before = (source[:, None] == source[None, :]) & (slot_line[None, :] < slot_line[:, None])
    arrival = source * share + jnp.sum(before.astype(jnp.int32), axis=1)
    take_pick = one_hot(arrival[:, None], line[None, :])

    def spread(v):
        sent = product(send_pick, v, "pt,tf->pf").astype(BF)
        got = lax.all_to_all(sent, both, split_axis=0, concat_axis=0, tiled=True)
        return product(take_pick, got, "ja,af->jf").astype(BF)

    def bring_back(v):
        sent = product(take_pick, v, "ja,jf->af").astype(BF)
        got = lax.all_to_all(sent, both, split_axis=0, concat_axis=0, tiled=True)
        return product(send_pick, got, "pt,pf->tf").astype(BF)

    ff = w_gate.shape[1]
    ff_pad = -(-ff // 128) * 128
    attn_shard = jnp.concatenate([w_query, key_weight, value_weight, w_out.T], axis=1)
    attn_pieces = grid.collect(attn_shard)
    gate_p, up_p, down_p = (
        grid.collect(pad_columns(v, ff_pad)) for v in (w_gate, w_up, w_down.T)
    )
    shard_rows = w_gate.shape[0]
    order = grid.order()
    grad_order = [d for d in range(0, grid.ctx, 2)] + [d for d in range(1, grid.ctx, 2)]
    grad_order = [order[d * grid.n + k] for d in grad_order for k in range(grid.n)]
    offsets = (jnp.stack(order + grad_order) * shard_rows).astype(jnp.int32)

    packed_tok = spread(tokens)
    x_full = grid.tp_gather(packed_tok)
    packed_cot = spread(cotangent)
    dy_full = grid.tp_gather(packed_cot)
    own_slots = grid.c * local_len + jnp.arange(local_len, dtype=jnp.int32)
    position = slot_tables(lengths[0], own_slots)[1]
    start = own_slots - position
    frequency = ROPE_THETA ** (-jnp.arange(0, HEAD_SIZE, 2).astype(F32) / HEAD_SIZE)
    angles = position.astype(F32)[:, None] * frequency[None, :]
    cosines = jnp.tile(jnp.cos(angles), (1, 4))
    sin = jnp.sin(angles)
    sines = jnp.tile(jnp.concatenate([-sin, sin], axis=1), (1, 2))
    head_gain = jnp.concatenate(
        [
            jnp.tile(gain_query, q_heads),
            jnp.tile(gain_key, key_value_heads),
            jnp.ones((kv_width,), F32),
        ]
    )[None, :]
    place = grid.c.astype(jnp.int32)[None]
    pieces = groups
    qkv_width = q_width + 2 * kv_width
    attn_width = attn_shard.shape[1]
    n_pairs = q_width // 128
    rows = flat_len

    qb, kv, raw, attn_w = once(
        functools.partial(qkv_kernel, q_width, kv_width, pieces, shard_rows),
        1,
        5,
        pieces,
        [
            shape((rows, q_width), BF),
            shape((rows, 2 * kv_width), BF),
            shape((rows, qkv_width), F32),
            shape((MODEL_WIDTH, attn_width), BF),
        ],
        [pltpu.SemaphoreType.DMA((pieces,))],
        2 * rows * MODEL_WIDTH * qkv_width,
    )(offsets, x_full, gain_attn[None, :], head_gain, cosines, sines, *attn_pieces)
    row_kv = lax.all_gather(kv, "ctx", axis=0, tiled=True)
    attn_flops = 4 * 2 * rows * row_len * q_width
    heads, sums, attn_part = once(
        functools.partial(attend_kernel, q_width, kv_width, local_len),
        1,
        4,
        0,
        [
            shape((rows, q_width), F32),
            shape((n_pairs, 8, 2 * rows), F32),
            shape((rows, MODEL_WIDTH), BF),
        ],
        [
            pltpu.VMEM((n_pairs, 2 * rows, 128), F32),
            pltpu.VMEM((n_pairs, 2 * rows, 128), F32),
            pltpu.VMEM((rows, local_len), F32),
        ],
        attn_flops,
    )(place, qb, row_kv, start[:, None], attn_w)
    attn_a, attn_b = grid.tp_parts(attn_part)

    own_features = lambda v: lax.dynamic_slice_in_dim(v, grid.t * feat_len, feat_len, 1)
    middle_own = (
        packed_tok.astype(F32)
        + own_features(attn_a).astype(F32)
        + own_features(attn_b).astype(F32)
    )
    ffn_part, d_mid_part, d_gain_ffn, squares, normed_two, hidden, d_gate, d_up = ffn_pass(
        x_full, attn_a, attn_b, dy_full, gain_ffn[None, :], gate_p, up_p, down_p, offsets
    )
    d_middle_full = dy_full.astype(F32) + grid.tp_sum(d_mid_part)
    d_middle = own_features(d_middle_full)
    d_attn = d_middle_full.astype(BF)

    def reduce_weight(pair):
        keep, send = pair
        blocks = (keep.shape[0] // shard_rows, shard_rows, keep.shape[1])
        return grid.reduce_ring(grid.reduce_ctx(keep.reshape(blocks), send.reshape(blocks)))

    sum_down = reduce_weight(weight_grad(dy_full, hidden, offsets, pieces))[:, :ff].T
    sum_gate = reduce_weight(weight_grad(normed_two, d_gate, offsets, pieces))[:, :ff]
    sum_up = reduce_weight(weight_grad(normed_two, d_up, offsets, pieces))[:, :ff]
    ffn_out = grid.tp_scatter(ffn_part)

    dq, dkv, g_out = once(
        functools.partial(attend_back_kernel, q_width, kv_width, local_len),
        1,
        7,
        0,
        [
            shape((rows, q_width), F32),
            shape((row_len, 2 * kv_width), BF),
            shape((MODEL_WIDTH, q_width), BF),
        ],
        [
            pltpu.VMEM((rows, q_width), BF),
            pltpu.VMEM((local_len, rows), F32),
            pltpu.VMEM((n_pairs, 128, 2 * rows), F32),
        ],
        3 * attn_flops,
    )(place, qb, row_kv, heads, sums, start[None, :], attn_w, d_attn)
    own_kv = lax.psum_scatter(dkv, "ctx", scatter_dimension=0, tiled=True).astype(F32)
    own_kv = jnp.concatenate(
        [own_kv[:, :kv_width], own_kv[:, kv_width:].astype(BF).astype(F32)], axis=1
    )
    d_x_part, d_gain_attn, d_head_gain, keep, send = once(
        functools.partial(qkv_back_kernel, q_width, kv_width, pieces, shard_rows),
        1,
        10,
        0,
        [
            shape((rows, MODEL_WIDTH), BF),
            shape((1, MODEL_WIDTH), F32),
            shape((1, qkv_width), F32),
            shape((MODEL_WIDTH // 2, attn_width), BF),
            shape((MODEL_WIDTH // 2, attn_width), BF),
        ],
        [
            pltpu.VMEM((rows, qkv_width), BF),
            pltpu.VMEM((MODEL_WIDTH, rows), BF),
            pltpu.VMEM((MODEL_WIDTH, attn_width), BF),
        ],
        4 * rows * MODEL_WIDTH * qkv_width,
    )(
        offsets, x_full, gain_attn[None, :], head_gain, cosines, sines, raw, attn_w, dq, own_kv, g_out
    )
    d_x = grid.tp_scatter(d_x_part)
    grad_packed = (d_middle + d_x).astype(BF)
    output_packed = (middle_own + ffn_out).astype(BF)
    sum_attn = reduce_weight((keep, send))
    a, b, c = q_width, q_width + kv_width, q_width + 2 * kv_width

    per_head = d_head_gain[0].reshape(-1, HEAD_SIZE)
    d_gain_q = jnp.sum(per_head[:q_heads], axis=0)
    d_gain_k = jnp.sum(per_head[q_heads : q_heads + key_value_heads], axis=0)
    sums_of_squares = jnp.concatenate(
        [jnp.sum(squares, axis=1) / grid.tp, jnp.sum(ffn_out * ffn_out)[None]]
    )
    small = jnp.concatenate([d_gain_attn[0], d_gain_ffn[0], d_gain_q, d_gain_k, sums_of_squares])
    small = grid.sum_all(small)
    w, h = MODEL_WIDTH, HEAD_SIZE
    gain_a, gain_f = small[:w], small[w : 2 * w]
    gain_qs, gain_ks = small[2 * w : 2 * w + h], small[2 * w + h : 2 * w + 2 * h]
    entry_count = flat_len * groups * MODEL_WIDTH
    rms_stats = jnp.sqrt(small[2 * w + 2 * h :] / entry_count)
    output = bring_back(output_packed)
    grad_tokens = bring_back(grad_packed)
    return (
        output,
        grad_tokens,
        sum_attn[:, :a],
        sum_attn[:, a:b],
        sum_attn[:, b:c],
        sum_attn[:, c:].T,
        sum_gate,
        sum_up,
        sum_down,
        gain_a,
        gain_f,
        gain_qs,
        gain_ks,
        rms_stats,
    )


def solution(mesh):
    row = P(("fsdp", "ctx"), "tp")
    column = P("tp", ("fsdp", "ctx"))
    in_specs = (row, row, P(), P("fsdp", None), row, row, row, column, row, row, column) + (P(),) * 4
    out_specs = (row, row, row, row, row, column, row, row, column) + (P(),) * 5
    return jax.shard_map(local, mesh=mesh, in_specs=in_specs, out_specs=out_specs, check_vma=False)
```

time: 691 us -> 557 us (0.81)
  matrix products: 115 us -> 11.5 us
  Pallas kernels: 35.7 us -> 105 us
  starting transfers between devices: 81.4 us -> 136 us
  other arithmetic: 92 us -> 37.7 us
  blocking collectives: 46.7 us -> 0 us
  local copies, waits for them, and re-layouts: 50.1 us -> 14.5 us
  waiting for transfers between devices: 243 us -> 225 us
    dot_general x23 -> x9, matrix products: 115 us -> 11.5 us  [product(): return jnp.einsum(pattern, left_arr, right_arr, preferred_element_type=F32)]
    pallas_call x0 -> x7, Pallas kernels: none -> 77.1 us  [the longest x4 46.6 us: call(): pl.pallas_call(body, grid_spec=pltpu.PrefetchScalarGridSpec(num_scalar_pr...]
    psum x1 -> x0, blocking collectives: 46.7 us -> none  [local(): small = lax.psum(small, ('fsdp', 'ctx', 'tp'))]
    ppermute x56, starting transfers between devices: 28.6 us -> 61.3 us  [flip(): return lax.ppermute(v, 'ctx', [(i, i ^ bit) for i in range(self.ctx)])]
    ppermute x2, waiting for transfers between devices: 30 us -> 0.01 us  [tp_scatter(): other = lax.ppermute(away, 'tp', [(0, 1), (1, 0)])]
    unnamed x232 -> x122, local copies, waits for them, and re-layouts: 30.8 us -> 3.28 us
    convert_element_type x4 -> x1, other arithmetic: 30.1 us -> 3.12 us  [local(): d_attn = d_middle_full.astype(BF)]
    ppermute x56, waiting for transfers between devices: 115 us -> 138 us  [flip(): return lax.ppermute(v, 'ctx', [(i, i ^ bit) for i in range(self.ctx)])]
  transfers between devices with their start and end apart: 92 -> 97, of which waited for: 27 -> 33; matrix products, arithmetic and copies ran while one was open for 35% -> 10% of each run, Pallas kernels for 0% -> 12%
where the time goes in v2:
time: 557 us; the launch traced here: 547 us
  waiting for transfers between devices  225 us (40%)
  starting transfers between devices  136 us (24%)
  Pallas kernels  105 us (19%)
  other arithmetic  37.7 us (7%)
  between operations  17.4 us (3%)
  local copies, waits for them, and re-layouts  14.5 us (3%)
  matrix products  11.5 us (2%)
    ppermute x56, waiting for transfers between devices, flip(): return lax.ppermute(v, 'ctx', [(i, i ^ bit) for i in range(self.ctx)])  138 us
    ppermute x56, starting transfers between devices, flip(): return lax.ppermute(v, 'ctx', [(i, i ^ bit) for i in range(self.ctx)])  61.3 us
    ppermute x24, waiting for transfers between devices, ring(): lax.ppermute(v, 'fsdp', [(i, (i + 1) % self.n) for i in range(self.n)])  51.8 us
    pallas_call x4, Pallas kernels, call(): pl.pallas_call(body, grid_spec=pltpu.PrefetchScalarGridSpec(num_scalar_pr...  46.6 us
    pallas_call x3, Pallas kernels, weight_grad(): pl.pallas_call(functools.partial(weight_grad_kernel, pieces, width // pie...  30.5 us
    pallas_call x1, Pallas kernels, ffn_pass(): pl.pallas_call(functools.partial(ffn_kernel, pieces, shard_rows, tile, gr...  28.2 us
    ppermute x24, starting transfers between devices, ring(): lax.ppermute(v, 'fsdp', [(i, (i + 1) % self.n) for i in range(self.n)])  22.1 us
    ppermute x2, waiting for transfers between devices, tp_gather(): other = lax.ppermute(v, 'tp', [(0, 1), (1, 0)])  19.7 us
  transfers between devices with their start and end apart: 97, of which 33 were waited for; matrix products, arithmetic and copies ran while one was open for 10% of the time, Pallas kernels for 12%

profile of v2, /device:TPU:0, one launch (start us, length us, event | category | flops | bytes accessed | tf_op | source)
XLA Modules:
  0.0 547.2 jit_solution(16625370664331225230)
XLA Ops:
  27.4 12.0 %all-to-all-done = bf16[16,32,512]{2,1,0:T(8,128)(2,1)S(1)} async-done(((bf16[16,32,512]{2,1,0:T(8,128)(2,1)}), bf16[16,32,512]{2,1,0:T(8,128)(2,1)S(1)}, u32[]{:S(2)}, u32[]{:S(2)}) %all-to-all-start) | async-done | bytes 524320 | tf_op jit(solution)/shard_map/all_to_all | solution.py:610
  67.7 9.1 %shard_map.254 = (bf16[512,512]{1,0:T(8,128)(2,1)}, bf16[512,512]{1,0:T(8,128)(2,1)}, f32[512,1024]{1,0:T(8,128)}, bf16[1024,1536]{1,0:T(8,128)(2,1)}) custom-call(s32[32]{0:T(128)} %broadcast_multiply_fusion.1.offs, bf16[512,1024]{1,0:T(8,128)(2,1)} %pad_maximum_fusion.x, f32[1,1024]{1,0:T(1,128)} %bitcast.141, f32[1,1024]{1,0:T(1,128)} %bitcast.139, ...), custom_call_target="tpu_custom_call" | custom-call | flops 1073741824 | bytes 8388608 | tf_op jit(solution)/shard_map/pallas_call | solution.py:458
  79.0 8.2 %collective-permute-done.55.refs_40_ = bf16[64,2304]{1,0:T(8,128)(2,1)S(1)} collective-permute-done((bf16[64,2304]{1,0:T(8,128)(2,1)S(1)}, bf16[64,2304]{1,0:T(8,128)(2,1)S(1)}, u32[]{:S(2)}, u32[]{:S(2)}) %collective-permute-start.55) | collective-permute-done | bytes 294944 | tf_op jit(solution)/shard_map/ppermute | solution.py:60
  96.1 7.6 %collective-permute-done.25.refs_8_ = bf16[64,2304]{1,0:T(8,128)(2,1)S(1)} collective-permute-done((bf16[64,2304]{1,0:T(8,128)(2,1)S(1)}, bf16[64,2304]{1,0:T(8,128)(2,1)S(1)}, u32[]{:S(2)}, u32[]{:S(2)}) %collective-permute-start.25) | collective-permute-done | bytes 294944 | tf_op jit(solution)/shard_map/ppermute | solution.py:60
  148.5 7.7 %collective-permute-done.27.refs_10_ = bf16[64,2304]{1,0:T(8,128)(2,1)} collective-permute-done((bf16[64,2304]{1,0:T(8,128)(2,1)}, bf16[64,2304]{1,0:T(8,128)(2,1)}, u32[]{:S(2)}, u32[]{:S(2)}) %collective-permute-start.27) | collective-permute-done | bytes 294944 | tf_op jit(solution)/shard_map/ppermute | solution.py:60
  162.3 9.5 %shard_map.255 = (f32[512,512]{1,0:T(8,128)}, f32[4,8,1024]{2,1,0:T(8,128)}, bf16[512,1024]{1,0:T(8,128)(2,1)}) custom-call(s32[1]{0:T(128)} %bitcast.2.where, bf16[512,512]{1,0:T(8,128)(2,1)} %get-tuple-element.43.qb, bf16[2048,512]{1,0:T(8,128)(2,1)} %all-gather.2.cloned.1.call-done.kv, s32[512,1]{1,0:T(8,128)} %select_add_fusion.start_col, ...), custom_call_target="tpu_custom_call" | custom-call | flops 4294967296 | bytes 8388608 | tf_op jit(solution)/shard_map/pallas_call | solution.py:458
  175.2 6.5 %collective-permute-start.28 = (bf16[64,2304]{1,0:T(8,128)(2,1)}, bf16[64,2304]{1,0:T(8,128)(2,1)}, u32[]{:S(2)}, u32[]{:S(2)}) collective-permute-start(bf16[64,2304]{1,0:T(8,128)(2,1)} %collective-permute-done.20.refs_3_), channel_id=1, source_target_pairs={{0,4},{2,6},{4,0},{6,2},{1,5},{3,7},{5,1},{7,3},{8,12},{10,14},{12... | collective-permute-start | bytes 884744 | tf_op jit(solution)/shard_map/ppermute | solution.py:60
  198.8 19.7 %collective-permute-done.17 = bf16[512,512]{1,0:T(8,128)(2,1)S(1)} collective-permute-done((bf16[512,512]{1,0:T(8,128)(2,1)S(1)}, bf16[512,512]{1,0:T(8,128)(2,1)S(1)}, u32[]{:S(2)}, u32[]{:S(2)}) %collective-permute-start.17) | collective-permute-done | bytes 524320 | tf_op jit(solution)/shard_map/ppermute | solution.py:108
  221.1 28.2 %shard_map.256 = (bf16[512,1024]{1,0:T(8,128)(2,1)}, bf16[512,1024]{1,0:T(8,128)(2,1)}, f32[1,1024]{1,0:T(1,128)}, f32[2,1024]{1,0:T(2,128)}, bf16[512,1024]{1,0...) custom-call(s32[32]{0:T(128)} %broadcast_multiply_fusion.1.offs, ...), custom_call_target="tpu_custom_call" | custom-call | flops 14495514624 | bytes 14155776 | tf_op jit(solution)/shard_map/pallas_call | solution.py:483
  253.2 10.1 %shard_map.261 = (bf16[512,2304]{1,0:T(8,128)(2,1)}, bf16[512,2304]{1,0:T(8,128)(2,1)}) custom-call(s32[32]{0:T(128)} %broadcast_multiply_fusion.1.offs, bf16[512,1024]{1,0:T(8,128)(2,1)} %pad_maximum_fusion.1.dy.left, bf16[512,2304]{1,0:T(8,128)(2,1)} %get-tuple-element.65.right), custom_call_target="tpu_custom_call" | custom-call | flops 2415919104 | bytes 4718592 | tf_op jit(solution)/shard_map/pallas_call | solution.py:518
  263.3 10.1 %shard_map.260 = (bf16[512,2304]{1,0:T(8,128)(2,1)}, bf16[512,2304]{1,0:T(8,128)(2,1)}) custom-call(s32[32]{0:T(128)} %broadcast_multiply_fusion.1.offs, bf16[512,1024]{1,0:T(8,128)(2,1)} %get-tuple-element.58.left, bf16[512,2304]{1,0:T(8,128)(2,1)} %get-tuple-element.62.right), custom_call_target="tpu_custom_call" | custom-call | flops 2415919104 | bytes 4718592 | tf_op jit(solution)/shard_map/pallas_call | solution.py:518
  274.0 10.2 %shard_map.259 = (bf16[512,2304]{1,0:T(8,128)(2,1)}, bf16[512,2304]{1,0:T(8,128)(2,1)}) custom-call(s32[32]{0:T(128)} %broadcast_multiply_fusion.1.offs, bf16[512,1024]{1,0:T(8,128)(2,1)} %get-tuple-element.58.left, bf16[512,2304]{1,0:T(8,128)(2,1)} %get-tuple-element.59.right), custom_call_target="tpu_custom_call" | custom-call | flops 2415919104 | bytes 4718592 | tf_op jit(solution)/shard_map/pallas_call | solution.py:518
  291.4 10.2 %reduce-scatter.2.cloned.1.call-start = ((), (), s32[]{:S(2)}) async-start(), calls=%async_computation.6 | async-start | bytes 2621440 | tf_op jit(solution)/shard_map/reduce_scatter | solution.py:732
  305.6 14.4 %shard_map.257 = (f32[512,512]{1,0:T(8,128)}, bf16[2048,512]{1,0:T(8,128)(2,1)}, bf16[1024,512]{1,0:T(8,128)(2,1)}) custom-call(s32[1]{0:T(128)} %bitcast.2.where, bf16[512,512]{1,0:T(8,128)(2,1)} %get-tuple-element.43.qb, bf16[2048,512]{1,0:T(8,128)(2,1)} %all-gather.2.cloned.1.call-done.kv, f32[512,512]{1,0:T(8,128)} %get-tuple-element.50.heads, ...), custom_call_target="tpu_custom_call" | custom-call | flops 12884901888 | bytes 8388608 | tf_op jit(solution)/shard_map/pallas_call | solution.py:458
  325.4 17.1 %collective-permute-start.77 = (bf16[4,64,2304]{2,1,0:T(8,128)(2,1)S(1)}, bf16[4,64,2304]{2,1,0:T(8,128)(2,1)S(1)}, u32[]{:S(2)}, u32[]{:S(2)}) collective-permute-start(bf16[4,64,2304]{2,1,0:T(8,128)(2,1)S(1)} %slice.188), channel_id=1, source_target_pairs={{0,4},{2,6},{4,0},{6,2},{1,5},{3,7},{5,1},{7,3},{8,12},{10,14},{12... | collective-permute-start | bytes 3538952 | tf_op jit(solution)/shard_map/ppermute | solution.py:60
  350.3 13.7 %collective-permute-done.77 = bf16[4,64,2304]{2,1,0:T(8,128)(2,1)S(1)} collective-permute-done((bf16[4,64,2304]{2,1,0:T(8,128)(2,1)S(1)}, bf16[4,64,2304]{2,1,0:T(8,128)(2,1)S(1)}, u32[]{:S(2)}, u32[]{:S(2)}) %collective-permute-start.77) | collective-permute-done | bytes 1179680 | tf_op jit(solution)/shard_map/ppermute | solution.py:60
  365.6 33.2 %collective-permute-done.82 = bf16[4,64,2304]{2,1,0:T(8,128)(2,1)S(1)} collective-permute-done((bf16[4,64,2304]{2,1,0:T(8,128)(2,1)S(1)}, bf16[4,64,2304]{2,1,0:T(8,128)(2,1)S(1)}, u32[]{:S(2)}, u32[]{:S(2)}) %collective-permute-start.82) | collective-permute-done | bytes 1179680 | tf_op jit(solution)/shard_map/ppermute | solution.py:60
  400.6 23.4 %collective-permute-done.72 = bf16[4,64,2304]{2,1,0:T(8,128)(2,1)S(1)} collective-permute-done((bf16[4,64,2304]{2,1,0:T(8,128)(2,1)S(1)}, bf16[4,64,2304]{2,1,0:T(8,128)(2,1)S(1)}, u32[]{:S(2)}, u32[]{:S(2)}) %collective-permute-start.72) | collective-permute-done | bytes 1179680 | tf_op jit(solution)/shard_map/ppermute | solution.py:60
  436.9 5.5 %collective-permute-done.84 = bf16[64,2304]{1,0:T(8,128)(2,1)S(1)} collective-permute-done((bf16[64,2304]{1,0:T(8,128)(2,1)S(1)}, bf16[64,2304]{1,0:T(8,128)(2,1)S(1)}, u32[]{:S(2)}, u32[]{:S(2)}) %collective-permute-start.84) | collective-permute-done | bytes 294944 | tf_op jit(solution)/shard_map/ppermute | solution.py:57
  445.6 13.6 %shard_map.258 = (bf16[512,1024]{1,0:T(8,128)(2,1)}, f32[1,1024]{1,0:T(1,128)}, f32[1,1024]{1,0:T(1,128)}, bf16[512,1536]{1,0:T(8,128)(2,1)}, bf16[512,1536]{1,0:T(8,128)(2,1)}) custom-call(s32[32]{0:T(128)} %broadcast_multiply_fusion.1.offs, bf16[512,1024]{1,0:T(8,128)(2,1)} %pad_maximum_fusion.x, f32[1,1024]{1,0:T(1,128)} %bitcast.142, ...), custom_call_target="tpu_custom_call" | custom-call | flops 2147483648 | bytes 8388608 | tf_op jit(solution)/shard_map/pallas_call | solution.py:458
  462.2 12.9 %collective-permute-start.86 = (f32[2179]{0:T(1024)S(1)}, f32[2179]{0:T(1024)S(1)}, u32[]{:S(2)}, u32[]{:S(2)}) collective-permute-start(f32[2179]{0:T(1024)S(1)} %concatenate.27), channel_id=1, source_target_pairs={{0,2},{2,0},{4,6},{6,4},{1,3},{3,1},{5,7},{7,5},{8,10},{10,8},{12,... | collective-permute-start | bytes 26156 | tf_op jit(solution)/shard_map/ppermute | solution.py:136
  495.2 9.8 %collective-permute-done.67 = bf16[4,64,1536]{2,1,0:T(8,128)(2,1)S(1)} collective-permute-done((bf16[4,64,1536]{2,1,0:T(8,128)(2,1)S(1)}, bf16[4,64,1536]{2,1,0:T(8,128)(2,1)S(1)}, u32[]{:S(2)}, u32[]{:S(2)}) %collective-permute-start.67) | collective-permute-done | bytes 786464 | tf_op jit(solution)/shard_map/ppermute | solution.py:60
  515.1 15.2 %collective-permute-done.69 = bf16[64,1536]{1,0:T(8,128)(2,1)S(1)} collective-permute-done((bf16[64,1536]{1,0:T(8,128)(2,1)S(1)}, bf16[64,1536]{1,0:T(8,128)(2,1)S(1)}, u32[]{:S(2)}, u32[]{:S(2)}) %collective-permute-start.69) | collective-permute-done | bytes 196640 | tf_op jit(solution)/shard_map/ppermute | solution.py:57
  532.1 6.5 %collective-permute-done.70 = bf16[64,1536]{1,0:T(8,128)(2,1)S(1)} collective-permute-done((bf16[64,1536]{1,0:T(8,128)(2,1)S(1)}, bf16[64,1536]{1,0:T(8,128)(2,1)S(1)}, u32[]{:S(2)}, u32[]{:S(2)}) %collective-permute-start.70) | collective-permute-done | bytes 196640 | tf_op jit(solution)/shard_map/ppermute | solution.py:57
  (394 shorter events, 215.2 us)
Async XLA Ops:
  8.2 33.9 %collective-permute-start.8 = (bf16[64,1536]{1,0:T(8,128)(2,1)S(1)}, bf16[64,1536]{1,0:T(8,128)(2,1)S(1)}, u32[]{:S(2)}, u32[]{:S(2)}) collective-permute-start(bf16[64,1536]{1,0:T(8,128)(2,1)S(1)} %pad_maximum_fusion.2.refs_0_), channel_id=1, source_target_pairs={{0,4},{2,6},{4,0},{6,2},{1,5},{3,7},{5,1},{7,3},{8,12},{10,14},{12... | collective-permute-start | bytes 589832 | tf_op jit(solution)/shard_map/ppermute | solution.py:60
  11.2 39.6 %collective-permute-start.4 = (bf16[64,1536]{1,0:T(8,128)(2,1)S(1)}, bf16[64,1536]{1,0:T(8,128)(2,1)S(1)}, u32[]{:S(2)}, u32[]{:S(2)}) collective-permute-start(bf16[64,1536]{1,0:T(8,128)(2,1)S(1)} %pad_maximum_fusion.2.refs_0_), channel_id=1, source_target_pairs={{0,2},{2,0},{4,6},{6,4},{1,3},{3,1},{5,7},{7,5},{8,10},{10,8},{12,... | collective-permute-start | bytes 589832 | tf_op jit(solution)/shard_map/ppermute | solution.py:60
  24.5 137.7 %all-gather.2.cloned.1.call-start = ((), (), s32[]{:S(2)}) async-start(), calls=%async_computation.5 | async-start | bytes 2621440 | tf_op jit(solution)/shard_map/all_gather | solution.py:671
  39.9 24.9 %collective-permute-start = (bf16[512,512]{1,0:T(8,128)(2,1)S(1)}, bf16[512,512]{1,0:T(8,128)(2,1)S(1)}, u32[]{:S(2)}, u32[]{:S(2)}) collective-permute-start(bf16[512,512]{1,0:T(8,128)(2,1)S(1)} %convolution_convert_fusion.6), channel_id=1, source_target_pairs={{0,1},{1,0},{2,3},{3,2},{4,5},{5,4},{6,7},{7,6},{8,9},{9,8},{10,11... | collective-permute-start | bytes 1572872 | tf_op jit(solution)/shard_map/ppermute | solution.py:108
  137.1 44.7 %all-to-all-start.1 = ((bf16[16,32,512]{2,1,0:T(8,128)(2,1)}), bf16[16,32,512]{2,1,0:T(8,128)(2,1)S(1)}, u32[]{:S(2)}, u32[]{:S(2)}) async-start(bf16[16,32,512]{2,1,0:T(8,128)(2,1)} %bitcast.27), calls=%async_computation.1 | async-start | bytes 1048576 | tf_op jit(solution)/shard_map/all_to_all | solution.py:610
  181.8 38.5 %collective-permute-start.16 = (bf16[512,1024]{1,0:T(8,128)(2,1)}, bf16[512,1024]{1,0:T(8,128)(2,1)}, u32[]{:S(2)}, u32[]{:S(2)}) collective-permute-start(bf16[512,1024]{1,0:T(8,128)(2,1)} %get-tuple-element.46.att_a), channel_id=1, source_target_pairs={{0,1},{1,0},{2,3},{3,2},{4,5},{5,4},{6,7},{7,6},{8,9},{9,8},{10,11... | collective-permute-start | bytes 3145736 | tf_op jit(solution)/shard_map/ppermute | solution.py:129
  182.3 36.2 %collective-permute-start.17 = (bf16[512,512]{1,0:T(8,128)(2,1)S(1)}, bf16[512,512]{1,0:T(8,128)(2,1)S(1)}, u32[]{:S(2)}, u32[]{:S(2)}) collective-permute-start(bf16[512,512]{1,0:T(8,128)(2,1)S(1)} %convolution_convert_fusion.4), channel_id=1, source_target_pairs={{0,1},{1,0},{2,3},{3,2},{4,5},{5,4},{6,7},{7,6},{8,9},{9,8},{10,11... | collective-permute-start | bytes 1572872 | tf_op jit(solution)/shard_map/ppermute | solution.py:108
  194.0 25.8 %collective-permute-start.39 = (bf16[64,2304]{1,0:T(8,128)(2,1)}, bf16[64,2304]{1,0:T(8,128)(2,1)S(1)}, u32[]{:S(2)}, u32[]{:S(2)}) collective-permute-start(bf16[64,2304]{1,0:T(8,128)(2,1)} %collective-permute-done.35.refs_19_), channel_id=1, source_target_pairs={{0,2},{2,0},{4,6},{6,4},{1,3},{3,1},{5,7},{7,5},{8,10},{10,8},{12,... | collective-permute-start | bytes 884744 | tf_op jit(solution)/shard_map/ppermute | solution.py:60
  194.0 25.8 %collective-permute-start.62 = (bf16[64,2304]{1,0:T(8,128)(2,1)}, bf16[64,2304]{1,0:T(8,128)(2,1)S(1)}, u32[]{:S(2)}, u32[]{:S(2)}) collective-permute-start(bf16[64,2304]{1,0:T(8,128)(2,1)} %collective-permute-done.58.refs_43_), channel_id=1, source_target_pairs={{0,2},{2,0},{4,6},{6,4},{1,3},{3,1},{5,7},{7,5},{8,10},{10,8},{12,... | collective-permute-start | bytes 884744 | tf_op jit(solution)/shard_map/ppermute | solution.py:60
  251.2 33.2 %collective-permute-start.63 = (bf16[512,512]{1,0:T(8,128)(2,1)}, bf16[512,512]{1,0:T(8,128)(2,1)S(1)}, u32[]{:S(2)}, u32[]{:S(2)}) collective-permute-start(bf16[512,512]{1,0:T(8,128)(2,1)} %constant_dynamic-slice_fusion), channel_id=1, source_target_pairs={{0,1},{1,0},{2,3},{3,2},{4,5},{5,4},{6,7},{7,6},{8,9},{9,8},{10,11... | collective-permute-start | bytes 1572872 | tf_op jit(solution)/shard_map/ppermute | solution.py:123
  251.4 51.1 %collective-permute-start.64 = (bf16[512,1024]{1,0:T(8,128)(2,1)}, bf16[512,1024]{1,0:T(8,128)(2,1)}, u32[]{:S(2)}, u32[]{:S(2)}) collective-permute-start(bf16[512,1024]{1,0:T(8,128)(2,1)} %get-tuple-element.48), channel_id=1, source_target_pairs={{0,1},{1,0},{2,3},{3,2},{4,5},{5,4},{6,7},{7,6},{8,9},{9,8},{10,11... | collective-permute-start | bytes 3145736 | tf_op jit(solution)/shard_map/ppermute | solution.py:114
  273.4 49.0 %collective-permute-start.76 = (bf16[8,64,2304]{2,1,0:T(8,128)(2,1)}, bf16[8,64,2304]{2,1,0:T(8,128)(2,1)}, u32[]{:S(2)}, u32[]{:S(2)}) collective-permute-start(bf16[8,64,2304]{2,1,0:T(8,128)(2,1)} %bitcast.146), channel_id=1, source_target_pairs={{0,2},{2,0},{4,6},{6,4},{1,3},{3,1},{5,7},{7,5},{8,10},{10,8},{12,... | collective-permute-start | bytes 7077896 | tf_op jit(solution)/shard_map/ppermute | solution.py:60
  273.4 69.1 %collective-permute-start.81 = (bf16[8,64,2304]{2,1,0:T(8,128)(2,1)}, bf16[8,64,2304]{2,1,0:T(8,128)(2,1)}, u32[]{:S(2)}, u32[]{:S(2)}) collective-permute-start(bf16[8,64,2304]{2,1,0:T(8,128)(2,1)} %bitcast.55), channel_id=1, source_target_pairs={{0,2},{2,0},{4,6},{6,4},{1,3},{3,1},{5,7},{7,5},{8,10},{10,8},{12,... | collective-permute-start | bytes 7077896 | tf_op jit(solution)/shard_map/ppermute | solution.py:60
  284.2 62.2 %collective-permute-start.71 = (bf16[8,64,2304]{2,1,0:T(8,128)(2,1)}, bf16[8,64,2304]{2,1,0:T(8,128)(2,1)}, u32[]{:S(2)}, u32[]{:S(2)}) collective-permute-start(bf16[8,64,2304]{2,1,0:T(8,128)(2,1)} %bitcast.145), channel_id=1, source_target_pairs={{0,2},{2,0},{4,6},{6,4},{1,3},{3,1},{5,7},{7,5},{8,10},{10,8},{12,... | collective-permute-start | bytes 7077896 | tf_op jit(solution)/shard_map/ppermute | solution.py:60
  287.1 33.0 %all-to-all-start.2 = ((bf16[16,32,512]{2,1,0:T(8,128)(2,1)}), bf16[16,32,512]{2,1,0:T(8,128)(2,1)}, u32[]{:S(2)}, u32[]{:S(2)}) async-start(bf16[16,32,512]{2,1,0:T(8,128)(2,1)} %bitcast.135), calls=%async_computation.2 | async-start | bytes 1048576 | tf_op jit(solution)/shard_map/all_to_all | solution.py:615
  291.4 152.0 %reduce-scatter.2.cloned.1.call-start = ((), (), s32[]{:S(2)}) async-start(), calls=%async_computation.6 | async-start | bytes 2621440 | tf_op jit(solution)/shard_map/reduce_scatter | solution.py:732
  325.4 38.6 %collective-permute-start.77 = (bf16[4,64,2304]{2,1,0:T(8,128)(2,1)S(1)}, bf16[4,64,2304]{2,1,0:T(8,128)(2,1)S(1)}, u32[]{:S(2)}, u32[]{:S(2)}) collective-permute-start(bf16[4,64,2304]{2,1,0:T(8,128)(2,1)S(1)} %slice.188), channel_id=1, source_target_pairs={{0,4},{2,6},{4,0},{6,2},{1,5},{3,7},{5,1},{7,3},{8,12},{10,14},{12... | collective-permute-start | bytes 3538952 | tf_op jit(solution)/shard_map/ppermute | solution.py:60
  344.9 53.9 %collective-permute-start.82 = (bf16[4,64,2304]{2,1,0:T(8,128)(2,1)S(1)}, bf16[4,64,2304]{2,1,0:T(8,128)(2,1)S(1)}, u32[]{:S(2)}, u32[]{:S(2)}) collective-permute-start(bf16[4,64,2304]{2,1,0:T(8,128)(2,1)S(1)} %slice.194), channel_id=1, source_target_pairs={{0,4},{2,6},{4,0},{6,2},{1,5},{3,7},{5,1},{7,3},{8,12},{10,14},{12... | collective-permute-start | bytes 3538952 | tf_op jit(solution)/shard_map/ppermute | solution.py:60
  348.7 75.3 %collective-permute-start.72 = (bf16[4,64,2304]{2,1,0:T(8,128)(2,1)S(1)}, bf16[4,64,2304]{2,1,0:T(8,128)(2,1)S(1)}, u32[]{:S(2)}, u32[]{:S(2)}) collective-permute-start(bf16[4,64,2304]{2,1,0:T(8,128)(2,1)S(1)} %slice.182), channel_id=1, source_target_pairs={{0,4},{2,6},{4,0},{6,2},{1,5},{3,7},{5,1},{7,3},{8,12},{10,14},{12... | collective-permute-start | bytes 3538952 | tf_op jit(solution)/shard_map/ppermute | solution.py:60
  364.3 61.6 %collective-permute-start.78 = (bf16[64,2304]{1,0:T(8,128)(2,1)S(1)}, bf16[64,2304]{1,0:T(8,128)(2,1)S(1)}, u32[]{:S(2)}, u32[]{:S(2)}) collective-permute-start(bf16[64,2304]{1,0:T(8,128)(2,1)S(1)} %slice_bitcast_fusion.7), channel_id=1, source_target_pairs={{0,8},{8,16},{16,24},{24,0},{1,9},{9,17},{17,25},{25,1},{2,10},{10... | collective-permute-start | bytes 884744 | tf_op jit(solution)/shard_map/ppermute | solution.py:57
  399.1 28.4 %collective-permute-start.83 = (bf16[64,2304]{1,0:T(8,128)(2,1)S(1)}, bf16[64,2304]{1,0:T(8,128)(2,1)S(1)}, u32[]{:S(2)}, u32[]{:S(2)}) collective-permute-start(bf16[64,2304]{1,0:T(8,128)(2,1)S(1)} %slice_bitcast_fusion.3), channel_id=1, source_target_pairs={{0,8},{8,16},{16,24},{24,0},{1,9},{9,17},{17,25},{25,1},{2,10},{10... | collective-permute-start | bytes 884744 | tf_op jit(solution)/shard_map/ppermute | solution.py:57
  433.7 41.5 %collective-permute-start.74 = (bf16[64,2304]{1,0:T(8,128)(2,1)}, bf16[64,2304]{1,0:T(8,128)(2,1)}, u32[]{:S(2)}, u32[]{:S(2)}) collective-permute-start(bf16[64,2304]{1,0:T(8,128)(2,1)} %fusion.11), channel_id=1, source_target_pairs={{0,8},{8,16},{16,24},{24,0},{1,9},{9,17},{17,25},{25,1},{2,10},{10... | collective-permute-start | bytes 884744 | tf_op jit(solution)/shard_map/ppermute | solution.py:57
  436.9 42.2 %collective-permute-start.80 = (bf16[64,2304]{1,0:T(8,128)(2,1)}, bf16[64,2304]{1,0:T(8,128)(2,1)}, u32[]{:S(2)}, u32[]{:S(2)}) collective-permute-start(bf16[64,2304]{1,0:T(8,128)(2,1)} %fusion.8), channel_id=1, source_target_pairs={{0,8},{8,16},{16,24},{24,0},{1,9},{9,17},{17,25},{25,1},{2,10},{10... | collective-permute-start | bytes 884744 | tf_op jit(solution)/shard_map/ppermute | solution.py:57
  443.2 38.2 %collective-permute-start.85 = (bf16[64,2304]{1,0:T(8,128)(2,1)}, bf16[64,2304]{1,0:T(8,128)(2,1)}, u32[]{:S(2)}, u32[]{:S(2)}) collective-permute-start(bf16[64,2304]{1,0:T(8,128)(2,1)} %fusion.6), channel_id=1, source_target_pairs={{0,8},{8,16},{16,24},{24,0},{1,9},{9,17},{17,25},{25,1},{2,10},{10... | collective-permute-start | bytes 884744 | tf_op jit(solution)/shard_map/ppermute | solution.py:57
  (134 other events, 2214.7 us)
Sparse Core Ops, SparseCore 0:
  76.9 29.7 all-gather.1
  320.2 65.6 reduce-scatter.1

commit v3 on v2

--- a/solution.py
+++ b/solution.py
@@ -66,21 +66,6 @@
             for k in range(self.n)
         ]
 
-    def collect(self, shard):
-        have = [shard]
-        for _ in range(self.n - 1):
-            have.append(self.ring(have[-1]))
-        bits = []
-        b = self.ctx // 2
-        while b:
-            bits.append(b)
-            b //= 2
-        got = {(0, k): v for k, v in enumerate(have)}
-        for bit in bits:
-            more = {(d | bit, k): self.flip(v, bit) for (d, k), v in got.items()}
-            got.update(more)
-        return [got[(d, k)] for d in range(self.ctx) for k in range(self.n)]
-
     def reduce_ctx(self, keep, send):
         total = (keep.astype(F32) + self.flip(send, 1).astype(F32)).astype(BF)
         bit = self.ctx // 2
@@ -204,72 +189,6 @@
 def doubled(ref, rows, column):
     v = ref[rows, column : column + HEAD_SIZE]
     return jnp.concatenate([v, v], axis=1)
-
-
-def qkv_kernel(q_width, kv_width, pieces, shard_rows, offs, x, gain, head_gain, cosines, sines, *refs):
-    sources = refs[:pieces]
-    qb, kv, raw, w, sem = refs[pieces:]
-    copies = [
-        pltpu.make_async_copy(
-            sources[i], w.at[pl.ds(pl.multiple_of(offs[i], shard_rows), shard_rows), :], sem.at[i]
-        )
-        for i in range(pieces)
-    ]
-    for c in copies:
-        c.start()
-    v = x[...].astype(F32)
-    normed = (v * row_scale(v) * gain[...]).astype(BF)
-    for c in copies:
-        c.wait()
-    total = q_width + 2 * kv_width
-    values_from = q_width + kv_width
-    for b in range(0, total, 128):
-        block = dot(normed, w[:, b : b + 128], 1, 0)
-        is_value = lanes(block.shape) + b >= values_from
-        done = qk_forward(block, head_gain[:, b : b + 128], cosines[...], sines[...], is_value)
-        raw[:, b : b + 128] = block
-        if b < q_width:
-            qb[:, b : b + 128] = done.astype(BF)
-        else:
-            kv[:, b - q_width : b - q_width + 128] = done.astype(BF)
-
-
-def attend_kernel(q_width, kv_width, piece, where, qb, kv, start_col, w, heads, sums, part, acc, total, bias):
-    ctx = where[0]
-    rows = qb.shape[0]
-    q_slot = ctx * piece + lax.broadcasted_iota(jnp.int32, (rows, piece), 0)
-    n_pairs = q_width // 128
-
-    def one_piece(p, carry):
-        k_slot = p * piece + lanes((rows, piece))
-        open_ = (k_slot >= start_col[...]) & (k_slot <= q_slot)
-        bias[...] = jnp.where(open_, 0.0, NEG_FILL)
-        at = pl.ds(pl.multiple_of(p * piece, piece), piece)
-        for g in range(n_pairs):
-            q2 = two_heads(qb[:, 128 * g : 128 * g + 128])
-            k2 = doubled(kv, at, HEAD_SIZE * g)
-            v2 = doubled(kv, at, kv_width + HEAD_SIZE * g)
-            s = dot(q2, k2, 1, 1)
-            for h in range(2):
-                e = jnp.exp(s[h * rows : (h + 1) * rows] * 0.125 + bias[...])
-                part_sum = e[:, :128]
-                for b in range(128, piece, 128):
-                    part_sum = part_sum + e[:, b : b + 128]
-                o = dot(e.astype(BF), v2, 1, 0)
-                acc[g, h * rows : (h + 1) * rows, :] += o
-                total[g, h * rows : (h + 1) * rows, :] += part_sum
-        return carry
-
-    acc[...] = jnp.zeros_like(acc)
-    total[...] = jnp.zeros_like(total)
-    lax.fori_loop(0, ctx + 1, one_piece, 0)
-    ones = jnp.ones((8, 128), F32)
-    for g in range(n_pairs):
-        row_total = jnp.sum(total[g], axis=1, keepdims=True)
-        heads[:, 128 * g : 128 * g + 128] = one_row(acc[g] / row_total)
-        sums[g] = 1.0 / dot(ones, total[g], 1, 1, lax.Precision.HIGHEST)
-    out_from = q_width + 2 * kv_width
-    part[...] = dot(heads[...].astype(BF), w[:, out_from:], 1, 1).astype(BF)
 
 
 def attend_back_kernel(
@@ -358,59 +277,20 @@
     d_gain[...] = gain_sum
 
 
-def ffn_kernel(pieces, shard_rows, tile, group, offs, x, att_a, att_b, dy, gain, *refs):
-    wg_in = refs[:pieces]
-    wu_in = refs[pieces : 2 * pieces]
-    wd_in = refs[2 * pieces : 3 * pieces]
-    ffn, dmid, dgain, squares, nb, hid, dgt, dup = refs[3 * pieces : 3 * pieces + 8]
-    (wg, wu, wd, mid, ffn_acc, dn_acc, sem) = refs[3 * pieces + 8 :]
+def ffn_kernel(mid, dy, gain, w_gate, w_up, w_down, ffn, dmid, dgain, nb, hid, dgt, dup, ffn_acc, dn_acc):
     step = pl.program_id(0)
-    steps = pl.num_programs(0)
-    n_groups = wg.shape[1] // group
-    per_group = group // tile
-
-    def copies(g):
-        out = []
-        cols = pl.ds(g * group, group)
-        for m, (src, dst) in enumerate(((wg_in, wg), (wu_in, wu), (wd_in, wd))):
-            for i in range(pieces):
-                rows = pl.ds(pl.multiple_of(offs[i], shard_rows), shard_rows)
-                out.append(
-                    pltpu.make_async_copy(src[i].at[:, cols], dst.at[rows, cols], sem.at[g, m, i])
-                )
-        return out
 
     @pl.when(step == 0)
     def _():
-        for g in range(n_groups):
-            for c in copies(g):
-                c.start()
-        v = x[...].astype(F32)
-        att = att_a[...].astype(F32) + att_b[...].astype(F32)
-        squares[0:1, :] = jnp.sum(v * v, axis=0, keepdims=True)
-        squares[1:2, :] = jnp.sum(att * att, axis=0, keepdims=True)
-        mid[...] = (v + att).astype(BF)
-        v = mid[...].astype(F32)
+        v = mid[...].astype(BF).astype(F32)
         nb[...] = (v * row_scale(v) * gain[...]).astype(BF)
         ffn_acc[...] = jnp.zeros_like(ffn_acc)
         dn_acc[...] = jnp.zeros_like(dn_acc)
 
-    for g in range(n_groups):
-
-        @pl.when(step == g * per_group)
-        def _(g=g):
-            for c in copies(g):
-                c.wait()
-
-    cols = pl.ds(pl.multiple_of(step * tile, tile), tile)
-    w_gate = wg[:, cols]
-    w_up = wu[:, cols]
-    w_down = wd[:, cols]
     normed = nb[...]
-    dyb = dy[...]
-    gate = dot(normed, w_gate, 1, 0)
-    up = dot(normed, w_up, 1, 0)
-    d_hidden = dot(dyb, w_down, 1, 0)
+    gate = dot(normed, w_gate[...], 1, 0)
+    up = dot(normed, w_up[...], 1, 0)
+    d_hidden = dot(dy[...], w_down[...], 1, 0)
     sig = 1.0 / (1.0 + jnp.exp(-gate))
     silu = gate * sig
     hidden = (silu * up).astype(BF)
@@ -419,12 +299,13 @@
     hid[...] = hidden
     dgt[...] = d_gate
     dup[...] = d_up
-    ffn_acc[...] += dot(hidden, w_down, 1, 1)
-    dn_acc[...] += dot(d_gate, w_gate, 1, 1) + dot(d_up, w_up, 1, 1)
-
-    @pl.when(step == steps - 1)
+    ffn_acc[...] += dot(hidden, w_down[...], 1, 1)
+    dn_acc[...] += dot(d_gate, w_gate[...], 1, 1) + dot(d_up, w_up[...], 1, 1)
+
+    @pl.when(step == pl.num_programs(0) - 1)
     def _():
-        grad, gain_sum = norm_back(dn_acc[...], mid[...].astype(F32), gain[...])
+        v = mid[...].astype(BF).astype(F32)
+        grad, gain_sum = norm_back(dn_acc[...], v, gain[...])
         dgain[...] = gain_sum
         dmid[...] = grad.astype(BF)
         ffn[...] = ffn_acc[...].astype(BF)
@@ -441,6 +322,418 @@
     half = ordered.shape[0] // 2
     keep[...] = dot(ordered[:half, :], right[...], 1, 0).astype(BF)
     send[...] = dot(ordered[half:, :], right[...], 1, 0).astype(BF)
+
+
+class Place:
+    def __init__(self, n, ctx, tp):
+        self.n, self.ctx, self.tp = n, ctx, tp
+        self.z = lax.axis_index("fsdp")
+        self.c = lax.axis_index("ctx")
+        self.t = lax.axis_index("tp")
+        self.me = self.z * ctx + self.c
+
+    def at(self, z=None, c=None, t=None):
+        return (
+            self.z if z is None else z,
+            self.c if c is None else c,
+            self.t if t is None else t,
+        )
+
+    def peer(self, j):
+        p = lax.rem(self.me + j, self.n * self.ctx)
+        return self.at(p // self.ctx, lax.rem(p, self.ctx))
+
+    def up(self, j):
+        return self.at(z=lax.rem(self.z + j, self.n))
+
+    def flip(self, bit):
+        if bit == 1:
+            return self.c + 1 - 2 * lax.rem(self.c, 2)
+        return lax.rem(self.c + 2, 4)
+
+    def side(self, j):
+        return self.at(t=lax.rem(self.t + j, self.tp))
+
+    def owner(self, k, c):
+        return lax.rem(self.z - k + self.n, self.n) * self.ctx + c
+
+    def greet(self):
+        barrier = pltpu.get_barrier_semaphore()
+        group = self.n * self.ctx
+        for j in range(1, group):
+            pl.semaphore_signal(barrier, inc=1, device_id=self.peer(j), device_id_type=MESH)
+        for j in range(1, self.tp):
+            pl.semaphore_signal(barrier, inc=1, device_id=self.side(j), device_id_type=MESH)
+        pl.semaphore_wait(barrier, group + self.tp - 2)
+
+
+MESH = pl.DeviceIdType.MESH
+
+
+def remote(src, dst, send, recv, device):
+    return pltpu.make_async_remote_copy(
+        src_ref=src, dst_ref=dst, send_sem=send, recv_sem=recv, device_id=device, device_id_type=MESH
+    )
+
+
+def block_rows(index, size):
+    return pl.ds(pl.multiple_of(index * size, size), size)
+
+
+class Gather:
+    def __init__(self, place, shard, whole, columns, number, sems):
+        z_send, z_recv, x_send, x_recv, c_send, c_recv, own = sems
+        h = shard.shape[0]
+        n = place.n
+        view = lambda index: whole.at[block_rows(index, h), columns]
+        here, there = place.c, place.flip(2)
+        mine = shard.at[:, columns]
+        self.own = pltpu.make_async_copy(mine, view(place.me), own.at[number])
+        self.line = [
+            remote(mine, view(place.me), z_send.at[number, j], z_recv.at[number, j], place.up(j))
+            for j in range(1, n)
+        ]
+        self.chip = [
+            remote(
+                mine if k == 0 else view(place.owner(k, here)),
+                view(place.owner(k, here)),
+                x_send.at[number, k],
+                x_recv.at[number, k],
+                place.at(c=there),
+            )
+            for k in range(n)
+        ]
+        self.core = [
+            remote(
+                mine if i == 0 else view(place.owner(i % n, here if i < n else there)),
+                view(place.owner(i % n, here if i < n else there)),
+                c_send.at[number, i],
+                c_recv.at[number, i],
+                place.at(c=place.flip(1)),
+            )
+            for i in range(2 * n)
+        ]
+
+    def begin(self):
+        for copy in self.line:
+            copy.start()
+        self.chip[0].start()
+        self.own.start()
+        self.core[0].start()
+
+    def pass_line(self, k):
+        self.line[k - 1].wait_recv()
+        self.chip[k].start()
+        self.core[k].start()
+
+    def pass_chip(self, k):
+        self.chip[k].wait_recv()
+        self.core[len(self.chip) + k].start()
+
+    def finish(self):
+        for copy in self.core:
+            copy.wait_recv()
+        self.own.wait()
+
+    def drain(self):
+        for copy in self.line + self.chip + self.core:
+            copy.wait_send()
+
+
+def forward_kernel(
+    n, ctx, tp, q_width, kv_width, ff,
+    sent_x, sent_y, pick, gain, head_gain, cosines, sines, start_col, attn_shard, ffn_shard,
+    x, dy, qb, kv, raw, heads, sums, mid, squares, w_attn, w_ffn,
+    got_x, got_y, own_x, own_y, x_land, y_land, w, kv_all, part, land, acc, total, bias,
+    route_send, route_recv, tp_send, tp_recv, kv_send, kv_recv, out_sem, *gather_sems
+):
+    place = Place(n, ctx, tp)
+    group = n * ctx
+    rows = got_x.shape[0]
+    share = rows // group
+    feat = got_x.shape[1]
+    width = x_land.shape[1]
+    piece = rows
+    every = pl.ds(0, attn_shard.shape[1])
+    attn = Gather(place, attn_shard, w, every, 0, gather_sems)
+    ffn = [
+        Gather(place, ffn_shard, w_ffn, pl.ds(i * ff, ff), 1 + i, gather_sems) for i in range(3)
+    ]
+
+    def route(number, src, dst):
+        return [
+            remote(
+                src.at[block_rows(lax.rem(place.me + j, group), share), :],
+                dst.at[block_rows(place.me, share), :],
+                route_send.at[number, j],
+                route_recv.at[number, j],
+                place.peer(j),
+            )
+            for j in range(1, group)
+        ]
+
+    def widen(number, src, dst):
+        return [
+            remote(
+                src,
+                dst.at[:, block_rows(place.t, feat)],
+                tp_send.at[number, j],
+                tp_recv.at[number, j],
+                place.side(j),
+            )
+            for j in range(1, tp)
+        ]
+
+    def own_block(src, dst):
+        at = block_rows(place.me, share)
+        dst[at, :] = src[at, :]
+
+    route_x, route_y = route(0, sent_x, got_x), route(1, sent_y, got_y)
+    wide_x, wide_y = widen(0, own_x, x_land), widen(1, own_y, y_land)
+    place.greet()
+    for copy in route_x:
+        copy.start()
+    attn.begin()
+    for g in ffn:
+        g.begin()
+    own_block(sent_x, got_x)
+    for copy in route_x:
+        copy.wait_recv()
+    own_x[...] = dot(pick[...], got_x[...], 1, 0).astype(BF)
+    for copy in wide_x:
+        copy.start()
+    x_land[:, block_rows(place.t, feat)] = own_x[...]
+    for copy in route_y:
+        copy.start()
+    own_block(sent_y, got_y)
+    for k in range(1, n):
+        attn.pass_line(k)
+    for k in range(n):
+        attn.pass_chip(k)
+    for copy in wide_x:
+        copy.wait_recv()
+    v = x_land[...].astype(F32)
+    x[...] = x_land[...]
+    normed = (v * row_scale(v) * gain[...]).astype(BF)
+    attn.finish()
+    write_w = pltpu.make_async_copy(w, w_attn, out_sem.at[0])
+    write_w.start()
+
+    own_rows = block_rows(place.c, piece)
+    values_from = q_width + kv_width
+    for b in list(range(q_width, q_width + 2 * kv_width, 128)) + list(range(0, q_width, 128)):
+        if b == 0:
+            later = start_keys(place, kv_all, own_rows, kv_send, kv_recv)
+        block = dot(normed, w[:, b : b + 128], 1, 0)
+        is_value = lanes(block.shape) + b >= values_from
+        done = qk_forward(block, head_gain[:, b : b + 128], cosines[...], sines[...], is_value)
+        raw[:, b : b + 128] = block
+        if b < q_width:
+            qb[:, b : b + 128] = done.astype(BF)
+        else:
+            kv_all[own_rows, b - q_width : b - q_width + 128] = done.astype(BF)
+    for g in ffn:
+        g.pass_line(1)
+        g.pass_chip(0)
+
+    q_slot = place.c * piece + lax.broadcasted_iota(jnp.int32, (rows, piece), 0)
+    n_pairs = q_width // 128
+
+    def one_piece(p):
+        k_slot = p * piece + lanes((rows, piece))
+        open_ = (k_slot >= start_col[...]) & (k_slot <= q_slot)
+        bias[...] = jnp.where(open_, 0.0, NEG_FILL)
+        at = block_rows(p, piece)
+
+        for g in range(n_pairs):
+            q2 = two_heads(qb[:, 128 * g : 128 * g + 128])
+            k2 = doubled(kv_all, at, HEAD_SIZE * g)
+            v2 = doubled(kv_all, at, kv_width + HEAD_SIZE * g)
+            s = dot(q2, k2, 1, 1)
+            for h in range(2):
+                e = jnp.exp(s[h * rows : (h + 1) * rows] * 0.125 + bias[...])
+                part_sum = e[:, :128]
+                for b in range(128, piece, 128):
+                    part_sum = part_sum + e[:, b : b + 128]
+                o = dot(e.astype(BF), v2, 1, 0)
+                acc[g, h * rows : (h + 1) * rows, :] += o
+                total[g, h * rows : (h + 1) * rows, :] += part_sum
+
+    acc[...] = jnp.zeros_like(acc)
+    total[...] = jnp.zeros_like(total)
+    one_piece(place.c)
+    x_bit, core_bit = place.c // 2, lax.rem(place.c, 2)
+    near, across, passed = later
+
+    @pl.when(x_bit == 1)
+    def _():
+        across.wait_recv()
+        passed.start()
+
+    for g in ffn:
+        g.pass_line(2)
+        g.pass_chip(1)
+
+    @pl.when(core_bit == 1)
+    def _():
+        near.wait_recv()
+        one_piece(place.c - 1)
+
+    for g in ffn:
+        g.pass_line(3)
+
+    @pl.when(x_bit == 1)
+    def _():
+        passed.wait_recv()
+
+        def step(p, carry):
+            one_piece(p)
+            return carry
+
+        lax.fori_loop(0, 2, step, 0)
+
+    ones = jnp.ones((8, 128), F32)
+    for g in range(n_pairs):
+        row_total = jnp.sum(total[g], axis=1, keepdims=True)
+        heads[:, 128 * g : 128 * g + 128] = one_row(acc[g] / row_total)
+        sums[g] = 1.0 / dot(ones, total[g], 1, 1, lax.Precision.HIGHEST)
+    part[...] = dot(heads[...].astype(BF), w[:, q_width + 2 * kv_width :], 1, 1).astype(BF)
+    attention = [
+        remote(part, land.at[j - 1], tp_send.at[2, j], tp_recv.at[2, j], place.side(j))
+        for j in range(1, tp)
+    ]
+    for copy in attention:
+        copy.start()
+    write_kv = pltpu.make_async_copy(kv_all, kv, out_sem.at[1])
+    for copy in route_y:
+        copy.wait_recv()
+    own_y[...] = dot(pick[...], got_y[...], 1, 0).astype(BF)
+    for copy in wide_y:
+        copy.start()
+    y_land[:, block_rows(place.t, feat)] = own_y[...]
+    for g in ffn:
+        g.pass_chip(2)
+    for copy in attention:
+        copy.wait_recv()
+    att = part[...].astype(F32)
+    for j in range(1, tp):
+        att = att + land[j - 1].astype(F32)
+    v = x_land[...].astype(F32)
+    squares[0:1, :] = jnp.sum(v * v, axis=0, keepdims=True)
+    squares[1:2, :] = jnp.sum(att * att, axis=0, keepdims=True)
+    mid[...] = v + att
+    for copy in wide_y:
+        copy.wait_recv()
+    dy[...] = y_land[...]
+    for g in ffn:
+        g.pass_chip(3)
+
+    @pl.when(core_bit == 0)
+    def _():
+        near.wait_send()
+
+    @pl.when(x_bit == 0)
+    def _():
+        across.wait_send()
+
+    @pl.when(x_bit == 1)
+    def _():
+        passed.wait_send()
+
+    write_kv.start()
+    for g in ffn:
+        g.finish()
+    for copy in route_x + route_y + wide_x + wide_y + attention:
+        copy.wait_send()
+    for g in [attn] + ffn:
+        g.drain()
+    write_w.wait()
+    write_kv.wait()
+
+
+def start_keys(place, kv_all, own_rows, send, recv):
+    x_bit, core_bit = place.c // 2, lax.rem(place.c, 2)
+    mine = kv_all.at[own_rows, :]
+    near = remote(mine, mine, send.at[0], recv.at[0], place.at(c=place.flip(1)))
+    across = remote(mine, mine, send.at[1], recv.at[1], place.at(c=place.flip(2)))
+    from_chip = kv_all.at[block_rows(place.flip(2), own_rows.size), :]
+    passed = remote(from_chip, from_chip, send.at[2], recv.at[2], place.at(c=place.flip(1)))
+
+    @pl.when(x_bit == 0)
+    def _():
+        across.start()
+
+    @pl.when(core_bit == 0)
+    def _():
+        near.start()
+
+    return near, across, passed
+
+
+def forward_pass(grid, q_width, kv_width, ff, *operands):
+    sent_x, attn_shard = operands[0], operands[8]
+    rows, feat = sent_x.shape
+    n, ctx, tp = grid.n, grid.ctx, grid.tp
+    width = feat * tp
+    n_pairs = q_width // 128
+    row_len = rows * ctx
+    qkv_width = q_width + 2 * kv_width
+    vm = pl.BlockSpec(memory_space=pltpu.VMEM)
+    dma = pltpu.SemaphoreType.DMA
+    group = n * ctx
+    return pl.pallas_call(
+        functools.partial(forward_kernel, n, ctx, tp, q_width, kv_width, ff),
+        in_specs=[vm] * 8 + [ANYWHERE] * 2,
+        out_specs=[vm] * 3 + [ANYWHERE] + [vm] * 5 + [ANYWHERE] * 2,
+        out_shape=[
+            shape((rows, width), BF),
+            shape((rows, width), BF),
+            shape((rows, q_width), BF),
+            shape((row_len, 2 * kv_width), BF),
+            shape((rows, qkv_width), F32),
+            shape((rows, q_width), F32),
+            shape((n_pairs, 8, 2 * rows), F32),
+            shape((rows, width), F32),
+            shape((2, width), F32),
+            shape((width, attn_shard.shape[1]), BF),
+            shape((width, 3 * ff), BF),
+        ],
+        scratch_shapes=[
+            pltpu.VMEM((rows, feat), BF),
+            pltpu.VMEM((rows, feat), BF),
+            pltpu.VMEM((rows, feat), BF),
+            pltpu.VMEM((rows, feat), BF),
+            pltpu.VMEM((rows, width), BF),
+            pltpu.VMEM((rows, width), BF),
+            pltpu.VMEM((width, attn_shard.shape[1]), BF),
+            pltpu.VMEM((row_len, 2 * kv_width), BF),
+            pltpu.VMEM((rows, width), BF),
+            pltpu.VMEM((tp - 1, rows, width), BF),
+            pltpu.VMEM((n_pairs, 2 * rows, 128), F32),
+            pltpu.VMEM((n_pairs, 2 * rows, 128), F32),
+            pltpu.VMEM((rows, rows), F32),
+            dma((2, group)),
+            dma((2, group)),
+            dma((3, tp)),
+            dma((3, tp)),
+            dma((3,)),
+            dma((3,)),
+            dma((2,)),
+            dma((4, n)),
+            dma((4, n)),
+            dma((4, n)),
+            dma((4, n)),
+            dma((4, 2 * n)),
+            dma((4, 2 * n)),
+            dma((4,)),
+        ],
+        compiler_params=pltpu.CompilerParams(
+            vmem_limit_bytes=58 * 2**20, collective_id=0, has_side_effects=True
+        ),
+        cost_estimate=pl.CostEstimate(
+            flops=8 * rows * row_len * q_width, bytes_accessed=40 * 2**20, transcendentals=0
+        ),
+    )(*operands)
 
 
 def shape(s, t):
@@ -472,41 +765,30 @@
     return call
 
 
-def ffn_pass(x, att_a, att_b, dy, gain, gate_p, up_p, down_p, offsets):
-    rows, width = x.shape
-    pieces = len(gate_p)
-    shard_rows, ff = gate_p[0].shape
+def ffn_pass(mid, dy, gain, w_ffn):
+    rows, width = mid.shape
+    ff = w_ffn.shape[1] // 3
     tile = 256 if ff % 256 == 0 else 128
-    group = 3 * tile if ff % (3 * tile) == 0 else tile
-    whole = lambda shape: pl.BlockSpec(shape, lambda s, o: (0, 0))
-    column = pl.BlockSpec((rows, tile), lambda s, o: (0, s))
+    steps = ff // tile
+    whole = lambda shape: pl.BlockSpec(shape, lambda s: (0, 0))
+    column = pl.BlockSpec((rows, tile), lambda s: (0, s))
+    weight = lambda i: pl.BlockSpec((width, tile), lambda s: (0, i * steps + s))
     return pl.pallas_call(
-        functools.partial(ffn_kernel, pieces, shard_rows, tile, group),
-        grid_spec=pltpu.PrefetchScalarGridSpec(
-            num_scalar_prefetch=1,
-            grid=(ff // tile,),
-            in_specs=[whole((rows, width))] * 4 + [whole((1, width))] + [ANYWHERE] * (3 * pieces),
-            out_specs=[whole((rows, width))] * 2
-            + [whole((1, width)), whole((2, width)), whole((rows, width))]
-            + [column] * 3,
-            scratch_shapes=[
-                pltpu.VMEM((width, ff), BF),
-                pltpu.VMEM((width, ff), BF),
-                pltpu.VMEM((width, ff), BF),
-                pltpu.VMEM((rows, width), BF),
-                pltpu.VMEM((rows, width), F32),
-                pltpu.VMEM((rows, width), F32),
-                pltpu.SemaphoreType.DMA((ff // group, 3, pieces)),
-            ],
-        ),
+        ffn_kernel,
+        grid=(steps,),
+        in_specs=[whole((rows, width))] * 2 + [whole((1, width))] + [weight(i) for i in range(3)],
+        out_specs=[whole((rows, width))] * 2
+        + [whole((1, width)), whole((rows, width))]
+        + [column] * 3,
+        scratch_shapes=[pltpu.VMEM((rows, width), F32), pltpu.VMEM((rows, width), F32)],
         out_shape=[shape((rows, width), BF)] * 2
-        + [shape((1, width), F32), shape((2, width), F32), shape((rows, width), BF)]
+        + [shape((1, width), F32), shape((rows, width), BF)]
         + [shape((rows, ff), BF)] * 3,
         compiler_params=VMEM_LIMIT,
         cost_estimate=pl.CostEstimate(
             flops=12 * rows * width * ff, bytes_accessed=6 * width * ff, transcendentals=rows * ff
         ),
-    )(offsets, x, att_a, att_b, dy, gain, *gate_p, *up_p, *down_p)
+    )(mid, dy, gain, w_ffn, w_ffn, w_ffn)
 
 
 def weight_grad(left, right, offsets, pieces):
@@ -605,10 +887,8 @@
     arrival = source * share + jnp.sum(before.astype(jnp.int32), axis=1)
     take_pick = one_hot(arrival[:, None], line[None, :])
 
-    def spread(v):
-        sent = product(send_pick, v, "pt,tf->pf").astype(BF)
-        got = lax.all_to_all(sent, both, split_axis=0, concat_axis=0, tiled=True)
-        return product(take_pick, got, "ja,af->jf").astype(BF)
+    def sent_order(v):
+        return product(send_pick, v, "pt,tf->pf").astype(BF)
 
     def bring_back(v):
         sent = product(take_pick, v, "ja,jf->af").astype(BF)
@@ -618,9 +898,8 @@
     ff = w_gate.shape[1]
     ff_pad = -(-ff // 128) * 128
     attn_shard = jnp.concatenate([w_query, key_weight, value_weight, w_out.T], axis=1)
-    attn_pieces = grid.collect(attn_shard)
-    gate_p, up_p, down_p = (
-        grid.collect(pad_columns(v, ff_pad)) for v in (w_gate, w_up, w_down.T)
+    ffn_shard = jnp.concatenate(
+        [pad_columns(v, ff_pad) for v in (w_gate, w_up, w_down.T)], axis=1
     )
     shard_rows = w_gate.shape[0]
     order = grid.order()
@@ -628,10 +907,6 @@
     grad_order = [order[d * grid.n + k] for d in grad_order for k in range(grid.n)]
     offsets = (jnp.stack(order + grad_order) * shard_rows).astype(jnp.int32)
 
-    packed_tok = spread(tokens)
-    x_full = grid.tp_gather(packed_tok)
-    packed_cot = spread(cotangent)
-    dy_full = grid.tp_gather(packed_cot)
     own_slots = grid.c * local_len + jnp.arange(local_len, dtype=jnp.int32)
     position = slot_tables(lengths[0], own_slots)[1]
     start = own_slots - position
@@ -654,49 +929,27 @@
     n_pairs = q_width // 128
     rows = flat_len
 
-    qb, kv, raw, attn_w = once(
-        functools.partial(qkv_kernel, q_width, kv_width, pieces, shard_rows),
-        1,
-        5,
-        pieces,
-        [
-            shape((rows, q_width), BF),
-            shape((rows, 2 * kv_width), BF),
-            shape((rows, qkv_width), F32),
-            shape((MODEL_WIDTH, attn_width), BF),
-        ],
-        [pltpu.SemaphoreType.DMA((pieces,))],
-        2 * rows * MODEL_WIDTH * qkv_width,
-    )(offsets, x_full, gain_attn[None, :], head_gain, cosines, sines, *attn_pieces)
-    row_kv = lax.all_gather(kv, "ctx", axis=0, tiled=True)
     attn_flops = 4 * 2 * rows * row_len * q_width
-    heads, sums, attn_part = once(
-        functools.partial(attend_kernel, q_width, kv_width, local_len),
-        1,
-        4,
-        0,
-        [
-            shape((rows, q_width), F32),
-            shape((n_pairs, 8, 2 * rows), F32),
-            shape((rows, MODEL_WIDTH), BF),
-        ],
-        [
-            pltpu.VMEM((n_pairs, 2 * rows, 128), F32),
-            pltpu.VMEM((n_pairs, 2 * rows, 128), F32),
-            pltpu.VMEM((rows, local_len), F32),
-        ],
-        attn_flops,
-    )(place, qb, row_kv, start[:, None], attn_w)
-    attn_a, attn_b = grid.tp_parts(attn_part)
-
+    x_full, dy_full, qb, row_kv, raw, heads, sums, middle, squares, attn_w, ffn_w = forward_pass(
+        grid,
+        q_width,
+        kv_width,
+        ff_pad,
+        sent_order(tokens),
+        sent_order(cotangent),
+        take_pick,
+        gain_attn[None, :],
+        head_gain,
+        cosines,
+        sines,
+        start[:, None],
+        attn_shard,
+        ffn_shard,
+    )
     own_features = lambda v: lax.dynamic_slice_in_dim(v, grid.t * feat_len, feat_len, 1)
-    middle_own = (
-        packed_tok.astype(F32)
-        + own_features(attn_a).astype(F32)
-        + own_features(attn_b).astype(F32)
-    )
-    ffn_part, d_mid_part, d_gain_ffn, squares, normed_two, hidden, d_gate, d_up = ffn_pass(
-        x_full, attn_a, attn_b, dy_full, gain_ffn[None, :], gate_p, up_p, down_p, offsets
+    middle_own = own_features(middle)
+    ffn_part, d_mid_part, d_gain_ffn, normed_two, hidden, d_gate, d_up = ffn_pass(
+        middle, dy_full, gain_ffn[None, :], ffn_w
     )
     d_middle_full = dy_full.astype(F32) + grid.tp_sum(d_mid_part)
     d_middle = own_features(d_middle_full)

time: 557 us -> 531 us (0.953); the launches traced: 547 us -> 527 us
  Pallas kernels: 105 us -> 253 us
  waiting for transfers between devices: 225 us -> 117 us
  starting transfers between devices: 136 us -> 79.8 us
    pallas_call x1 -> x2, Pallas kernels: 28.2 us -> 195 us  [the longest x1 171 us: forward_pass(): pl.pallas_call(functools.partial(forward_kernel, n, ctx, tp, q_width, kv_...]
    ppermute x56 -> x8, waiting for transfers between devices: 138 us -> 80.2 us  [flip(): return lax.ppermute(v, 'ctx', [(i, i ^ bit) for i in range(self.ctx)])]
    ppermute x56 -> x8, starting transfers between devices: 61.3 us -> 22.6 us  [flip(): return lax.ppermute(v, 'ctx', [(i, i ^ bit) for i in range(self.ctx)])]
    ppermute x3 -> x0, waiting for transfers between devices: 19.7 us -> none  [the longest x2 19.7 us: tp_gather(): other = lax.ppermute(v, 'tp', [(0, 1), (1, 0)])]
    pallas_call x4 -> x2, Pallas kernels: 46.6 us -> 28.1 us  [call(): pl.pallas_call(body, grid_spec=pltpu.PrefetchScalarGridSpec(num_scalar_pr...]
    ppermute x24 -> x12, waiting for transfers between devices: 51.8 us -> 33.8 us  [ring(): lax.ppermute(v, 'fsdp', [(i, (i + 1) % self.n) for i in range(self.n)])]
    all_to_all x2, starting transfers between devices: 9.49 us -> 23.7 us  [bring_back(): got = lax.all_to_all(sent, both, split_axis=0, concat_axis=0, tiled=True)]
    all_to_all x2 -> x0, waiting for transfers between devices: 12 us -> none  [spread(): got = lax.all_to_all(sent, both, split_axis=0, concat_axis=0, tiled=True)]
  transfers between devices with their start and end apart: 97 -> 31, of which waited for: 33 -> 12; matrix products, arithmetic and copies ran while one was open for 10% -> 7% of each run, Pallas kernels for 12% -> 11%
where the time goes in v3:
time: 531 us; the launch traced here: 527 us
  Pallas kernels  253 us (48%)
  waiting for transfers between devices  117 us (22%)
  starting transfers between devices  79.8 us (15%)
  other arithmetic  38.6 us (7%)
  between operations  16.6 us (3%)
  local copies, waits for them, and re-layouts  11.8 us (2%)
  matrix products  10.5 us (2%)
    pallas_call x1, Pallas kernels, forward_pass(): pl.pallas_call(functools.partial(forward_kernel, n, ctx, tp, q_width, kv_...  171 us
    ppermute x8, waiting for transfers between devices, flip(): return lax.ppermute(v, 'ctx', [(i, i ^ bit) for i in range(self.ctx)])  80.2 us
    ppermute x12, waiting for transfers between devices, ring(): lax.ppermute(v, 'fsdp', [(i, (i + 1) % self.n) for i in range(self.n)])  33.8 us
    pallas_call x3, Pallas kernels, weight_grad(): pl.pallas_call(functools.partial(weight_grad_kernel, pieces, width // pie...  30.5 us
    pallas_call x2, Pallas kernels, call(): pl.pallas_call(body, grid_spec=pltpu.PrefetchScalarGridSpec(num_scalar_pr...  28.1 us
    pallas_call x1, Pallas kernels, ffn_pass(): pl.pallas_call(ffn_kernel, grid=(steps,), in_specs=[whole((rows, width))]...  23.9 us
    all_to_all x2, starting transfers between devices, bring_back(): got = lax.all_to_all(sent, both, split_axis=0, concat_axis=0, tiled=True)  23.7 us
    ppermute x8, starting transfers between devices, flip(): return lax.ppermute(v, 'ctx', [(i, i ^ bit) for i in range(self.ctx)])  22.6 us
  transfers between devices with their start and end apart: 31, of which 12 were waited for; matrix products, arithmetic and copies ran while one was open for 7% of the time, Pallas kernels for 11%

profile of v3, /device:TPU:0, one launch (start us, length us, event | category | flops | bytes accessed | tf_op | source)
XLA Modules:
  0.0 527.3 jit_solution(15381523245616856752)
XLA Ops:
  13.7 2.7 select_add_fusion.start_col
  16.4 2.7 fusion.45
  28.1 170.8 %shard_map.254 = (bf16[512,1024]{1,0:T(8,128)(2,1)}, bf16[512,1024]{1,0:T(8,128)(2,1)}, bf16[512,512]{1,0:T(8,128)(2,1)}, bf16[2048,512]{1,0:T(8,128)(2,1)}, f32...) custom-call(bf16[512,512]{1,0:T(8,128)(2,1)} %convolution_convert_fu, ...), custom_call_target="tpu_custom_call" | custom-call | flops 4294967296 | bytes 41943040 | tf_op jit(solution)/shard_map/pallas_call | solution.py:684
  198.9 23.9 %shard_map.255 = (bf16[512,1024]{1,0:T(8,128)(2,1)}, bf16[512,1024]{1,0:T(8,128)(2,1)}, f32[1,1024]{1,0:T(1,128)}, bf16[512,1024]{1,0:T(8,128)(2,1)}, bf16[512,2...) custom-call(f32[512,1024]{1,0:T(8,128)} %get-tuple-element.46.mid, ...), custom_call_target="tpu_custom_call" | custom-call | flops 14495514624 | bytes 14155776 | tf_op jit(solution)/shard_map/pallas_call | solution.py:776
  226.6 10.1 %shard_map.259 = (bf16[512,2304]{1,0:T(8,128)(2,1)}, bf16[512,2304]{1,0:T(8,128)(2,1)}) custom-call(s32[32]{0:T(128)} %broadcast_multiply_fusion.1.offs, bf16[512,1024]{1,0:T(8,128)(2,1)} %get-tuple-element.64.left, bf16[512,2304]{1,0:T(8,128)(2,1)} %get-tuple-element.68.right), custom_call_target="tpu_custom_call" | custom-call | flops 2415919104 | bytes 4718592 | tf_op jit(solution)/shard_map/pallas_call | solution.py:800
  236.7 10.1 %shard_map.258 = (bf16[512,2304]{1,0:T(8,128)(2,1)}, bf16[512,2304]{1,0:T(8,128)(2,1)}) custom-call(s32[32]{0:T(128)} %broadcast_multiply_fusion.1.offs, bf16[512,1024]{1,0:T(8,128)(2,1)} %get-tuple-element.64.left, bf16[512,2304]{1,0:T(8,128)(2,1)} %get-tuple-element.65.right), custom_call_target="tpu_custom_call" | custom-call | flops 2415919104 | bytes 4718592 | tf_op jit(solution)/shard_map/pallas_call | solution.py:800
  247.3 10.2 %shard_map.260 = (bf16[512,2304]{1,0:T(8,128)(2,1)}, bf16[512,2304]{1,0:T(8,128)(2,1)}) custom-call(s32[32]{0:T(128)} %broadcast_multiply_fusion.1.offs, bf16[512,1024]{1,0:T(8,128)(2,1)} %get-tuple-element.47.dy.left, bf16[512,2304]{1,0:T(8,128)(2,1)} %get-tuple-element.71.right), custom_call_target="tpu_custom_call" | custom-call | flops 2415919104 | bytes 4718592 | tf_op jit(solution)/shard_map/pallas_call | solution.py:800
  260.2 2.7 convolution_convert_fusion.3
  262.9 18.4 %all-to-all-start = ((bf16[16,32,512]{2,1,0:T(8,128)(2,1)}), bf16[16,32,512]{2,1,0:T(8,128)(2,1)}, u32[]{:S(2)}, u32[]{:S(2)}) async-start(bf16[16,32,512]{2,1,0:T(8,128)(2,1)} %bitcast.10), calls=%async_computation | async-start | bytes 1048576 | tf_op jit(solution)/shard_map/all_to_all | solution.py:895
  282.7 3.2 fusion.58
  285.9 14.4 %shard_map.256 = (f32[512,512]{1,0:T(8,128)}, bf16[2048,512]{1,0:T(8,128)(2,1)}, bf16[1024,512]{1,0:T(8,128)(2,1)}) custom-call(s32[1]{0:T(128)} %bitcast.28.where, bf16[512,512]{1,0:T(8,128)(2,1)} %get-tuple-element.54.qb, bf16[2048,512]{1,0:T(8,128)(2,1)} %get-tuple-element.55.kv, f32[512,512]{1,0:T(8,128)} %get-tuple-element.56.heads, ...), custom_call_target="tpu_custom_call" | custom-call | flops 12884901888 | bytes 8388608 | tf_op jit(solution)/shard_map/pallas_call | solution.py:751
  302.7 2.9 fusion.1
  305.7 17.1 %collective-permute-start.14 = (bf16[4,64,2304]{2,1,0:T(8,128)(2,1)S(1)}, bf16[4,64,2304]{2,1,0:T(8,128)(2,1)S(1)}, u32[]{:S(2)}, u32[]{:S(2)}) collective-permute-start(bf16[4,64,2304]{2,1,0:T(8,128)(2,1)S(1)} %slice.188), channel_id=1, source_target_pairs={{0,4},{2,6},{4,0},{6,2},{1,5},{3,7},{5,1},{7,3},{8,12},{10,14},{12... | collective-permute-start | bytes 3538952 | tf_op jit(solution)/shard_map/ppermute | solution.py:60
  330.6 13.7 %collective-permute-done.14 = bf16[4,64,2304]{2,1,0:T(8,128)(2,1)S(1)} collective-permute-done((bf16[4,64,2304]{2,1,0:T(8,128)(2,1)S(1)}, bf16[4,64,2304]{2,1,0:T(8,128)(2,1)S(1)}, u32[]{:S(2)}, u32[]{:S(2)}) %collective-permute-start.14) | collective-permute-done | bytes 1179680 | tf_op jit(solution)/shard_map/ppermute | solution.py:60
  345.8 33.2 %collective-permute-done.9 = bf16[4,64,2304]{2,1,0:T(8,128)(2,1)S(1)} collective-permute-done((bf16[4,64,2304]{2,1,0:T(8,128)(2,1)S(1)}, bf16[4,64,2304]{2,1,0:T(8,128)(2,1)S(1)}, u32[]{:S(2)}, u32[]{:S(2)}) %collective-permute-start.9) | collective-permute-done | bytes 1179680 | tf_op jit(solution)/shard_map/ppermute | solution.py:60
  380.9 23.4 %collective-permute-done.19 = bf16[4,64,2304]{2,1,0:T(8,128)(2,1)S(1)} collective-permute-done((bf16[4,64,2304]{2,1,0:T(8,128)(2,1)S(1)}, bf16[4,64,2304]{2,1,0:T(8,128)(2,1)S(1)}, u32[]{:S(2)}, u32[]{:S(2)}) %collective-permute-start.19) | collective-permute-done | bytes 1179680 | tf_op jit(solution)/shard_map/ppermute | solution.py:60
  409.3 3.9 collective-permute-done.20
  417.2 5.5 %collective-permute-done.11 = bf16[64,2304]{1,0:T(8,128)(2,1)S(1)} collective-permute-done((bf16[64,2304]{1,0:T(8,128)(2,1)S(1)}, bf16[64,2304]{1,0:T(8,128)(2,1)S(1)}, u32[]{:S(2)}, u32[]{:S(2)}) %collective-permute-start.11) | collective-permute-done | bytes 294944 | tf_op jit(solution)/shard_map/ppermute | solution.py:57
  425.8 13.7 %shard_map.257 = (bf16[512,1024]{1,0:T(8,128)(2,1)}, f32[1,1024]{1,0:T(1,128)}, f32[1,1024]{1,0:T(1,128)}, bf16[512,1536]{1,0:T(8,128)(2,1)}, bf16[512,1536]{1,0:T(8,128)(2,1)}) custom-call(s32[32]{0:T(128)} %broadcast_multiply_fusion.1.offs, bf16[512,1024]{1,0:T(8,128)(2,1)} %get-tuple-element.51.x, f32[1,1024]{1,0:T(1,128)} %bitcast.134, ...), custom_call_target="tpu_custom_call" | custom-call | flops 2147483648 | bytes 8388608 | tf_op jit(solution)/shard_map/pallas_call | solution.py:751
  442.5 12.9 %collective-permute-start.23 = (f32[2179]{0:T(1024)S(1)}, f32[2179]{0:T(1024)S(1)}, u32[]{:S(2)}, u32[]{:S(2)}) collective-permute-start(f32[2179]{0:T(1024)S(1)} %concatenate.23), channel_id=1, source_target_pairs={{0,2},{2,0},{4,6},{6,4},{1,3},{3,1},{5,7},{7,5},{8,10},{10,8},{12,... | collective-permute-start | bytes 26156 | tf_op jit(solution)/shard_map/ppermute | solution.py:121
  475.5 9.8 %collective-permute-done.4 = bf16[4,64,1536]{2,1,0:T(8,128)(2,1)S(1)} collective-permute-done((bf16[4,64,1536]{2,1,0:T(8,128)(2,1)S(1)}, bf16[4,64,1536]{2,1,0:T(8,128)(2,1)S(1)}, u32[]{:S(2)}, u32[]{:S(2)}) %collective-permute-start.4) | collective-permute-done | bytes 786464 | tf_op jit(solution)/shard_map/ppermute | solution.py:60
  487.6 5.2 all-to-all-start.1
  495.4 15.2 %collective-permute-done.6 = bf16[64,1536]{1,0:T(8,128)(2,1)S(1)} collective-permute-done((bf16[64,1536]{1,0:T(8,128)(2,1)S(1)}, bf16[64,1536]{1,0:T(8,128)(2,1)S(1)}, u32[]{:S(2)}, u32[]{:S(2)}) %collective-permute-start.6) | collective-permute-done | bytes 196640 | tf_op jit(solution)/shard_map/ppermute | solution.py:57
  512.4 6.5 %collective-permute-done.7 = bf16[64,1536]{1,0:T(8,128)(2,1)S(1)} collective-permute-done((bf16[64,1536]{1,0:T(8,128)(2,1)S(1)}, bf16[64,1536]{1,0:T(8,128)(2,1)S(1)}, u32[]{:S(2)}, u32[]{:S(2)}) %collective-permute-start.7) | collective-permute-done | bytes 196640 | tf_op jit(solution)/shard_map/ppermute | solution.py:57
  (174 shorter events, 78.4 us)
Async XLA Ops:
  223.8 36.4 %collective-permute-start = (bf16[512,512]{1,0:T(8,128)(2,1)S(1)}, bf16[512,512]{1,0:T(8,128)(2,1)S(1)}, u32[]{:S(2)}, u32[]{:S(2)}) collective-permute-start(bf16[512,512]{1,0:T(8,128)(2,1)S(1)} %constant_dynamic-slice_fusion.1), channel_id=1, source_target_pairs={{0,1},{1,0},{2,3},{3,2},{4,5},{5,4},{6,7},{7,6},{8,9},{9,8},{10,11... | collective-permute-start | bytes 1572872 | tf_op jit(solution)/shard_map/ppermute | solution.py:108
  224.4 58.3 %collective-permute-start.1 = (bf16[512,1024]{1,0:T(8,128)(2,1)}, bf16[512,1024]{1,0:T(8,128)(2,1)}, u32[]{:S(2)}, u32[]{:S(2)}) collective-permute-start(bf16[512,1024]{1,0:T(8,128)(2,1)} %get-tuple-element.50), channel_id=1, source_target_pairs={{0,1},{1,0},{2,3},{3,2},{4,5},{5,4},{6,7},{7,6},{8,9},{9,8},{10,11... | collective-permute-start | bytes 3145736 | tf_op jit(solution)/shard_map/ppermute | solution.py:99
  236.7 66.0 %collective-permute-start.13 = (bf16[8,64,2304]{2,1,0:T(8,128)(2,1)}, bf16[8,64,2304]{2,1,0:T(8,128)(2,1)}, u32[]{:S(2)}, u32[]{:S(2)}) collective-permute-start(bf16[8,64,2304]{2,1,0:T(8,128)(2,1)} %bitcast.139), channel_id=1, source_target_pairs={{0,2},{2,0},{4,6},{6,4},{1,3},{3,1},{5,7},{7,5},{8,10},{10,8},{12,... | collective-permute-start | bytes 7077896 | tf_op jit(solution)/shard_map/ppermute | solution.py:60
  246.8 76.0 %collective-permute-start.8 = (bf16[8,64,2304]{2,1,0:T(8,128)(2,1)}, bf16[8,64,2304]{2,1,0:T(8,128)(2,1)}, u32[]{:S(2)}, u32[]{:S(2)}) collective-permute-start(bf16[8,64,2304]{2,1,0:T(8,128)(2,1)} %bitcast.138), channel_id=1, source_target_pairs={{0,2},{2,0},{4,6},{6,4},{1,3},{3,1},{5,7},{7,5},{8,10},{10,8},{12,... | collective-permute-start | bytes 7077896 | tf_op jit(solution)/shard_map/ppermute | solution.py:60
  257.5 69.2 %collective-permute-start.18 = (bf16[8,64,2304]{2,1,0:T(8,128)(2,1)}, bf16[8,64,2304]{2,1,0:T(8,128)(2,1)}, u32[]{:S(2)}, u32[]{:S(2)}) collective-permute-start(bf16[8,64,2304]{2,1,0:T(8,128)(2,1)} %bitcast.137), channel_id=1, source_target_pairs={{0,2},{2,0},{4,6},{6,4},{1,3},{3,1},{5,7},{7,5},{8,10},{10,8},{12,... | collective-permute-start | bytes 7077896 | tf_op jit(solution)/shard_map/ppermute | solution.py:60
  262.9 37.5 %all-to-all-start = ((bf16[16,32,512]{2,1,0:T(8,128)(2,1)}), bf16[16,32,512]{2,1,0:T(8,128)(2,1)}, u32[]{:S(2)}, u32[]{:S(2)}) async-start(bf16[16,32,512]{2,1,0:T(8,128)(2,1)} %bitcast.10), calls=%async_computation | async-start | bytes 1048576 | tf_op jit(solution)/shard_map/all_to_all | solution.py:895
  281.4 142.3 %reduce-scatter.2.cloned.1.call-start = ((), (), s32[]{:S(2)}) async-start(), calls=%async_computation.3 | async-start | bytes 2621440 | tf_op jit(solution)/shard_map/reduce_scatter | solution.py:985
  305.7 38.5 %collective-permute-start.14 = (bf16[4,64,2304]{2,1,0:T(8,128)(2,1)S(1)}, bf16[4,64,2304]{2,1,0:T(8,128)(2,1)S(1)}, u32[]{:S(2)}, u32[]{:S(2)}) collective-permute-start(bf16[4,64,2304]{2,1,0:T(8,128)(2,1)S(1)} %slice.188), channel_id=1, source_target_pairs={{0,4},{2,6},{4,0},{6,2},{1,5},{3,7},{5,1},{7,3},{8,12},{10,14},{12... | collective-permute-start | bytes 3538952 | tf_op jit(solution)/shard_map/ppermute | solution.py:60
  325.2 53.9 %collective-permute-start.9 = (bf16[4,64,2304]{2,1,0:T(8,128)(2,1)S(1)}, bf16[4,64,2304]{2,1,0:T(8,128)(2,1)S(1)}, u32[]{:S(2)}, u32[]{:S(2)}) collective-permute-start(bf16[4,64,2304]{2,1,0:T(8,128)(2,1)S(1)} %slice.182), channel_id=1, source_target_pairs={{0,4},{2,6},{4,0},{6,2},{1,5},{3,7},{5,1},{7,3},{8,12},{10,14},{12... | collective-permute-start | bytes 3538952 | tf_op jit(solution)/shard_map/ppermute | solution.py:60
  329.0 75.3 %collective-permute-start.19 = (bf16[4,64,2304]{2,1,0:T(8,128)(2,1)S(1)}, bf16[4,64,2304]{2,1,0:T(8,128)(2,1)S(1)}, u32[]{:S(2)}, u32[]{:S(2)}) collective-permute-start(bf16[4,64,2304]{2,1,0:T(8,128)(2,1)S(1)} %slice.194), channel_id=1, source_target_pairs={{0,4},{2,6},{4,0},{6,2},{1,5},{3,7},{5,1},{7,3},{8,12},{10,14},{12... | collective-permute-start | bytes 3538952 | tf_op jit(solution)/shard_map/ppermute | solution.py:60
  344.6 61.6 %collective-permute-start.15 = (bf16[64,2304]{1,0:T(8,128)(2,1)S(1)}, bf16[64,2304]{1,0:T(8,128)(2,1)S(1)}, u32[]{:S(2)}, u32[]{:S(2)}) collective-permute-start(bf16[64,2304]{1,0:T(8,128)(2,1)S(1)} %slice_bitcast_fusion.7), channel_id=1, source_target_pairs={{0,8},{8,16},{16,24},{24,0},{1,9},{9,17},{17,25},{25,1},{2,10},{10... | collective-permute-start | bytes 884744 | tf_op jit(solution)/shard_map/ppermute | solution.py:57
  379.4 28.4 %collective-permute-start.10 = (bf16[64,2304]{1,0:T(8,128)(2,1)S(1)}, bf16[64,2304]{1,0:T(8,128)(2,1)S(1)}, u32[]{:S(2)}, u32[]{:S(2)}) collective-permute-start(bf16[64,2304]{1,0:T(8,128)(2,1)S(1)} %slice_bitcast_fusion.11), channel_id=1, source_target_pairs={{0,8},{8,16},{16,24},{24,0},{1,9},{9,17},{17,25},{25,1},{2,10},{10... | collective-permute-start | bytes 884744 | tf_op jit(solution)/shard_map/ppermute | solution.py:57
  406.2 10.1 %collective-permute-start.16 = (bf16[64,2304]{1,0:T(8,128)(2,1)S(1)}, bf16[64,2304]{1,0:T(8,128)(2,1)S(1)}, u32[]{:S(2)}, u32[]{:S(2)}) collective-permute-start(bf16[64,2304]{1,0:T(8,128)(2,1)S(1)} %fusion.10), channel_id=1, source_target_pairs={{0,8},{8,16},{16,24},{24,0},{1,9},{9,17},{17,25},{25,1},{2,10},{10... | collective-permute-start | bytes 884744 | tf_op jit(solution)/shard_map/ppermute | solution.py:57
  407.8 14.8 %collective-permute-start.11 = (bf16[64,2304]{1,0:T(8,128)(2,1)S(1)}, bf16[64,2304]{1,0:T(8,128)(2,1)S(1)}, u32[]{:S(2)}, u32[]{:S(2)}) collective-permute-start(bf16[64,2304]{1,0:T(8,128)(2,1)S(1)} %fusion.12), channel_id=1, source_target_pairs={{0,8},{8,16},{16,24},{24,0},{1,9},{9,17},{17,25},{25,1},{2,10},{10... | collective-permute-start | bytes 884744 | tf_op jit(solution)/shard_map/ppermute | solution.py:57
  414.0 41.5 %collective-permute-start.21 = (bf16[64,2304]{1,0:T(8,128)(2,1)}, bf16[64,2304]{1,0:T(8,128)(2,1)}, u32[]{:S(2)}, u32[]{:S(2)}) collective-permute-start(bf16[64,2304]{1,0:T(8,128)(2,1)} %fusion.8), channel_id=1, source_target_pairs={{0,8},{8,16},{16,24},{24,0},{1,9},{9,17},{17,25},{25,1},{2,10},{10... | collective-permute-start | bytes 884744 | tf_op jit(solution)/shard_map/ppermute | solution.py:57
  417.2 42.3 %collective-permute-start.17 = (bf16[64,2304]{1,0:T(8,128)(2,1)}, bf16[64,2304]{1,0:T(8,128)(2,1)}, u32[]{:S(2)}, u32[]{:S(2)}) collective-permute-start(bf16[64,2304]{1,0:T(8,128)(2,1)} %fusion.9), channel_id=1, source_target_pairs={{0,8},{8,16},{16,24},{24,0},{1,9},{9,17},{17,25},{25,1},{2,10},{10... | collective-permute-start | bytes 884744 | tf_op jit(solution)/shard_map/ppermute | solution.py:57
  423.5 38.5 %collective-permute-start.12 = (bf16[64,2304]{1,0:T(8,128)(2,1)}, bf16[64,2304]{1,0:T(8,128)(2,1)}, u32[]{:S(2)}, u32[]{:S(2)}) collective-permute-start(bf16[64,2304]{1,0:T(8,128)(2,1)} %fusion.11), channel_id=1, source_target_pairs={{0,8},{8,16},{16,24},{24,0},{1,9},{9,17},{17,25},{25,1},{2,10},{10... | collective-permute-start | bytes 884744 | tf_op jit(solution)/shard_map/ppermute | solution.py:57
  442.5 14.9 %collective-permute-start.23 = (f32[2179]{0:T(1024)S(1)}, f32[2179]{0:T(1024)S(1)}, u32[]{:S(2)}, u32[]{:S(2)}) collective-permute-start(f32[2179]{0:T(1024)S(1)} %concatenate.23), channel_id=1, source_target_pairs={{0,2},{2,0},{4,6},{6,4},{1,3},{3,1},{5,7},{7,5},{8,10},{10,8},{12,... | collective-permute-start | bytes 26156 | tf_op jit(solution)/shard_map/ppermute | solution.py:121
  455.4 11.2 %collective-permute-start.3 = (bf16[8,64,1536]{2,1,0:T(8,128)(2,1)}, bf16[8,64,1536]{2,1,0:T(8,128)(2,1)S(1)}, u32[]{:S(2)}, u32[]{:S(2)}) collective-permute-start(bf16[8,64,1536]{2,1,0:T(8,128)(2,1)} %bitcast.140), channel_id=1, source_target_pairs={{0,2},{2,0},{4,6},{6,4},{1,3},{3,1},{5,7},{7,5},{8,10},{10,8},{12,... | collective-permute-start | bytes 4718600 | tf_op jit(solution)/shard_map/ppermute | solution.py:60
  456.5 12.3 %collective-permute-start.22 = (bf16[64,2304]{1,0:T(8,128)(2,1)S(1)}, bf16[64,2304]{1,0:T(8,128)(2,1)S(1)}, u32[]{:S(2)}, u32[]{:S(2)}) collective-permute-start(bf16[64,2304]{1,0:T(8,128)(2,1)S(1)} %fusion.7), channel_id=1, source_target_pairs={{0,8},{8,16},{16,24},{24,0},{1,9},{9,17},{17,25},{25,1},{2,10},{10... | collective-permute-start | bytes 884744 | tf_op jit(solution)/shard_map/ppermute | solution.py:57
  467.1 18.3 %collective-permute-start.4 = (bf16[4,64,1536]{2,1,0:T(8,128)(2,1)S(1)}, bf16[4,64,1536]{2,1,0:T(8,128)(2,1)S(1)}, u32[]{:S(2)}, u32[]{:S(2)}) collective-permute-start(bf16[4,64,1536]{2,1,0:T(8,128)(2,1)S(1)} %slice.172), channel_id=1, source_target_pairs={{0,4},{2,6},{4,0},{6,2},{1,5},{3,7},{5,1},{7,3},{8,12},{10,14},{12... | collective-permute-start | bytes 2359304 | tf_op jit(solution)/shard_map/ppermute | solution.py:60
  472.1 14.1 %collective-permute-start.2 = (bf16[512,512]{1,0:T(8,128)(2,1)S(1)}, bf16[512,512]{1,0:T(8,128)(2,1)S(1)}, u32[]{:S(2)}, u32[]{:S(2)}) collective-permute-start(bf16[512,512]{1,0:T(8,128)(2,1)S(1)} %constant_dynamic-slice_fusion), channel_id=1, source_target_pairs={{0,1},{1,0},{2,3},{3,2},{4,5},{5,4},{6,7},{7,6},{8,9},{9,8},{10,11... | collective-permute-start | bytes 1572872 | tf_op jit(solution)/shard_map/ppermute | solution.py:108
  487.6 23.5 %all-to-all-start.1 = ((bf16[16,32,512]{2,1,0:T(8,128)(2,1)}), bf16[16,32,512]{2,1,0:T(8,128)(2,1)S(1)}, u32[]{:S(2)}, u32[]{:S(2)}) async-start(bf16[16,32,512]{2,1,0:T(8,128)(2,1)} %bitcast.29), calls=%async_computation.2 | async-start | bytes 1048576 | tf_op jit(solution)/shard_map/all_to_all | solution.py:895
  493.2 17.4 %collective-permute-start.6 = (bf16[64,1536]{1,0:T(8,128)(2,1)S(1)}, bf16[64,1536]{1,0:T(8,128)(2,1)S(1)}, u32[]{:S(2)}, u32[]{:S(2)}) collective-permute-start(bf16[64,1536]{1,0:T(8,128)(2,1)S(1)} %fusion.24), channel_id=1, source_target_pairs={{0,8},{8,16},{16,24},{24,0},{1,9},{9,17},{17,25},{25,1},{2,10},{10... | collective-permute-start | bytes 589832 | tf_op jit(solution)/shard_map/ppermute | solution.py:57
  (27 other events, 351.8 us)
Sparse Core Ops, SparseCore 0:
  300.5 65.7 reduce-scatter.1
